TPU v7x, 256 devices: a whole 4x4x8 slice. The times are simulated.
256 devices in a mesh: ctx: 32 (over y, z), head: 8 (over x, core).
Axes of the slice: x: 4, y: 4, z: 8, core: 2. Of those that a mesh axis runs over, the one named last changes fastest.
Arguments:
- queries: bfloat16 [8, 16384, 128], P('head', 'ctx'), may hold values from -170 to 170
- keys: bfloat16 [16384, 128], P('ctx'), may hold values from -6 to 6
- values: bfloat16 [16384, 128], P('ctx'), may hold values from -6 to 6
- outputs: bfloat16 [8, 16384, 128], P('head', 'ctx'), may hold values from -2 to 2
- dout: bfloat16 [8, 16384, 128], P('head', 'ctx'), may hold values from -6 to 6
- docs: int32 [16384], P('ctx'), may hold values from 0 to 63, never falling along the last dimension, each value on 1 to 8704 neighbouring positions
Outputs:
- dq: bfloat16 [8, 16384, 128], P('head', 'ctx')
- dk: bfloat16 [16384, 128], P(('ctx', 'head'))
- dv: bfloat16 [16384, 128], P(('ctx', 'head'))
Inputs may be any that keep to these rules, and one draw needn't show every extreme that they name: `docs`: document numbers never fall along the sequence; each document holds 1 to 8704 tokens and one holds exactly 8704.
All inputs are finite; a program needn't handle non-finite values.
Results may differ from a plain program's by a relative error of at most 0.0049.
Values may be sent and summed in bfloat16 or wider, within the bound.
No kernel may reach another device: no remote copies, remote signals or barrier semaphores. Data moves between devices by JAX's collectives and lax.ppermute only.
A program may use at most 64 MiB of HBM per device.

v0:
```python
import math

import jax
import jax.numpy as jnp
from jax import lax
from jax.sharding import PartitionSpec as P


def shifted(block, axis, distance):
    devices = range(lax.axis_size(axis))
    route = [(i - distance, i) for i in devices if i - distance in devices]
    return lax.ppermute(block, axis, route)


def contract(left, right, left_dim, right_dim):
    return lax.dot_general(
        left, right, (((left_dim,), (right_dim,)), ((), ())), preferred_element_type=jnp.float32
    )


def local(queries, keys, values, outputs, dout, docs):
    heads_loc, tok, width = queries.shape
    nctx = lax.axis_size("ctx")
    total = tok * nctx
    scale = 1.0 / math.sqrt(width)
    me = lax.axis_index("ctx")
    span = nctx // 2 + 1
    qpos = me * tok + jnp.arange(tok, dtype=jnp.int32)
    rows = heads_loc * tok
    q_flat = queries.reshape(rows, width)
    do_flat = dout.reshape(rows, width)
    qpos_flat = jnp.tile(qpos, heads_loc)
    qdoc_flat = jnp.tile(docs, heads_loc)
    delta = jnp.sum(dout.astype(jnp.float32) * outputs.astype(jnp.float32), axis=-1).reshape(rows)
    docs_words = docs.astype(jnp.bfloat16)
    key_src, val_src, doc_words = (
        lax.all_gather(keys, "ctx", axis=0, tiled=True),
        lax.all_gather(values, "ctx", axis=0, tiled=True),
        lax.all_gather(docs_words, "ctx", axis=0, tiled=True),
    )
    src_docs = doc_words.astype(jnp.int32)
    block = min(1024, total)
    nblock = total // block
    qlast = me * tok + tok - 1
    qdoc_first = docs[0]

    def needed(start, count):
        return (start <= qlast) & (src_docs[start + count - 1] >= qdoc_first)

    def key_tile(start, count):
        key_blk = lax.dynamic_slice_in_dim(key_src, start, count, 0)
        val_blk = lax.dynamic_slice_in_dim(val_src, start, count, 0)
        kdoc = lax.dynamic_slice_in_dim(src_docs, start, count, 0)
        kpos = start + jnp.arange(count, dtype=jnp.int32)
        visible = (qdoc_flat[:, None] == kdoc[None, :]) & (kpos[None, :] <= qpos_flat[:, None])
        score = contract(q_flat, key_blk, 1, 1) * scale
        score = jnp.where(visible, score, jnp.float32(-1e30))
        return (score, visible, key_blk, val_blk)

    def stat_step(index, carry):
        start = index * block

        def stat_run(state):
            top, summed = state
            score, visible, key_blk, val_blk = key_tile(start, block)
            new_top = jnp.maximum(top, jnp.max(score, axis=1))
            terms = jnp.where(visible, jnp.exp(score - new_top[:, None]), jnp.float32(0.0))
            return (new_top, summed * jnp.exp(top - new_top) + jnp.sum(terms, axis=1))

        return lax.cond(needed(start, block), stat_run, lambda state: state, carry)

    top, summed = lax.fori_loop(
        0,
        nblock,
        stat_step,
        (jnp.full((rows,), -1e30, jnp.float32), jnp.zeros((rows,), jnp.float32)),
    )
    lse = top + jnp.log(summed)

    def query_step(index, acc):
        start = index * block

        def query_run(state):
            score, visible, key_blk, val_blk = key_tile(start, block)
            prob = jnp.where(visible, jnp.exp(score - lse[:, None]), jnp.float32(0.0))
            dprob = contract(do_flat, val_blk, 1, 1)
            dscore = (prob * (dprob - delta[:, None])).astype(jnp.bfloat16)
            return state + jnp.dot(dscore, key_blk, preferred_element_type=jnp.float32)

        return lax.cond(needed(start, block), query_run, lambda state: state, acc)

    dq_acc = lax.fori_loop(0, nblock, query_step, jnp.zeros((rows, width), jnp.float32))
    dq = (dq_acc * scale).astype(jnp.bfloat16).reshape(heads_loc, tok, width)
    empty = jnp.zeros((tok, width), jnp.float32)
    key_doc_last = docs[tok - 1]

    def add_rows(hop, query_piece, grad_piece, lse_piece, delta_piece, doc_piece, dk_acc, dv_acc):
        anchor = me + hop
        piece_docs = doc_piece[0].astype(jnp.int32)

        def add_run(state):
            acc_k, acc_v = state
            query = query_piece.reshape(rows, width)
            grad_out = grad_piece.reshape(rows, width)
            lse_rows = lse_piece.reshape(rows)
            delta_rows = delta_piece.reshape(rows)
            positions = jnp.tile(anchor * tok + jnp.arange(tok, dtype=jnp.int32), heads_loc)
            row_docs = jnp.tile(piece_docs, heads_loc)
            visible = (row_docs[:, None] == docs[None, :]) & (qpos[None, :] <= positions[:, None])
            score = jnp.where(visible, contract(query, keys, 1, 1) * scale, jnp.float32(-1e30))
            prob = jnp.where(visible, jnp.exp(score - lse_rows[:, None]), jnp.float32(0.0))
            dprob = contract(grad_out, values, 1, 1)
            dscore = (prob * (dprob - delta_rows[:, None])).astype(jnp.bfloat16)
            acc_k = acc_k + contract(dscore, query, 0, 0) * scale
            acc_v = acc_v + contract(prob.astype(jnp.bfloat16), grad_out, 0, 0)
            return (acc_k, acc_v)

        wanted = (anchor < nctx) & (piece_docs[0] <= key_doc_last)
        return lax.cond(wanted, add_run, lambda state: state, (dk_acc, dv_acc))

    lse_own = lse.reshape(heads_loc, tok)
    delta_own = delta.reshape(heads_loc, tok)
    docs_float = docs.astype(jnp.float32).reshape(1, tok)
    dk_first, dv_first = add_rows(0, queries, dout, lse_own, delta_own, docs_float, empty, empty)

    def fetch(index, carry):
        query_piece, grad_piece, lse_piece, delta_piece, doc_piece, dk_acc, dv_acc = carry
        query_piece, grad_piece = shifted((query_piece, grad_piece), "ctx", -1)
        lse_piece, delta_piece, doc_piece = shifted((lse_piece, delta_piece, doc_piece), "ctx", -1)
        dk_acc, dv_acc = add_rows(
            index + 1, query_piece, grad_piece, lse_piece, delta_piece, doc_piece, dk_acc, dv_acc
        )
        return (query_piece, grad_piece, lse_piece, delta_piece, doc_piece, dk_acc, dv_acc)

    fetched = lax.fori_loop(
        0, span, fetch, (queries, dout, lse_own, delta_own, docs_float, dk_first, dv_first)
    )
    dk_part, dv_part = (fetched[5], fetched[6])
    dk_sum, dv_sum = (
        lax.psum_scatter(dk_part, "head", scatter_dimension=0, tiled=True),
        lax.psum_scatter(dv_part, "head", scatter_dimension=0, tiled=True),
    )
    dk = dk_sum.astype(jnp.bfloat16)
    dv = dv_sum.astype(jnp.bfloat16)
    return (dq, dk, dv)


def solution(mesh):
    in_specs = (
        P("head", "ctx", None),
        P("ctx", None),
        P("ctx", None),
        P("head", "ctx", None),
        P("head", "ctx", None),
        P("ctx"),
    )
    out_specs = (P("head", "ctx", None), P(("ctx", "head"), None), P(("ctx", "head"), None))
    return jax.shard_map(local, mesh=mesh, in_specs=in_specs, out_specs=out_specs, check_vma=False)
```

profile of v0, /device:TPU:32, one launch (start us, length us, event | category | flops | bytes accessed | tf_op | source)
XLA Modules:
  0.0 523.7 jit_solution(11516787402330788192)
XLA Ops:
  9.5 51.2 %all-gather = bf16[32,1,512]{2,1,0:T(2,128)(2,1)S(1)} all-gather(bf16[1,1,512]{2,1,0:T(2,128)(2,1)S(1)} %reshape.79), channel_id=1, replica_groups=mesh['ctx'=32,'head'=8] {'ctx'}, dimensions={0}, use_global_device_ids=true | all-gather | bytes 33792 | tf_op jit(solution)/shard_map/all_gather | solution.py:39
  67.0 28.2 %all-gather.4.cloned.1.call-done = bf16[16384,128]{1,0:T(8,128)(2,1)} async-done(((bf16[512,128]{1,0:T(8,128)(2,1)}), bf16[16384,128]{1,0:T(8,128)(2,1)}) %all-gather.4.cloned.1.call-update) | async-done | bytes 4194320 | tf_op jit(solution)/shard_map/all_gather | solution.py:37
  95.2 34.2 %while.67 = (s32[]{:T(128)}, f32[512]{0:T(512)S(1)}, f32[512]{0:T(512)S(1)}, s32[]{:T(128)}, s32[16384]{0:T(1024)S(1)}, /*index=5*/s32[]{:T(128)}, s32[512]{0:T(...) while((s32[]{:T(128)}, f32[512]{0:T(512)S(1)}, ...), condition=%wide.region_5.6_spmd.clone, body=%wide.region_0.5_spmd.clone.sunk | while | flops 141560336 | bytes 4665779 | solution.py:72
  97.2 2.9 conditional.11
  129.5 2.5 conditional.4
  132.1 255.1 %while.69 = (s32[]{:T(128)}, bf16[1,512,128]{2,1,0:T(8,128)(2,1)S(1)}, bf16[1,512,128]{2,1,0:T(8,128)(2,1)S(1)}, f32[1,512]{1,0:T(1,128)S(1)}, f32[1,512]{1,0:T(...) while((s32[]{:T(128)}, ...), condition=%wide.region_16.17_spmd.clone, body=%wide.region_13.16_spmd.clone.sunk | while | flops 271517184 | bytes 6615599 | solution.py:135
  132.1 2.3 collective-permute-start
  144.6 1.9 collective-permute-done.3
  146.5 2.3 conditional.13
  158.6 3.0 collective-permute-done.4
  163.6 3.0 collective-permute-start
  174.3 5.2 collective-permute-done.4
  221.1 1.9 collective-permute-done.3
  235.6 1.9 collective-permute-done.3
  250.2 1.9 collective-permute-done.3
  305.3 2.6 collective-permute-done.4
  319.8 2.1 collective-permute-done.4
  354.3 1.9 collective-permute-done.3
  369.7 1.9 collective-permute-done.3
  388.5 35.2 %while.68 = (s32[]{:T(128)}, f32[512,128]{1,0:T(8,128)S(1)}, s32[]{:T(128)}, s32[16384]{0:T(1024)S(1)}, s32[]{:T(128)}, /*index=5*/s32[512]{0:T(512)}, bf16[1638...) while((s32[]{:T(128)}, f32[512,128]{1,0:T(8,128)S(1)}, ...), condition=%wide.region_10.11_spmd.clone, body=%wide.region_7.10_spmd.clone.sunk | while | flops 407963136 | bytes 5811651 | solution.py:92
  390.5 3.7 conditional.12
  392.0 2.2 fusion.15
  424.4 56.9 %reduce-scatter.3.cloned.1.call-done = f32[64,128]{1,0:T(8,128)} async-done(((f32[512,128]{1,0:T(8,128)}), f32[64,128]{1,0:T(8,128)}) %reduce-scatter.3.cloned.1.call-update) | async-done | bytes 32784 | tf_op jit(solution)/shard_map/reduce_scatter | solution.py:140
  482.7 33.1 %reduce-scatter.5.cloned.1.call-done = f32[64,128]{1,0:T(8,128)} async-done(((f32[512,128]{1,0:T(8,128)}), f32[64,128]{1,0:T(8,128)}) %reduce-scatter.5.cloned.1.call-update) | async-done | bytes 32784 | tf_op jit(solution)/shard_map/reduce_scatter | solution.py:141
  (469 shorter events, 239.9 us)
Async XLA Ops:
  7.2 88.1 %all-gather.4.cloned.1.call-start = ((), (), s32[]{:S(2)}) async-start(), calls=%async_computation.2 | async-start | bytes 4325376 | tf_op jit(solution)/shard_map/all_gather | solution.py:37
  7.9 380.6 %all-gather.6.cloned.1.call-start = ((), (), s32[]{:S(2)}) async-start(), calls=%async_computation.3 | async-start | bytes 4325376 | tf_op jit(solution)/shard_map/all_gather | solution.py:38
  8.6 472.7 %reduce-scatter.3.cloned.1.call-start = ((), (), s32[]{:S(2)}) async-start(), calls=%async_computation.4 | async-start | bytes 294912 | tf_op jit(solution)/shard_map/reduce_scatter | solution.py:140
  132.1 14.5 %collective-permute-start = (bf16[1,512,128]{2,1,0:T(8,128)(2,1)S(1)}, bf16[1,512,128]{2,1,0:T(8,128)(2,1)S(1)}, u32[]{:S(2)}, u32[]{:S(2)}) collective-permute-start(bf16[1,512,128]{2,1,0:T(8,128)(2,1)S(1)} %get-tuple-element.1675), channel_id=1, source_target_pairs={{8,0},{16,8},{24,16},{32,24},{40,32},{48,40},{56,48},{64,56},{72,6... | collective-permute-start | bytes 393224 | tf_op jit(solution)/shard_map/while/body/eval_jaxpr/ppermute | solution.py:12
  148.9 14.6 %collective-permute-start = (bf16[1,512,128]{2,1,0:T(8,128)(2,1)S(1)}, bf16[1,512,128]{2,1,0:T(8,128)(2,1)S(1)}, u32[]{:S(2)}, u32[]{:S(2)}) collective-permute-start(bf16[1,512,128]{2,1,0:T(8,128)(2,1)S(1)} %get-tuple-element.1675), channel_id=1, source_target_pairs={{8,0},{16,8},{24,16},{32,24},{40,32},{48,40},{56,48},{64,56},{72,6... | collective-permute-start | bytes 393224 | tf_op jit(solution)/shard_map/while/body/eval_jaxpr/ppermute | solution.py:12
  163.6 17.9 %collective-permute-start = (bf16[1,512,128]{2,1,0:T(8,128)(2,1)S(1)}, bf16[1,512,128]{2,1,0:T(8,128)(2,1)S(1)}, u32[]{:S(2)}, u32[]{:S(2)}) collective-permute-start(bf16[1,512,128]{2,1,0:T(8,128)(2,1)S(1)} %get-tuple-element.1675), channel_id=1, source_target_pairs={{8,0},{16,8},{24,16},{32,24},{40,32},{48,40},{56,48},{64,56},{72,6... | collective-permute-start | bytes 393224 | tf_op jit(solution)/shard_map/while/body/eval_jaxpr/ppermute | solution.py:12
  166.6 14.9 %collective-permute-start.1 = (bf16[1,512,128]{2,1,0:T(8,128)(2,1)S(1)}, bf16[1,512,128]{2,1,0:T(8,128)(2,1)S(1)}, u32[]{:S(2)}, u32[]{:S(2)}) collective-permute-start(bf16[1,512,128]{2,1,0:T(8,128)(2,1)S(1)} %get-tuple-element.1676), channel_id=1, source_target_pairs={{8,0},{16,8},{24,16},{32,24},{40,32},{48,40},{56,48},{64,56},{72,6... | collective-permute-start | bytes 393224 | tf_op jit(solution)/shard_map/while/body/eval_jaxpr/ppermute | solution.py:12
  181.6 13.5 %collective-permute-start = (bf16[1,512,128]{2,1,0:T(8,128)(2,1)S(1)}, bf16[1,512,128]{2,1,0:T(8,128)(2,1)S(1)}, u32[]{:S(2)}, u32[]{:S(2)}) collective-permute-start(bf16[1,512,128]{2,1,0:T(8,128)(2,1)S(1)} %get-tuple-element.1675), channel_id=1, source_target_pairs={{8,0},{16,8},{24,16},{32,24},{40,32},{48,40},{56,48},{64,56},{72,6... | collective-permute-start | bytes 393224 | tf_op jit(solution)/shard_map/while/body/eval_jaxpr/ppermute | solution.py:12
  195.1 13.4 %collective-permute-start = (bf16[1,512,128]{2,1,0:T(8,128)(2,1)S(1)}, bf16[1,512,128]{2,1,0:T(8,128)(2,1)S(1)}, u32[]{:S(2)}, u32[]{:S(2)}) collective-permute-start(bf16[1,512,128]{2,1,0:T(8,128)(2,1)S(1)} %get-tuple-element.1675), channel_id=1, source_target_pairs={{8,0},{16,8},{24,16},{32,24},{40,32},{48,40},{56,48},{64,56},{72,6... | collective-permute-start | bytes 393224 | tf_op jit(solution)/shard_map/while/body/eval_jaxpr/ppermute | solution.py:12
  208.6 14.4 %collective-permute-start = (bf16[1,512,128]{2,1,0:T(8,128)(2,1)S(1)}, bf16[1,512,128]{2,1,0:T(8,128)(2,1)S(1)}, u32[]{:S(2)}, u32[]{:S(2)}) collective-permute-start(bf16[1,512,128]{2,1,0:T(8,128)(2,1)S(1)} %get-tuple-element.1675), channel_id=1, source_target_pairs={{8,0},{16,8},{24,16},{32,24},{40,32},{48,40},{56,48},{64,56},{72,6... | collective-permute-start | bytes 393224 | tf_op jit(solution)/shard_map/while/body/eval_jaxpr/ppermute | solution.py:12
  223.1 14.4 %collective-permute-start = (bf16[1,512,128]{2,1,0:T(8,128)(2,1)S(1)}, bf16[1,512,128]{2,1,0:T(8,128)(2,1)S(1)}, u32[]{:S(2)}, u32[]{:S(2)}) collective-permute-start(bf16[1,512,128]{2,1,0:T(8,128)(2,1)S(1)} %get-tuple-element.1675), channel_id=1, source_target_pairs={{8,0},{16,8},{24,16},{32,24},{40,32},{48,40},{56,48},{64,56},{72,6... | collective-permute-start | bytes 393224 | tf_op jit(solution)/shard_map/while/body/eval_jaxpr/ppermute | solution.py:12
  237.6 14.5 %collective-permute-start = (bf16[1,512,128]{2,1,0:T(8,128)(2,1)S(1)}, bf16[1,512,128]{2,1,0:T(8,128)(2,1)S(1)}, u32[]{:S(2)}, u32[]{:S(2)}) collective-permute-start(bf16[1,512,128]{2,1,0:T(8,128)(2,1)S(1)} %get-tuple-element.1675), channel_id=1, source_target_pairs={{8,0},{16,8},{24,16},{32,24},{40,32},{48,40},{56,48},{64,56},{72,6... | collective-permute-start | bytes 393224 | tf_op jit(solution)/shard_map/while/body/eval_jaxpr/ppermute | solution.py:12
  252.2 14.4 %collective-permute-start = (bf16[1,512,128]{2,1,0:T(8,128)(2,1)S(1)}, bf16[1,512,128]{2,1,0:T(8,128)(2,1)S(1)}, u32[]{:S(2)}, u32[]{:S(2)}) collective-permute-start(bf16[1,512,128]{2,1,0:T(8,128)(2,1)S(1)} %get-tuple-element.1675), channel_id=1, source_target_pairs={{8,0},{16,8},{24,16},{32,24},{40,32},{48,40},{56,48},{64,56},{72,6... | collective-permute-start | bytes 393224 | tf_op jit(solution)/shard_map/while/body/eval_jaxpr/ppermute | solution.py:12
  266.7 14.4 %collective-permute-start = (bf16[1,512,128]{2,1,0:T(8,128)(2,1)S(1)}, bf16[1,512,128]{2,1,0:T(8,128)(2,1)S(1)}, u32[]{:S(2)}, u32[]{:S(2)}) collective-permute-start(bf16[1,512,128]{2,1,0:T(8,128)(2,1)S(1)} %get-tuple-element.1675), channel_id=1, source_target_pairs={{8,0},{16,8},{24,16},{32,24},{40,32},{48,40},{56,48},{64,56},{72,6... | collective-permute-start | bytes 393224 | tf_op jit(solution)/shard_map/while/body/eval_jaxpr/ppermute | solution.py:12
  281.2 14.4 %collective-permute-start = (bf16[1,512,128]{2,1,0:T(8,128)(2,1)S(1)}, bf16[1,512,128]{2,1,0:T(8,128)(2,1)S(1)}, u32[]{:S(2)}, u32[]{:S(2)}) collective-permute-start(bf16[1,512,128]{2,1,0:T(8,128)(2,1)S(1)} %get-tuple-element.1675), channel_id=1, source_target_pairs={{8,0},{16,8},{24,16},{32,24},{40,32},{48,40},{56,48},{64,56},{72,6... | collective-permute-start | bytes 393224 | tf_op jit(solution)/shard_map/while/body/eval_jaxpr/ppermute | solution.py:12
  295.7 14.4 %collective-permute-start = (bf16[1,512,128]{2,1,0:T(8,128)(2,1)S(1)}, bf16[1,512,128]{2,1,0:T(8,128)(2,1)S(1)}, u32[]{:S(2)}, u32[]{:S(2)}) collective-permute-start(bf16[1,512,128]{2,1,0:T(8,128)(2,1)S(1)} %get-tuple-element.1675), channel_id=1, source_target_pairs={{8,0},{16,8},{24,16},{32,24},{40,32},{48,40},{56,48},{64,56},{72,6... | collective-permute-start | bytes 393224 | tf_op jit(solution)/shard_map/while/body/eval_jaxpr/ppermute | solution.py:12
  310.2 15.3 %collective-permute-start = (bf16[1,512,128]{2,1,0:T(8,128)(2,1)S(1)}, bf16[1,512,128]{2,1,0:T(8,128)(2,1)S(1)}, u32[]{:S(2)}, u32[]{:S(2)}) collective-permute-start(bf16[1,512,128]{2,1,0:T(8,128)(2,1)S(1)} %get-tuple-element.1675), channel_id=1, source_target_pairs={{8,0},{16,8},{24,16},{32,24},{40,32},{48,40},{56,48},{64,56},{72,6... | collective-permute-start | bytes 393224 | tf_op jit(solution)/shard_map/while/body/eval_jaxpr/ppermute | solution.py:12
  325.6 15.3 %collective-permute-start = (bf16[1,512,128]{2,1,0:T(8,128)(2,1)S(1)}, bf16[1,512,128]{2,1,0:T(8,128)(2,1)S(1)}, u32[]{:S(2)}, u32[]{:S(2)}) collective-permute-start(bf16[1,512,128]{2,1,0:T(8,128)(2,1)S(1)} %get-tuple-element.1675), channel_id=1, source_target_pairs={{8,0},{16,8},{24,16},{32,24},{40,32},{48,40},{56,48},{64,56},{72,6... | collective-permute-start | bytes 393224 | tf_op jit(solution)/shard_map/while/body/eval_jaxpr/ppermute | solution.py:12
  327.5 13.4 %collective-permute-start.1 = (bf16[1,512,128]{2,1,0:T(8,128)(2,1)S(1)}, bf16[1,512,128]{2,1,0:T(8,128)(2,1)S(1)}, u32[]{:S(2)}, u32[]{:S(2)}) collective-permute-start(bf16[1,512,128]{2,1,0:T(8,128)(2,1)S(1)} %get-tuple-element.1676), channel_id=1, source_target_pairs={{8,0},{16,8},{24,16},{32,24},{40,32},{48,40},{56,48},{64,56},{72,6... | collective-permute-start | bytes 393224 | tf_op jit(solution)/shard_map/while/body/eval_jaxpr/ppermute | solution.py:12
  341.0 15.3 %collective-permute-start = (bf16[1,512,128]{2,1,0:T(8,128)(2,1)S(1)}, bf16[1,512,128]{2,1,0:T(8,128)(2,1)S(1)}, u32[]{:S(2)}, u32[]{:S(2)}) collective-permute-start(bf16[1,512,128]{2,1,0:T(8,128)(2,1)S(1)} %get-tuple-element.1675), channel_id=1, source_target_pairs={{8,0},{16,8},{24,16},{32,24},{40,32},{48,40},{56,48},{64,56},{72,6... | collective-permute-start | bytes 393224 | tf_op jit(solution)/shard_map/while/body/eval_jaxpr/ppermute | solution.py:12
  356.4 15.3 %collective-permute-start = (bf16[1,512,128]{2,1,0:T(8,128)(2,1)S(1)}, bf16[1,512,128]{2,1,0:T(8,128)(2,1)S(1)}, u32[]{:S(2)}, u32[]{:S(2)}) collective-permute-start(bf16[1,512,128]{2,1,0:T(8,128)(2,1)S(1)} %get-tuple-element.1675), channel_id=1, source_target_pairs={{8,0},{16,8},{24,16},{32,24},{40,32},{48,40},{56,48},{64,56},{72,6... | collective-permute-start | bytes 393224 | tf_op jit(solution)/shard_map/while/body/eval_jaxpr/ppermute | solution.py:12
  358.3 13.4 %collective-permute-start.1 = (bf16[1,512,128]{2,1,0:T(8,128)(2,1)S(1)}, bf16[1,512,128]{2,1,0:T(8,128)(2,1)S(1)}, u32[]{:S(2)}, u32[]{:S(2)}) collective-permute-start(bf16[1,512,128]{2,1,0:T(8,128)(2,1)S(1)} %get-tuple-element.1676), channel_id=1, source_target_pairs={{8,0},{16,8},{24,16},{32,24},{40,32},{48,40},{56,48},{64,56},{72,6... | collective-permute-start | bytes 393224 | tf_op jit(solution)/shard_map/while/body/eval_jaxpr/ppermute | solution.py:12
  371.8 15.3 %collective-permute-start = (bf16[1,512,128]{2,1,0:T(8,128)(2,1)S(1)}, bf16[1,512,128]{2,1,0:T(8,128)(2,1)S(1)}, u32[]{:S(2)}, u32[]{:S(2)}) collective-permute-start(bf16[1,512,128]{2,1,0:T(8,128)(2,1)S(1)} %get-tuple-element.1675), channel_id=1, source_target_pairs={{8,0},{16,8},{24,16},{32,24},{40,32},{48,40},{56,48},{64,56},{72,6... | collective-permute-start | bytes 393224 | tf_op jit(solution)/shard_map/while/body/eval_jaxpr/ppermute | solution.py:12
  387.9 127.9 %reduce-scatter.5.cloned.1.call-start = ((), (), s32[]{:S(2)}) async-start(), calls=%async_computation.5 | async-start | bytes 294912 | tf_op jit(solution)/shard_map/reduce_scatter | solution.py:141
  (74 other events, 911.3 us)
Sparse Core Ops, SparseCore 0:
  10.6 84.5 all-gather.3
  97.8 82.7 all-gather.5
  388.0 93.2 reduce-scatter.2
  483.9 31.9 reduce-scatter.4
where the time goes:
time: 528 us; the launch traced here: 524 us
  waiting for transfers between devices  173 us (33%)
  starting transfers between devices  165 us (31%)
  loops' own time  67.7 us (13%)
  blocking collectives  51.2 us (10%)
  local copies, waits for them, and re-layouts  34.9 us (7%)
  between operations  15.3 us (3%)
  matrix products  10.2 us (2%)
  other arithmetic  6.49 us (1%)
    ppermute x85, starting transfers between devices, shifted(): return lax.ppermute(block, axis, route)  165 us
    reduce_scatter x1, waiting for transfers between devices, local(): lax.psum_scatter(dk_part, 'head', scatter_dimension=0, tiled=True)  56.9 us
    ppermute x85, waiting for transfers between devices, shifted(): return lax.ppermute(block, axis, route)  53 us
    all_gather x1, blocking collectives, local(): lax.all_gather(docs_words, 'ctx', axis=0, tiled=True)  51.2 us
    reduce_scatter x1, waiting for transfers between devices, local(): lax.psum_scatter(dv_part, 'head', scatter_dimension=0, tiled=True)  33.1 us
    all_gather x1, waiting for transfers between devices, local(): lax.all_gather(keys, 'ctx', axis=0, tiled=True)  28.2 us
    another operation x1, loops' own time, local(): lax.fori_loop(0, span, fetch, (queries, dout, lse_own, delta_own, docs_fl...  24.6 us
    another operation x1, loops' own time, local(): lax.fori_loop(0, nblock, stat_step, (jnp.full((rows,), -1e+30, jnp.float3...  21.2 us
  transfers between devices with their start and end apart: 89, of which 34 were waited for; matrix products, arithmetic and copies ran while one was open for 9% of the time, Pallas kernels for 0%

commit v1 on v0

v1 whole, which is shorter than its diff:
```python
import functools
import math

import jax
import jax.numpy as jnp
from jax import lax
from jax.experimental import pallas as pl
from jax.experimental.pallas import tpu as pltpu
from jax.sharding import Mesh
from jax.sharding import PartitionSpec as P

BF16 = jnp.bfloat16
F32 = jnp.float32
NY, NX, NC = 4, 4, 2
DOCS = 64
EXTRA = 16
LOW = -1e30
TILE = 256
LOG2E = 1.0 / math.log(2.0)


def dot(left, right, left_dim, right_dim):
    return lax.dot_general(
        left, right, (((left_dim,), (right_dim,)), ((), ())), preferred_element_type=F32
    )


def split_row(row, count):
    part = row.shape[1] // count
    return [row[:, i * part : (i + 1) * part] for i in range(count)]


def rows_to_line(block):
    return jnp.concatenate([block[i : i + 1] for i in range(block.shape[0])], axis=1)


def prep_kernel(place, q, do, out, keys, values, docs, sent, pieces):
    tok, width = q.shape
    at = tok + EXTRA
    docs_rows = jnp.concatenate(split_row(docs[...].astype(F32), tok // width), axis=0)
    sent[0:tok, :] = q[...]
    pad = jnp.zeros((EXTRA - docs_rows.shape[0], width), F32)
    sent[tok:at, :] = jnp.concatenate([docs_rows, pad], axis=0).astype(BF16)
    prod = do[...].astype(F32) * out[...].astype(F32)
    delta = jnp.sum(jnp.transpose(prod), axis=0, keepdims=True)
    rows = jnp.concatenate(split_row(delta, tok // width), axis=0)
    high = rows.astype(BF16).astype(F32)
    middle = (rows - high).astype(BF16).astype(F32)
    low = rows - high - middle
    pad = jnp.zeros((EXTRA - 3 * rows.shape[0], width), F32)
    sent[at : at + tok, :] = do[...]
    sent[at + tok : 2 * at, :] = jnp.concatenate([high, middle, low, pad], axis=0).astype(BF16)
    share = (pieces.shape[1] - EXTRA) // 2
    first = pl.multiple_of(place[0] * share, share)
    line = lax.broadcasted_iota(jnp.int32, docs_rows.shape, 0)
    mine = jnp.sum(jnp.where(line == place[0] // NC, docs_rows, 0.0), axis=0, keepdims=True)
    line = lax.broadcasted_iota(jnp.int32, (EXTRA, width), 0)
    extra = jnp.where(line == 0, mine, 0.0).astype(BF16)
    key_rows, value_rows = keys[pl.ds(first, share), :], values[pl.ds(first, share), :]
    for i in range(pieces.shape[0]):
        pieces[i, 0:share, :] = key_rows
        pieces[i, share : share + EXTRA, :] = extra
        pieces[i, share + EXTRA :, :] = value_rows


def high_kernel(share, nz, place, rows, ends):
    x, y, z = place[1], place[2], place[3]
    tok = rows.shape[2]
    line = lax.broadcasted_iota(jnp.int32, (1, tok), 1)
    for m in range(NX):
        before, skipped = (lax.rem(y + x - m + NX, NY) * nz + z) * share, place[0] * share
        rows[m] = (before + jnp.clip(line - skipped + 1, 0, share)).astype(F32)
        ends[m, 0] = before + jnp.clip(1 - skipped, 0, share)
        ends[m, 1] = before + jnp.clip(tok - skipped, 0, share)


def tile_loops(bounds, m, step, carry):
    first = bounds[m, 0] // TILE
    last = (bounds[m, 3] + TILE - 1) // TILE
    full_first = jnp.minimum((bounds[m, 1] + TILE - 1) // TILE, last)
    full_last = jnp.maximum(bounds[m, 2] // TILE, full_first)
    carry = lax.fori_loop(first, full_first, functools.partial(step, True), carry)
    carry = lax.fori_loop(full_first, full_last, functools.partial(step, False), carry)
    return lax.fori_loop(full_last, last, functools.partial(step, True), carry)


def visible_of(tile, tok, low, high):
    index = (lax.broadcasted_iota(jnp.int32, (TILE, tok), 0) + tile * TILE).astype(F32)
    return (index >= low) & (index < high)


def stats_kernel(factor, place, ends, own, peer, high_in, p0, p1, p2, p3, lse, key_all, low_out, bounds):
    x, y, c = place[1], place[2], place[4]
    nz, rows, width = p2.shape
    share = rows - EXTRA
    tok = own.shape[1] // 2 - EXTRA
    number = lax.broadcasted_iota(jnp.int32, (DOCS, width), 0).astype(F32)
    below = jnp.zeros((DOCS, width), F32)
    for k, piece in enumerate((p0, p1, p2, p3)):
        for i in range(nz):
            where = block_row(y, k, i, nz, share)
            key_all[pl.ds(where, share), :] = piece[i, 0:share, :]
            docs = piece[i, share : share + EXTRA, :].astype(F32)[0:1, :]
            below = below + jnp.where(docs < number, 1.0, 0.0)
    lane = lax.broadcasted_iota(jnp.int32, (DOCS, width), 1)
    ours = (lane >= c * share) & (lane < (c + 1) * share)
    below = jnp.sum(jnp.where(ours, below, 0.0), axis=1, keepdims=True)
    number = lax.broadcasted_iota(jnp.int32, (DOCS, tok), 0).astype(F32)
    for m in range(NY):
        docs = rows_to_line(own[m, tok : tok + EXTRA, :].astype(F32)[0 : tok // width])
        low = jnp.sum(jnp.where(docs == number, below, 0.0), axis=0, keepdims=True)
        low_out[m] = low
        bounds[m, 0] = jnp.min(low).astype(jnp.int32)
        bounds[m, 1] = jnp.max(low).astype(jnp.int32)
        bounds[m, 2] = ends[m, 0]
        bounds[m, 3] = ends[m, 1]

    def group(m, carry):
        low = low_out[m]
        high = high_in[m]
        pair = [sets[m, 0:tok, :] for sets in (own, peer)]

        def step(masked, tile, state):
            key = key_all[pl.ds(pl.multiple_of(tile * TILE, TILE), TILE), :]
            visible = visible_of(tile, tok, low, high) if masked else None
            after = []
            for query, (top, total) in zip(pair, state):
                score = dot(key, query, 1, 1) * factor
                if masked:
                    score = jnp.where(visible, score, LOW)
                new_top = jnp.maximum(top, jnp.max(score, axis=0, keepdims=True))
                terms = jnp.sum(jnp.exp2(score - new_top), axis=0, keepdims=True)
                after.append((new_top, total * jnp.exp2(top - new_top) + terms))
            return tuple(after)

        start = (jnp.full((1, tok), LOW, F32), jnp.zeros((1, tok), F32))
        for half, (top, total) in enumerate(tile_loops(bounds, m, step, (start,) * NC)):
            lse[NC * lax.rem(x - m + NX, NX) + (NC - 1 - c if half else c)] = jnp.where(top > LOW, top + jnp.log2(jnp.maximum(total, 1e-30)), LOW)
        return carry

    lax.fori_loop(0, NY, group, 0)


def join(*parts):
    top = functools.reduce(jnp.maximum, parts)
    return top + jnp.log2(sum(jnp.exp2(part - top) for part in parts))


def grad_kernel(
    factor, scale, place, bounds, own, peer, high_in, p0, p1, p2, p3, key_all, low_in, l0, l1, l2, l3,
    dq_own, dq_peer, here, up, down, far_dk, far_dv, value_all, dk, dv, lse, dq_turned,
):
    x, y, c = place[1], place[2], place[4]
    nz, share, width = p2.shape
    slab = nz * share
    tok = own.shape[1] // 2 - EXTRA
    for k, piece in enumerate((p0, p1, p2, p3)):
        for i in range(nz):
            where = block_row(y, k, i, nz, share)
            value_all[pl.ds(where, share), :] = piece[i, piece.shape[1] - share :, :]
    dk[...] = jnp.zeros_like(dk)
    dv[...] = jnp.zeros_like(dv)
    lse[...] = join(l0[...], l1[...], l2[...], l3[...])
    n = tok // width

    def group(m, carry):
        low = low_in[m]
        high = high_in[m]
        heads = []
        for sets, head in ((own, c), (peer, NC - 1 - c)):
            at = tok + EXTRA
            extra = sets[m, at + tok : 2 * at, :].astype(F32)
            delta = rows_to_line(extra[0:n] + extra[n : 2 * n] + extra[2 * n : 3 * n])
            heads.append((sets[m, 0:tok, :], sets[m, at : at + tok, :], delta, lse[NC * lax.rem(x - m + NX, NX) + head]))
        dq_turned[...] = jnp.zeros_like(dq_turned)

        def step(masked, tile, carry):
            at = pl.ds(pl.multiple_of(tile * TILE, TILE), TILE)
            key, value = key_all[at, :], value_all[at, :]
            visible = visible_of(tile, tok, low, high) if masked else None
            new_dk, new_dv = dk[at, :], dv[at, :]
            for half, (query, grad, delta, norm) in enumerate(heads):
                prob = jnp.exp2(dot(key, query, 1, 1) * factor - norm)
                if masked:
                    prob = jnp.where(visible, prob, 0.0)
                dprob = dot(value, grad, 1, 1)
                dscore = (prob * (dprob - delta)).astype(BF16)
                new_dv = new_dv + dot(prob.astype(BF16), grad, 1, 0)
                new_dk = new_dk + dot(dscore, query, 1, 0)
                dq_turned[half] += dot(key, dscore, 0, 0)
            dk[at, :] = new_dk
            dv[at, :] = new_dv
            return carry

        tile_loops(bounds, m, step, 0)
        dq_own[m] = jnp.transpose(dq_turned[0]) * scale
        dq_peer[m] = jnp.transpose(dq_turned[1]) * scale
        return carry

    lax.fori_loop(0, NY, group, 0)

    def slab_of(ref, by):
        at = pl.ds(pl.multiple_of(lax.rem(y + by, NY) * slab, slab), slab)
        return (ref[at, :] * (scale if ref is dk else 1.0)).astype(BF16).reshape(nz, share, width)

    for out, by in ((here, 0), (up, 1), (down, NY - 1)):
        out[:, 0] = slab_of(dk, by)
        out[:, 1] = slab_of(dv, by)
    far_dk[...] = slab_of(dk, 2)
    far_dv[...] = slab_of(dv, 2)


def block_row(y, k, i, nz, share):
    return pl.multiple_of((lax.rem(y - k + NY, NY) * nz + i) * share, share)


def query_kernel(own, there, *outs):
    for k, out in enumerate(outs):
        out[...] = (own[k] + there[k]).astype(BF16)


def stack_kernel(*refs):
    for i, piece in enumerate(refs[:-1]):
        refs[-1][i] = piece[...]


def add_kernel(*refs):
    total = refs[0][...].astype(F32)
    for ref in refs[1:-1]:
        total = total + ref[...].astype(F32)
    refs[-1][...] = total.astype(BF16)


def relay_kernel(up, down, got_dk, got_dv, new_up, new_down):
    new_up[:, 0] = (up[:, 0].astype(F32) + got_dk[...].astype(F32)).astype(BF16)
    new_up[:, 1] = up[:, 1]
    new_down[:, 0] = down[:, 0]
    new_down[:, 1] = (down[:, 1].astype(F32) + got_dv[...].astype(F32)).astype(BF16)


def last_kernel(blocks, dk, dv):
    total = blocks[0].astype(F32)
    for i in range(1, blocks.shape[0]):
        total = total + blocks[i].astype(F32)
    dk[...] = total[0].astype(BF16)
    dv[...] = total[1].astype(BF16)


SMEM = pl.BlockSpec(memory_space=pltpu.SMEM)
VMEM = pl.BlockSpec(memory_space=pltpu.VMEM)


def call(kernel, out_shape, in_specs, out_specs, scratch=(), flops=0, moved=0, limit=40):
    return pl.pallas_call(
        kernel,
        out_shape=out_shape,
        in_specs=in_specs,
        out_specs=out_specs,
        scratch_shapes=list(scratch),
        compiler_params=pltpu.CompilerParams(vmem_limit_bytes=limit * 2**20),
        cost_estimate=pl.CostEstimate(flops=flops, bytes_accessed=moved, transcendentals=0),
    )


def ring(size, by):
    return [(i, (i + by) % size) for i in range(size)]


def local(queries, keys, values, outputs, dout, docs):
    heads, tok, width = queries.shape
    nz = lax.axis_size("z")
    scale = 1.0 / math.sqrt(width)
    factor = scale * LOG2E
    x, y, z, c = (lax.axis_index(name) for name in ("x", "y", "z", "c"))
    place = jnp.stack([x * NC + c, x, y, z, c]).astype(jnp.int32)
    share = tok // (NX * NC)
    shape = jax.ShapeDtypeStruct
    swap = ring(NC, 1)

    def shift(k, back=False):
        pairs = [(b * NX + a, (b - a) % NY * NX + (a + k) % NX) for b in range(NY) for a in range(NX)]
        return [(j, i) for i, j in pairs] if back else pairs

    sent, pieces = call(
        prep_kernel,
        (shape((2 * (tok + EXTRA), width), BF16), shape((nz, 2 * share + EXTRA, width), BF16)),
        [SMEM] + [VMEM] * 6,
        [VMEM] * 2,
        moved=2 * 2**20,
        limit=60,
    )(place, queries[0], dout[0], outputs[0], keys, values, docs.reshape(1, tok))

    skewed = lax.ppermute(sent, ("y", "x"), shift(0))
    along = lax.all_to_all(pieces, "z", 0, 0, tiled=True)
    along, skewed = lax.optimization_barrier((along, skewed))
    moved = [skewed] + [lax.ppermute(skewed, "x", ring(NX, k)) for k in (1, 2, 3)]
    before = lax.ppermute(along, "y", ring(NY, 1))
    after = lax.ppermute(along, "y", ring(NY, -1))
    far_keys = lax.ppermute(before[:, : share + EXTRA], "y", ring(NY, 1))
    far_values = lax.ppermute(after[:, share + EXTRA :], "y", ring(NY, -1))
    moved, far_keys, far_values = lax.optimization_barrier((moved, far_keys, far_values))
    own = call(stack_kernel, shape((NX,) + sent.shape, BF16), [VMEM] * NX, VMEM, moved=2**21)(
        *moved
    )
    peer = lax.ppermute(own, "c", swap)

    total = share * nz * NY
    high, ends = call(
        functools.partial(high_kernel, share, nz),
        (shape((NY, 1, tok), F32), shape((NY, 2), jnp.int32)),
        [SMEM],
        [VMEM, SMEM],
    )(place)
    lse_part, key_all, low, bounds = call(
        functools.partial(stats_kernel, factor),
        (
            shape((NC * NY, 1, tok), F32),
            shape((total, width), BF16),
            shape((NY, 1, tok), F32),
            shape((NY, 4), jnp.int32),
        ),
        [SMEM] * 2 + [VMEM] * 7,
        [VMEM] * 3 + [SMEM],
        flops=2 * 10**9,
        moved=4 * 2**20,
    )(place, ends, own, peer, high, along, before, far_keys, after)

    lse_chip = join(lse_part, lax.ppermute(lse_part, "c", swap))
    lse_all = [lse_chip] + [lax.ppermute(lse_chip, "x", ring(NX, k)) for k in (1, 3, 2)]

    dq_shape = shape((NY, tok, width), F32)
    slab_shape = shape((nz, 2, share, width), BF16)
    far_shape = shape((nz, share, width), BF16)
    dq_own, dq_peer, here, up, down, far_dk, far_dv = call(
        functools.partial(grad_kernel, factor, scale),
        (dq_shape, dq_shape, slab_shape, slab_shape, slab_shape, far_shape, far_shape),
        [SMEM] * 2 + [VMEM] * 13,
        [VMEM] * 7,
        scratch=(
            pltpu.VMEM((total, width), BF16),
            pltpu.VMEM((total, width), F32),
            pltpu.VMEM((total, width), F32),
            pltpu.VMEM((NC * NY, 1, tok), F32),
            pltpu.VMEM((NC, width, tok), F32),
        ),
        flops=8 * 10**9,
        moved=8 * 2**20,
    )(place, bounds, own, peer, high, along, before, far_values, after, key_all, low, *lse_all)

    one = shape((tok, width), BF16)
    kept, *away = call(query_kernel, (one,) * NX, [VMEM] * 2, [VMEM] * NX, moved=3 * 2**20)(
        dq_own, lax.ppermute(dq_peer, "c", swap)
    )
    got_dk = lax.ppermute(far_dk, "y", ring(NY, 1))
    got_dv = lax.ppermute(far_dv, "y", ring(NY, -1))
    up, down = call(relay_kernel, (slab_shape,) * 2, [VMEM] * 4, [VMEM] * 2, moved=5 * 2**18)(up, down, got_dk, got_dv)
    arrived = [here, lax.ppermute(up, "y", ring(NY, 1)), lax.ppermute(down, "y", ring(NY, -1))]
    away = [lax.ppermute(away[k - 1], "x", ring(NX, -k)) for k in (1, 2, 3)]
    arrived, away = lax.optimization_barrier((arrived, away))
    slab_sum = call(add_kernel, slab_shape, [VMEM] * 3, VMEM, moved=5 * 2**18)(*arrived)
    blocks = lax.all_to_all(slab_sum, "z", 0, 0, tiled=True)
    half = shape((share, width), BF16)
    dk, dv = call(last_kernel, (half, half), [VMEM], [VMEM] * 2, moved=2**18)(blocks)

    dq = call(add_kernel, one, [VMEM] * 4, VMEM, moved=2**19)(kept, *away)
    dq = lax.ppermute(dq, ("y", "x"), shift(0, True))
    return dq[None], dk, dv


def solution(mesh):
    nz = mesh.devices.shape[0] // NY
    fine = Mesh(mesh.devices.reshape(NY, nz, NX, NC), ("y", "z", "x", "c"))
    tokens, heads = ("y", "z"), ("x", "c")
    in_specs = (
        P(heads, tokens, None),
        P(tokens, None),
        P(tokens, None),
        P(heads, tokens, None),
        P(heads, tokens, None),
        P(tokens),
    )
    out_specs = (P(heads, tokens, None), P(tokens + heads, None), P(tokens + heads, None))
    return jax.shard_map(local, mesh=fine, in_specs=in_specs, out_specs=out_specs, check_vma=False)
```

time: 528 us -> 109 us (0.21)
  waiting for transfers between devices: 173 us -> 44.5 us
  starting transfers between devices: 165 us -> 38.5 us
  loops' own time: 67.7 us -> 0 us
  blocking collectives: 51.2 us -> 0 us
  local copies, waits for them, and re-layouts: 34.9 us -> 1.35 us
  Pallas kernels: 0 us -> 23.1 us
  between operations: 15.3 us -> 0.76 us
  matrix products: 10.2 us -> 0 us
  other arithmetic: 6.49 us -> 0.07 us
    ppermute x85 -> x22, starting transfers between devices: 165 us -> 25.3 us  [the longest x3 4.58 us: local(): lax.ppermute(skewed, 'x', ring(NX, k))]
    reduce_scatter x2 -> x0, waiting for transfers between devices: 90.1 us -> none  [the longest x1 56.9 us: local(): lax.psum_scatter(dk_part, 'head', scatter_dimension=0, tiled=True)]
    another operation x53 -> x0, loops' own time: 67.7 us -> none  [the longest x1 24.6 us: local(): lax.fori_loop(0, span, fetch, (queries, dout, lse_own, delta_own, docs_fl...]
    all_gather x1 -> x0, blocking collectives: 51.2 us -> none  [local(): lax.all_gather(docs_words, 'ctx', axis=0, tiled=True)]
    all_gather x2 -> x0, waiting for transfers between devices: 28.2 us -> none  [the longest x1 28.2 us: local(): lax.all_gather(keys, 'ctx', axis=0, tiled=True)]
    ppermute x85 -> x22, waiting for transfers between devices: 53 us -> 25.9 us  [the longest x3 7.81 us: local(): lax.ppermute(skewed, 'x', ring(NX, k))]
    pallas_call x0 -> x10, Pallas kernels: none -> 23.1 us  [the longest x1 11 us: local(): call(functools.partial(grad_kernel, factor, scale), (dq_shape, dq_shape,...]
    dynamic_slice x34 -> x0, local copies, waits for them, and re-layouts: 20.1 us -> none  [the longest x32 20.1 us: needed(): return (start <= qlast) & (src_docs[start + count - 1] >= qdoc_first)]
  transfers between devices with their start and end apart: 89 -> 24, of which waited for: 34 -> 16; matrix products, arithmetic and copies ran while one was open for 9% -> 0% of each run, Pallas kernels for 0% -> 1%
where the time goes in v1:
time: 109 us; the launch traced here: 108 us
  waiting for transfers between devices  44.5 us (41%)
  starting transfers between devices  38.5 us (35%)
  Pallas kernels  23.1 us (21%)
  local copies, waits for them, and re-layouts  1.35 us (1%)
    pallas_call x1, Pallas kernels, local(): call(functools.partial(grad_kernel, factor, scale), (dq_shape, dq_shape,...  11 us
    all_to_all x1, waiting for transfers between devices, local(): along = lax.all_to_all(pieces, 'z', 0, 0, tiled=True)  9.52 us
    all_to_all x1, waiting for transfers between devices, local(): blocks = lax.all_to_all(slab_sum, 'z', 0, 0, tiled=True)  9.1 us
    all_to_all x1, starting transfers between devices, local(): along = lax.all_to_all(pieces, 'z', 0, 0, tiled=True)  8.57 us
    ppermute x3, waiting for transfers between devices, local(): lax.ppermute(skewed, 'x', ring(NX, k))  7.81 us
    pallas_call x1, Pallas kernels, local(): call(functools.partial(stats_kernel, factor), (shape((NC * NY, 1, tok), F...  7.15 us
    all_to_all x1, starting transfers between devices, local(): blocks = lax.all_to_all(slab_sum, 'z', 0, 0, tiled=True)  4.69 us
    ppermute x3, starting transfers between devices, local(): lax.ppermute(skewed, 'x', ring(NX, k))  4.58 us
  transfers between devices with their start and end apart: 24, of which 16 were waited for; matrix products, arithmetic and copies ran while one was open for 0% of the time, Pallas kernels for 1%

profile of v1, /device:TPU:32, one launch (start us, length us, event | category | flops | bytes accessed | tf_op | source)
XLA Modules:
  0.0 108.4 jit_solution(6619733517458958372)
XLA Ops:
  1.3 2.1 %shard_map.86 = (bf16[1056,128]{1,0:T(8,128)(2,1)}, bf16[8,144,128]{2,1,0:T(8,128)(2,1)}) custom-call(s32[5]{0:T(128)} %stack.23.place, bf16[512,128]{1,0:T(8,128)(2,1)} %bitcast.11, bf16[512,128]{1,0:T(8,128)(2,1)} %bitcast.12, bf16[512,128]{1,0:T(8,128)(2,1)} %bitcast.13, bf16[512,128]{1,0:T(8,128)(2,1)} %keys.1, bf16[512,128]{1,0:T(8,128)(2,1)} %values.1, ...), custom_call_target="tpu_custom_call" | custom-call | bytes 2097152 | tf_op jit(solution)/shard_map/pallas_call | solution.py:284
  3.4 8.6 %all-to-all-start = ((bf16[8,144,128]{2,1,0:T(8,128)(2,1)}), bf16[8,144,128]{2,1,0:T(8,128)(2,1)S(1)}, u32[]{:S(2)}, u32[]{:S(2)}) async-start(bf16[8,144,128]{2,1,0:T(8,128)(2,1)} %get-tuple-element.41), calls=%async_computation | async-start | bytes 589824 | tf_op jit(solution)/shard_map/all_to_all | solution.py:294
  12.0 1.6 %collective-permute-start = (bf16[1056,128]{1,0:T(8,128)(2,1)}, bf16[1056,128]{1,0:T(8,128)(2,1)S(1)}, u32[]{:S(2)}, u32[]{:S(2)}) collective-permute-start(bf16[1056,128]{1,0:T(8,128)(2,1)} %get-tuple-element.42), channel_id=1, source_target_pairs={{0,0},{2,194},{4,132},{6,70},{64,64},{66,2},{68,196},{70,134},{128... | collective-permute-start | bytes 811016 | tf_op jit(solution)/shard_map/ppermute | solution.py:293
  13.6 9.5 %all-to-all-done.p0 = bf16[8,144,128]{2,1,0:T(8,128)(2,1)S(1)} async-done(((bf16[8,144,128]{2,1,0:T(8,128)(2,1)}), bf16[8,144,128]{2,1,0:T(8,128)(2,1)S(1)}, u32[]{:S(2)}, u32[]{:S(2)}) %all-to-all-start) | async-done | bytes 294944 | tf_op jit(solution)/shard_map/all_to_all | solution.py:294
  23.1 1.6 %collective-permute-start.4 = (bf16[8,144,128]{2,1,0:T(8,128)(2,1)S(1)}, bf16[8,144,128]{2,1,0:T(8,128)(2,1)S(1)}, u32[]{:S(2)}, u32[]{:S(2)}) collective-permute-start(bf16[8,144,128]{2,1,0:T(8,128)(2,1)S(1)} %all-to-all-done.p0), channel_id=1, source_target_pairs={{0,64},{64,128},{128,192},{192,0},{1,65},{65,129},{129,193},{193,1... | collective-permute-start | bytes 884744 | tf_op jit(solution)/shard_map/ppermute | solution.py:297
  24.7 1.7 %collective-permute-start.6 = (bf16[8,144,128]{2,1,0:T(8,128)(2,1)S(1)}, bf16[8,144,128]{2,1,0:T(8,128)(2,1)S(1)}, u32[]{:S(2)}, u32[]{:S(2)}) collective-permute-start(bf16[8,144,128]{2,1,0:T(8,128)(2,1)S(1)} %all-to-all-done.p0), channel_id=1, source_target_pairs={{0,192},{64,0},{128,64},{192,128},{1,193},{65,1},{129,65},{193,129... | collective-permute-start | bytes 884744 | tf_op jit(solution)/shard_map/ppermute | solution.py:298
  26.3 2.8 %collective-permute-start.3 = (bf16[1056,128]{1,0:T(8,128)(2,1)S(1)}, bf16[1056,128]{1,0:T(8,128)(2,1)S(1)}, u32[]{:S(2)}, u32[]{:S(2)}) collective-permute-start(bf16[1056,128]{1,0:T(8,128)(2,1)S(1)} %collective-permute-done.refs_0_), channel_id=1, source_target_pairs={{0,6},{2,0},{4,2},{6,4},{1,7},{3,1},{5,3},{7,5},{8,14},{10,8},{12,... | collective-permute-start | bytes 811016 | tf_op jit(solution)/shard_map/ppermute | solution.py:296
  32.0 2.5 %collective-permute-start.7 = (bf16[8,64,128]{2,1,0:T(8,128)(2,1)S(1)}, bf16[8,64,128]{2,1,0:T(8,128)(2,1)S(1)}, u32[]{:S(2)}, u32[]{:S(2)}) collective-permute-start(bf16[8,64,128]{2,1,0:T(8,128)(2,1)S(1)} %slice.9), channel_id=1, source_target_pairs={{0,192},{64,0},{128,64},{192,128},{1,193},{65,1},{129,65},{193,129... | collective-permute-start | bytes 393224 | tf_op jit(solution)/shard_map/ppermute | solution.py:300
  34.4 4.1 %collective-permute-done.3.refs_3_ = bf16[1056,128]{1,0:T(8,128)(2,1)S(1)} collective-permute-done((bf16[1056,128]{1,0:T(8,128)(2,1)S(1)}, bf16[1056,128]{1,0:T(8,128)(2,1)S(1)}, u32[]{:S(2)}, u32[]{:S(2)}) %collective-permute-start.3) | collective-permute-done | bytes 270368 | tf_op jit(solution)/shard_map/ppermute | solution.py:296
  39.5 2.8 %collective-permute-done.1.refs_1_ = bf16[1056,128]{1,0:T(8,128)(2,1)S(1)} collective-permute-done((bf16[1056,128]{1,0:T(8,128)(2,1)S(1)}, bf16[1056,128]{1,0:T(8,128)(2,1)S(1)}, u32[]{:S(2)}, u32[]{:S(2)}) %collective-permute-start.1) | collective-permute-done | bytes 270368 | tf_op jit(solution)/shard_map/ppermute | solution.py:296
  43.6 1.5 %collective-permute-done.8.peer = bf16[4,1056,128]{2,1,0:T(8,128)(2,1)S(1)} collective-permute-done((bf16[4,1056,128]{2,1,0:T(8,128)(2,1)S(1)}, bf16[4,1056,128]{2,1,0:T(8,128)(2,1)S(1)}, u32[]{:S(2)}, u32[]{:S(2)}) %collective-permute-start.8) | collective-permute-done | bytes 1081376 | tf_op jit(solution)/shard_map/ppermute | solution.py:305
  45.1 7.1 %shard_map.88 = (f32[8,1,512]{2,1,0:T(1,128)S(1)}, bf16[2048,128]{1,0:T(8,128)(2,1)S(1)}, f32[4,1,512]{2,1,0:T(1,128)S(1)}, s32[4,4]{1,0:T(4,128)S(1)}) custom-call(s32[5]{0:T(128)S(1)} %copy-done, s32[4,2]{1,0:T(4,128)S(1)} %get-tuple-element.40.ends, bf16[4,1056,128]{2,1,0:T(8,128)(2,1)S(1)} %shard_map.87.own, ...), custom_call_target="tpu_custom_call" | custom-call | flops 2000000000 | bytes 4194304 | tf_op jit(solution)/shard_map/pallas_call | solution.py:314
  54.4 1.2 %collective-permute-start.11 = (f32[8,1,512]{2,1,0:T(1,128)S(1)}, f32[8,1,512]{2,1,0:T(1,128)S(1)}, u32[]{:S(2)}, u32[]{:S(2)}) collective-permute-start(f32[8,1,512]{2,1,0:T(1,128)S(1)} %multiply_add_fusion.l0), channel_id=1, source_target_pairs={{0,6},{2,0},{4,2},{6,4},{1,7},{3,1},{5,3},{7,5},{8,14},{10,8},{12,... | collective-permute-start | bytes 49160 | tf_op jit(solution)/shard_map/ppermute | solution.py:329
  56.4 2.5 %collective-permute-done.12.l3 = f32[8,1,512]{2,1,0:T(1,128)S(1)} collective-permute-done((f32[8,1,512]{2,1,0:T(1,128)S(1)}, f32[8,1,512]{2,1,0:T(1,128)S(1)}, u32[]{:S(2)}, u32[]{:S(2)}) %collective-permute-start.12) | collective-permute-done | bytes 16416 | tf_op jit(solution)/shard_map/ppermute | solution.py:329
  59.0 1.6 %collective-permute-done.10.l1 = f32[8,1,512]{2,1,0:T(1,128)S(1)} collective-permute-done((f32[8,1,512]{2,1,0:T(1,128)S(1)}, f32[8,1,512]{2,1,0:T(1,128)S(1)}, u32[]{:S(2)}, u32[]{:S(2)}) %collective-permute-start.10) | collective-permute-done | bytes 16416 | tf_op jit(solution)/shard_map/ppermute | solution.py:329
  60.6 11.0 %shard_map.89 = (f32[4,512,128]{2,1,0:T(8,128)S(1)}, f32[4,512,128]{2,1,0:T(8,128)S(1)}, bf16[8,2,64,128]{3,2,1,0:T(8,128)(2,1)S(1)}, bf16[8,2,64,128]{3,2,1,0:T...) custom-call(s32[5]{0:T(128)S(1)} %copy-done, ...), custom_call_target="tpu_custom_call" | custom-call | flops 8000000000 | bytes 8388608 | tf_op jit(solution)/shard_map/pallas_call | solution.py:334
  72.0 2.9 %collective-permute-start.15 = (bf16[8,64,128]{2,1,0:T(8,128)(2,1)S(1)}, bf16[8,64,128]{2,1,0:T(8,128)(2,1)S(1)}, u32[]{:S(2)}, u32[]{:S(2)}) collective-permute-start(bf16[8,64,128]{2,1,0:T(8,128)(2,1)S(1)} %get-tuple-element.63), channel_id=1, source_target_pairs={{0,192},{64,0},{128,64},{192,128},{1,193},{65,1},{129,65},{193,129... | collective-permute-start | bytes 393224 | tf_op jit(solution)/shard_map/ppermute | solution.py:355
  75.0 3.8 %collective-permute-done.14.got_dk = bf16[8,64,128]{2,1,0:T(8,128)(2,1)S(1)} collective-permute-done((bf16[8,64,128]{2,1,0:T(8,128)(2,1)S(1)}, bf16[8,64,128]{2,1,0:T(8,128)(2,1)S(1)}, u32[]{:S(2)}, u32[]{:S(2)}) %collective-permute-start.14) | collective-permute-done | bytes 131104 | tf_op jit(solution)/shard_map/ppermute | solution.py:354
  79.3 2.9 %collective-permute-start.17 = (bf16[8,2,64,128]{3,2,1,0:T(8,128)(2,1)S(1)}, bf16[8,2,64,128]{3,2,1,0:T(8,128)(2,1)S(1)}, u32[]{:S(2)}, u32[]{:S(2)}) collective-permute-start(bf16[8,2,64,128]{3,2,1,0:T(8,128)(2,1)S(1)} %get-tuple-element.65), channel_id=1, source_target_pairs={{0,192},{64,0},{128,64},{192,128},{1,193},{65,1},{129,65},{193,129... | collective-permute-start | bytes 786440 | tf_op jit(solution)/shard_map/ppermute | solution.py:357
  84.4 3.6 %collective-permute-done.16.refs_1_ = bf16[8,2,64,128]{3,2,1,0:T(8,128)(2,1)S(1)} collective-permute-done((bf16[8,2,64,128]{3,2,1,0:T(8,128)(2,1)S(1)}, bf16[8,2,64,128]{3,2,1,0:T(8,128)(2,1)S(1)}, u32[]{:S(2)}, u32[]{:S(2)}) %collective-permute-start.16) | collective-permute-done | bytes 262176 | tf_op jit(solution)/shard_map/ppermute | solution.py:357
  88.3 2.2 %collective-permute-done.19.refs_2_ = bf16[512,128]{1,0:T(8,128)(2,1)S(1)} collective-permute-done((bf16[512,128]{1,0:T(8,128)(2,1)S(1)}, bf16[512,128]{1,0:T(8,128)(2,1)S(1)}, u32[]{:S(2)}, u32[]{:S(2)}) %collective-permute-start.19) | collective-permute-done | bytes 131104 | tf_op jit(solution)/shard_map/ppermute | solution.py:358
  90.5 1.3 %collective-permute-done.20.refs_3_ = bf16[512,128]{1,0:T(8,128)(2,1)S(1)} collective-permute-done((bf16[512,128]{1,0:T(8,128)(2,1)S(1)}, bf16[512,128]{1,0:T(8,128)(2,1)S(1)}, u32[]{:S(2)}, u32[]{:S(2)}) %collective-permute-start.20) | collective-permute-done | bytes 131104 | tf_op jit(solution)/shard_map/ppermute | solution.py:358
  92.5 4.7 %all-to-all-start.1 = ((bf16[8,2,64,128]{3,2,1,0:T(8,128)(2,1)}), bf16[8,2,64,128]{3,2,1,0:T(8,128)(2,1)S(1)}, u32[]{:S(2)}, u32[]{:S(2)}) async-start(bf16[8,2,64,128]{3,2,1,0:T(8,128)(2,1)} %shard_map.93), calls=%async_computation.1 | async-start | bytes 524288 | tf_op jit(solution)/shard_map/all_to_all | solution.py:361
  98.0 9.1 %all-to-all-done.1.blocks = bf16[8,2,64,128]{3,2,1,0:T(8,128)(2,1)S(1)} async-done(((bf16[8,2,64,128]{3,2,1,0:T(8,128)(2,1)}), bf16[8,2,64,128]{3,2,1,0:T(8,128)(2,1)S(1)}, u32[]{:S(2)}, u32[]{:S(2)}) %all-to-all-start.1) | async-done | bytes 262176 | tf_op jit(solution)/shard_map/all_to_all | solution.py:361
  (41 shorter events, 15.1 us)
Async XLA Ops:
  3.4 19.7 %all-to-all-start = ((bf16[8,144,128]{2,1,0:T(8,128)(2,1)}), bf16[8,144,128]{2,1,0:T(8,128)(2,1)S(1)}, u32[]{:S(2)}, u32[]{:S(2)}) async-start(bf16[8,144,128]{2,1,0:T(8,128)(2,1)} %get-tuple-element.41), calls=%async_computation | async-start | bytes 589824 | tf_op jit(solution)/shard_map/all_to_all | solution.py:294
  12.0 1.6 %collective-permute-start = (bf16[1056,128]{1,0:T(8,128)(2,1)}, bf16[1056,128]{1,0:T(8,128)(2,1)S(1)}, u32[]{:S(2)}, u32[]{:S(2)}) collective-permute-start(bf16[1056,128]{1,0:T(8,128)(2,1)} %get-tuple-element.42), channel_id=1, source_target_pairs={{0,0},{2,194},{4,132},{6,70},{64,64},{66,2},{68,196},{70,134},{128... | collective-permute-start | bytes 811016 | tf_op jit(solution)/shard_map/ppermute | solution.py:293
  23.1 7.9 %collective-permute-start.4 = (bf16[8,144,128]{2,1,0:T(8,128)(2,1)S(1)}, bf16[8,144,128]{2,1,0:T(8,128)(2,1)S(1)}, u32[]{:S(2)}, u32[]{:S(2)}) collective-permute-start(bf16[8,144,128]{2,1,0:T(8,128)(2,1)S(1)} %all-to-all-done.p0), channel_id=1, source_target_pairs={{0,64},{64,128},{128,192},{192,0},{1,65},{65,129},{129,193},{193,1... | collective-permute-start | bytes 884744 | tf_op jit(solution)/shard_map/ppermute | solution.py:297
  24.7 7.3 %collective-permute-start.6 = (bf16[8,144,128]{2,1,0:T(8,128)(2,1)S(1)}, bf16[8,144,128]{2,1,0:T(8,128)(2,1)S(1)}, u32[]{:S(2)}, u32[]{:S(2)}) collective-permute-start(bf16[8,144,128]{2,1,0:T(8,128)(2,1)S(1)} %all-to-all-done.p0), channel_id=1, source_target_pairs={{0,192},{64,0},{128,64},{192,128},{1,193},{65,1},{129,65},{193,129... | collective-permute-start | bytes 884744 | tf_op jit(solution)/shard_map/ppermute | solution.py:298
  26.3 12.2 %collective-permute-start.3 = (bf16[1056,128]{1,0:T(8,128)(2,1)S(1)}, bf16[1056,128]{1,0:T(8,128)(2,1)S(1)}, u32[]{:S(2)}, u32[]{:S(2)}) collective-permute-start(bf16[1056,128]{1,0:T(8,128)(2,1)S(1)} %collective-permute-done.refs_0_), channel_id=1, source_target_pairs={{0,6},{2,0},{4,2},{6,4},{1,7},{3,1},{5,3},{7,5},{8,14},{10,8},{12,... | collective-permute-start | bytes 811016 | tf_op jit(solution)/shard_map/ppermute | solution.py:296
  29.1 10.4 %collective-permute-start.2 = (bf16[1056,128]{1,0:T(8,128)(2,1)S(1)}, bf16[1056,128]{1,0:T(8,128)(2,1)S(1)}, u32[]{:S(2)}, u32[]{:S(2)}) collective-permute-start(bf16[1056,128]{1,0:T(8,128)(2,1)S(1)} %collective-permute-done.refs_0_), channel_id=1, source_target_pairs={{0,4},{2,6},{4,0},{6,2},{1,5},{3,7},{5,1},{7,3},{8,12},{10,14},{12... | collective-permute-start | bytes 811016 | tf_op jit(solution)/shard_map/ppermute | solution.py:296
  29.9 12.4 %collective-permute-start.1 = (bf16[1056,128]{1,0:T(8,128)(2,1)S(1)}, bf16[1056,128]{1,0:T(8,128)(2,1)S(1)}, u32[]{:S(2)}, u32[]{:S(2)}) collective-permute-start(bf16[1056,128]{1,0:T(8,128)(2,1)S(1)} %collective-permute-done.refs_0_), channel_id=1, source_target_pairs={{0,2},{2,4},{4,6},{6,0},{1,3},{3,5},{5,7},{7,1},{8,10},{10,12},{12... | collective-permute-start | bytes 811016 | tf_op jit(solution)/shard_map/ppermute | solution.py:296
  31.0 11.2 %collective-permute-start.5 = (bf16[8,80,128]{2,1,0:T(8,128)(2,1)S(1)}, bf16[8,80,128]{2,1,0:T(8,128)(2,1)S(1)}, u32[]{:S(2)}, u32[]{:S(2)}) collective-permute-start(bf16[8,80,128]{2,1,0:T(8,128)(2,1)S(1)} %slice.8), channel_id=1, source_target_pairs={{0,64},{64,128},{128,192},{192,0},{1,65},{65,129},{129,193},{193,1... | collective-permute-start | bytes 491528 | tf_op jit(solution)/shard_map/ppermute | solution.py:299
  32.0 10.3 %collective-permute-start.7 = (bf16[8,64,128]{2,1,0:T(8,128)(2,1)S(1)}, bf16[8,64,128]{2,1,0:T(8,128)(2,1)S(1)}, u32[]{:S(2)}, u32[]{:S(2)}) collective-permute-start(bf16[8,64,128]{2,1,0:T(8,128)(2,1)S(1)} %slice.9), channel_id=1, source_target_pairs={{0,192},{64,0},{128,64},{192,128},{1,193},{65,1},{129,65},{193,129... | collective-permute-start | bytes 393224 | tf_op jit(solution)/shard_map/ppermute | solution.py:300
  42.3 2.8 %collective-permute-start.8 = (bf16[4,1056,128]{2,1,0:T(8,128)(2,1)S(1)}, bf16[4,1056,128]{2,1,0:T(8,128)(2,1)S(1)}, u32[]{:S(2)}, u32[]{:S(2)}) collective-permute-start(bf16[4,1056,128]{2,1,0:T(8,128)(2,1)S(1)} %shard_map.87.own), channel_id=1, source_target_pairs={{0,1},{1,0},{2,3},{3,2},{4,5},{5,4},{6,7},{7,6},{8,9},{9,8},{10,11... | collective-permute-start | bytes 3244040 | tf_op jit(solution)/shard_map/ppermute | solution.py:305
  52.3 1.3 %collective-permute-start.9 = (f32[8,1,512]{2,1,0:T(1,128)S(1)}, f32[8,1,512]{2,1,0:T(1,128)S(1)}, u32[]{:S(2)}, u32[]{:S(2)}) collective-permute-start(f32[8,1,512]{2,1,0:T(1,128)S(1)} %get-tuple-element.55), channel_id=1, source_target_pairs={{0,1},{1,0},{2,3},{3,2},{4,5},{5,4},{6,7},{7,6},{8,9},{9,8},{10,11... | collective-permute-start | bytes 49160 | tf_op jit(solution)/shard_map/ppermute | solution.py:328
  53.6 5.3 %collective-permute-start.12 = (f32[8,1,512]{2,1,0:T(1,128)S(1)}, f32[8,1,512]{2,1,0:T(1,128)S(1)}, u32[]{:S(2)}, u32[]{:S(2)}) collective-permute-start(f32[8,1,512]{2,1,0:T(1,128)S(1)} %multiply_add_fusion.l0), channel_id=1, source_target_pairs={{0,4},{2,6},{4,0},{6,2},{1,5},{3,7},{5,1},{7,3},{8,12},{10,14},{12... | collective-permute-start | bytes 49160 | tf_op jit(solution)/shard_map/ppermute | solution.py:329
  54.4 4.5 %collective-permute-start.11 = (f32[8,1,512]{2,1,0:T(1,128)S(1)}, f32[8,1,512]{2,1,0:T(1,128)S(1)}, u32[]{:S(2)}, u32[]{:S(2)}) collective-permute-start(f32[8,1,512]{2,1,0:T(1,128)S(1)} %multiply_add_fusion.l0), channel_id=1, source_target_pairs={{0,6},{2,0},{4,2},{6,4},{1,7},{3,1},{5,3},{7,5},{8,14},{10,8},{12,... | collective-permute-start | bytes 49160 | tf_op jit(solution)/shard_map/ppermute | solution.py:329
  55.6 5.0 %collective-permute-start.10 = (f32[8,1,512]{2,1,0:T(1,128)S(1)}, f32[8,1,512]{2,1,0:T(1,128)S(1)}, u32[]{:S(2)}, u32[]{:S(2)}) collective-permute-start(f32[8,1,512]{2,1,0:T(1,128)S(1)} %multiply_add_fusion.l0), channel_id=1, source_target_pairs={{0,2},{2,4},{4,6},{6,0},{1,3},{3,5},{5,7},{7,1},{8,10},{10,12},{12... | collective-permute-start | bytes 49160 | tf_op jit(solution)/shard_map/ppermute | solution.py:329
  71.6 10.6 %collective-permute-start.13 = (f32[4,512,128]{2,1,0:T(8,128)S(1)}, f32[4,512,128]{2,1,0:T(8,128)S(1)}, u32[]{:S(2)}, u32[]{:S(2)}) collective-permute-start(f32[4,512,128]{2,1,0:T(8,128)S(1)} %get-tuple-element.57), channel_id=1, source_target_pairs={{0,1},{1,0},{2,3},{3,2},{4,5},{5,4},{6,7},{7,6},{8,9},{9,8},{10,11... | collective-permute-start | bytes 3145736 | tf_op jit(solution)/shard_map/ppermute | solution.py:352
  71.7 7.1 %collective-permute-start.14 = (bf16[8,64,128]{2,1,0:T(8,128)(2,1)S(1)}, bf16[8,64,128]{2,1,0:T(8,128)(2,1)S(1)}, u32[]{:S(2)}, u32[]{:S(2)}) collective-permute-start(bf16[8,64,128]{2,1,0:T(8,128)(2,1)S(1)} %get-tuple-element.62), channel_id=1, source_target_pairs={{0,64},{64,128},{128,192},{192,0},{1,65},{65,129},{129,193},{193,1... | collective-permute-start | bytes 393224 | tf_op jit(solution)/shard_map/ppermute | solution.py:354
  72.0 6.7 %collective-permute-start.15 = (bf16[8,64,128]{2,1,0:T(8,128)(2,1)S(1)}, bf16[8,64,128]{2,1,0:T(8,128)(2,1)S(1)}, u32[]{:S(2)}, u32[]{:S(2)}) collective-permute-start(bf16[8,64,128]{2,1,0:T(8,128)(2,1)S(1)} %get-tuple-element.63), channel_id=1, source_target_pairs={{0,192},{64,0},{128,64},{192,128},{1,193},{65,1},{129,65},{193,129... | collective-permute-start | bytes 393224 | tf_op jit(solution)/shard_map/ppermute | solution.py:355
  78.9 9.1 %collective-permute-start.16 = (bf16[8,2,64,128]{3,2,1,0:T(8,128)(2,1)S(1)}, bf16[8,2,64,128]{3,2,1,0:T(8,128)(2,1)S(1)}, u32[]{:S(2)}, u32[]{:S(2)}) collective-permute-start(bf16[8,2,64,128]{3,2,1,0:T(8,128)(2,1)S(1)} %get-tuple-element.64), channel_id=1, source_target_pairs={{0,64},{64,128},{128,192},{192,0},{1,65},{65,129},{129,193},{193,1... | collective-permute-start | bytes 786440 | tf_op jit(solution)/shard_map/ppermute | solution.py:357
  79.3 8.7 %collective-permute-start.17 = (bf16[8,2,64,128]{3,2,1,0:T(8,128)(2,1)S(1)}, bf16[8,2,64,128]{3,2,1,0:T(8,128)(2,1)S(1)}, u32[]{:S(2)}, u32[]{:S(2)}) collective-permute-start(bf16[8,2,64,128]{3,2,1,0:T(8,128)(2,1)S(1)} %get-tuple-element.65), channel_id=1, source_target_pairs={{0,192},{64,0},{128,64},{192,128},{1,193},{65,1},{129,65},{193,129... | collective-permute-start | bytes 786440 | tf_op jit(solution)/shard_map/ppermute | solution.py:357
  82.3 6.0 %collective-permute-start.18 = (bf16[512,128]{1,0:T(8,128)(2,1)S(1)}, bf16[512,128]{1,0:T(8,128)(2,1)S(1)}, u32[]{:S(2)}, u32[]{:S(2)}) collective-permute-start(bf16[512,128]{1,0:T(8,128)(2,1)S(1)} %get-tuple-element.66), channel_id=1, source_target_pairs={{0,6},{2,0},{4,2},{6,4},{1,7},{3,1},{5,3},{7,5},{8,14},{10,8},{12,... | collective-permute-start | bytes 393224 | tf_op jit(solution)/shard_map/ppermute | solution.py:358
  83.2 7.3 %collective-permute-start.19 = (bf16[512,128]{1,0:T(8,128)(2,1)S(1)}, bf16[512,128]{1,0:T(8,128)(2,1)S(1)}, u32[]{:S(2)}, u32[]{:S(2)}) collective-permute-start(bf16[512,128]{1,0:T(8,128)(2,1)S(1)} %get-tuple-element.67), channel_id=1, source_target_pairs={{0,4},{2,6},{4,0},{6,2},{1,5},{3,7},{5,1},{7,3},{8,12},{10,14},{12... | collective-permute-start | bytes 393224 | tf_op jit(solution)/shard_map/ppermute | solution.py:358
  83.9 7.8 %collective-permute-start.20 = (bf16[512,128]{1,0:T(8,128)(2,1)S(1)}, bf16[512,128]{1,0:T(8,128)(2,1)S(1)}, u32[]{:S(2)}, u32[]{:S(2)}) collective-permute-start(bf16[512,128]{1,0:T(8,128)(2,1)S(1)} %get-tuple-element.68), channel_id=1, source_target_pairs={{0,2},{2,4},{4,6},{6,0},{1,3},{3,5},{5,7},{7,1},{8,10},{10,12},{12... | collective-permute-start | bytes 393224 | tf_op jit(solution)/shard_map/ppermute | solution.py:358
  92.5 14.5 %all-to-all-start.1 = ((bf16[8,2,64,128]{3,2,1,0:T(8,128)(2,1)}), bf16[8,2,64,128]{3,2,1,0:T(8,128)(2,1)S(1)}, u32[]{:S(2)}, u32[]{:S(2)}) async-start(bf16[8,2,64,128]{3,2,1,0:T(8,128)(2,1)} %shard_map.93), calls=%async_computation.1 | async-start | bytes 524288 | tf_op jit(solution)/shard_map/all_to_all | solution.py:361
  97.3 0.7 collective-permute-start.21
  (1 other events, 10.5 us)

commit v2 on v1

--- a/solution.py
+++ b/solution.py
@@ -25,6 +25,10 @@
     )
 
 
+def share_index():
+    return lax.axis_index("x") * NC + lax.axis_index("c")
+
+
 def split_row(row, count):
     part = row.shape[1] // count
     return [row[:, i * part : (i + 1) * part] for i in range(count)]
@@ -34,7 +38,7 @@
     return jnp.concatenate([block[i : i + 1] for i in range(block.shape[0])], axis=1)
 
 
-def prep_kernel(place, q, do, out, keys, values, docs, sent, pieces):
+def prep_kernel(q, do, out, keys, values, docs, sent, pieces):
     tok, width = q.shape
     at = tok + EXTRA
     docs_rows = jnp.concatenate(split_row(docs[...].astype(F32), tok // width), axis=0)
@@ -51,9 +55,9 @@
     sent[at : at + tok, :] = do[...]
     sent[at + tok : 2 * at, :] = jnp.concatenate([high, middle, low, pad], axis=0).astype(BF16)
     share = (pieces.shape[1] - EXTRA) // 2
-    first = pl.multiple_of(place[0] * share, share)
+    first = pl.multiple_of(share_index() * share, share)
     line = lax.broadcasted_iota(jnp.int32, docs_rows.shape, 0)
-    mine = jnp.sum(jnp.where(line == place[0] // NC, docs_rows, 0.0), axis=0, keepdims=True)
+    mine = jnp.sum(jnp.where(line == share_index() // NC, docs_rows, 0.0), axis=0, keepdims=True)
     line = lax.broadcasted_iota(jnp.int32, (EXTRA, width), 0)
     extra = jnp.where(line == 0, mine, 0.0).astype(BF16)
     key_rows, value_rows = keys[pl.ds(first, share), :], values[pl.ds(first, share), :]
@@ -63,34 +67,42 @@
         pieces[i, share + EXTRA :, :] = value_rows
 
 
-def high_kernel(share, nz, place, rows, ends):
-    x, y, z = place[1], place[2], place[3]
+def high_kernel(share, nz, rows, ends):
+    x, y, z = (lax.axis_index(name) for name in ("x", "y", "z"))
     tok = rows.shape[2]
     line = lax.broadcasted_iota(jnp.int32, (1, tok), 1)
     for m in range(NX):
-        before, skipped = (lax.rem(y + x - m + NX, NY) * nz + z) * share, place[0] * share
+        before, skipped = (lax.rem(y + x - m + NX, NY) * nz + z) * share, share_index() * share
         rows[m] = (before + jnp.clip(line - skipped + 1, 0, share)).astype(F32)
         ends[m, 0] = before + jnp.clip(1 - skipped, 0, share)
         ends[m, 1] = before + jnp.clip(tok - skipped, 0, share)
 
 
-def tile_loops(bounds, m, step, carry):
-    first = bounds[m, 0] // TILE
-    last = (bounds[m, 3] + TILE - 1) // TILE
-    full_first = jnp.minimum((bounds[m, 1] + TILE - 1) // TILE, last)
-    full_last = jnp.maximum(bounds[m, 2] // TILE, full_first)
-    carry = lax.fori_loop(first, full_first, functools.partial(step, True), carry)
-    carry = lax.fori_loop(full_first, full_last, functools.partial(step, False), carry)
-    return lax.fori_loop(full_last, last, functools.partial(step, True), carry)
-
-
-def visible_of(tile, tok, low, high):
-    index = (lax.broadcasted_iota(jnp.int32, (TILE, tok), 0) + tile * TILE).astype(F32)
+def tile_loops(bounds, m, share, step, carry):
+    start = bounds[m, 0] // share * share
+    count = (bounds[m, 3] - start) // share
+    fold = TILE // share
+    rest = lax.rem(count - 1, fold) + 1
+    whole = (count - rest) // fold
+    unclear = jnp.clip((bounds[m, 1] - start + TILE - 1) // TILE, 0, whole)
+
+    def run(masked, size, i, carry):
+        return step(masked, size, pl.multiple_of(start + i * TILE, share), carry)
+
+    carry = lax.fori_loop(0, unclear, functools.partial(run, True, TILE), carry)
+    carry = lax.fori_loop(unclear, whole, functools.partial(run, False, TILE), carry)
+    small = jnp.where(2 * rest <= fold, 1, 0)
+    carry = lax.fori_loop(whole, whole + small, functools.partial(run, True, TILE // 2), carry)
+    return lax.fori_loop(whole, whole + 1 - small, functools.partial(run, True, TILE), carry)
+
+
+def visible_of(first, size, tok, low, high):
+    index = (lax.broadcasted_iota(jnp.int32, (size, tok), 0) + first).astype(F32)
     return (index >= low) & (index < high)
 
 
-def stats_kernel(factor, place, ends, own, peer, high_in, p0, p1, p2, p3, lse, key_all, low_out, bounds):
-    x, y, c = place[1], place[2], place[4]
+def stats_kernel(factor, ends, own, peer, high_in, p0, p1, p2, p3, lse, key_all, low_out, bounds):
+    x, y, c = (lax.axis_index(name) for name in ("x", "y", "c"))
     nz, rows, width = p2.shape
     share = rows - EXTRA
     tok = own.shape[1] // 2 - EXTRA
@@ -102,6 +114,8 @@
             key_all[pl.ds(where, share), :] = piece[i, 0:share, :]
             docs = piece[i, share : share + EXTRA, :].astype(F32)[0:1, :]
             below = below + jnp.where(docs < number, 1.0, 0.0)
+    end = NY * nz * share
+    key_all[end:, :] = jnp.zeros_like(key_all[end:, :])
     lane = lax.broadcasted_iota(jnp.int32, (DOCS, width), 1)
     ours = (lane >= c * share) & (lane < (c + 1) * share)
     below = jnp.sum(jnp.where(ours, below, 0.0), axis=1, keepdims=True)
@@ -120,21 +134,26 @@
         high = high_in[m]
         pair = [sets[m, 0:tok, :] for sets in (own, peer)]
 
-        def step(masked, tile, state):
-            key = key_all[pl.ds(pl.multiple_of(tile * TILE, TILE), TILE), :]
-            visible = visible_of(tile, tok, low, high) if masked else None
+        def step(masked, size, first, state):
+            key = key_all[pl.ds(first, size), :]
+            visible = visible_of(first, size, tok, low, high) if masked else None
             after = []
             for query, (top, total) in zip(pair, state):
                 score = dot(key, query, 1, 1) * factor
                 if masked:
                     score = jnp.where(visible, score, LOW)
-                new_top = jnp.maximum(top, jnp.max(score, axis=0, keepdims=True))
-                terms = jnp.sum(jnp.exp2(score - new_top), axis=0, keepdims=True)
-                after.append((new_top, total * jnp.exp2(top - new_top) + terms))
+                for part in range(size // 64):
+                    piece = score[part * 64 : (part + 1) * 64].reshape(8, 8, tok)
+                    new_top = jnp.maximum(top, jnp.max(piece, axis=0))
+                    terms = jnp.sum(jnp.exp2(piece - new_top[None]), axis=0)
+                    top, total = new_top, total * jnp.exp2(top - new_top) + terms
+                after.append((top, total))
             return tuple(after)
 
-        start = (jnp.full((1, tok), LOW, F32), jnp.zeros((1, tok), F32))
-        for half, (top, total) in enumerate(tile_loops(bounds, m, step, (start,) * NC)):
+        start = (jnp.full((8, tok), LOW, F32), jnp.zeros((8, tok), F32))
+        for half, (top, total) in enumerate(tile_loops(bounds, m, share, step, (start,) * NC)):
+            tops, top = top, jnp.max(top, axis=0, keepdims=True)
+            total = jnp.sum(total * jnp.exp2(tops - top), axis=0, keepdims=True)
             lse[NC * lax.rem(x - m + NX, NX) + (NC - 1 - c if half else c)] = jnp.where(top > LOW, top + jnp.log2(jnp.maximum(total, 1e-30)), LOW)
         return carry
 
@@ -147,10 +166,10 @@
 
 
 def grad_kernel(
-    factor, scale, place, bounds, own, peer, high_in, p0, p1, p2, p3, key_all, low_in, l0, l1, l2, l3,
+    factor, scale, bounds, own, peer, high_in, p0, p1, p2, p3, key_all, low_in, l0, l1, l2, l3,
     dq_own, dq_peer, here, up, down, far_dk, far_dv, value_all, dk, dv, lse, dq_turned,
 ):
-    x, y, c = place[1], place[2], place[4]
+    x, y, c = (lax.axis_index(name) for name in ("x", "y", "c"))
     nz, share, width = p2.shape
     slab = nz * share
     tok = own.shape[1] // 2 - EXTRA
@@ -158,6 +177,7 @@
         for i in range(nz):
             where = block_row(y, k, i, nz, share)
             value_all[pl.ds(where, share), :] = piece[i, piece.shape[1] - share :, :]
+    value_all[NY * slab :, :] = jnp.zeros_like(value_all[NY * slab :, :])
     dk[...] = jnp.zeros_like(dk)
     dv[...] = jnp.zeros_like(dv)
     lse[...] = join(l0[...], l1[...], l2[...], l3[...])
@@ -174,17 +194,18 @@
             heads.append((sets[m, 0:tok, :], sets[m, at : at + tok, :], delta, lse[NC * lax.rem(x - m + NX, NX) + head]))
         dq_turned[...] = jnp.zeros_like(dq_turned)
 
-        def step(masked, tile, carry):
-            at = pl.ds(pl.multiple_of(tile * TILE, TILE), TILE)
+        def step(masked, size, first, carry):
+            at = pl.ds(first, size)
             key, value = key_all[at, :], value_all[at, :]
-            visible = visible_of(tile, tok, low, high) if masked else None
+            visible = visible_of(first, size, tok, low, high) if masked else None
             new_dk, new_dv = dk[at, :], dv[at, :]
+            scores = [dot(key, head[0], 1, 1) for head in heads]
+            dprobs = [dot(value, head[1], 1, 1) for head in heads]
             for half, (query, grad, delta, norm) in enumerate(heads):
-                prob = jnp.exp2(dot(key, query, 1, 1) * factor - norm)
+                prob = jnp.exp2(scores[half] * factor - norm)
                 if masked:
                     prob = jnp.where(visible, prob, 0.0)
-                dprob = dot(value, grad, 1, 1)
-                dscore = (prob * (dprob - delta)).astype(BF16)
+                dscore = (prob * (dprobs[half] - delta)).astype(BF16)
                 new_dv = new_dv + dot(prob.astype(BF16), grad, 1, 0)
                 new_dk = new_dk + dot(dscore, query, 1, 0)
                 dq_turned[half] += dot(key, dscore, 0, 0)
@@ -192,9 +213,9 @@
             dv[at, :] = new_dv
             return carry
 
-        tile_loops(bounds, m, step, 0)
-        dq_own[m] = jnp.transpose(dq_turned[0]) * scale
-        dq_peer[m] = jnp.transpose(dq_turned[1]) * scale
+        tile_loops(bounds, m, share, step, 0)
+        dq_own[m] = dq_turned[0] * scale
+        dq_peer[m] = (dq_turned[1] * scale).astype(BF16)
         return carry
 
     lax.fori_loop(0, NY, group, 0)
@@ -216,7 +237,7 @@
 
 def query_kernel(own, there, *outs):
     for k, out in enumerate(outs):
-        out[...] = (own[k] + there[k]).astype(BF16)
+        out[...] = (own[k] + there[k].astype(F32)).astype(BF16)
 
 
 def stack_kernel(*refs):
@@ -229,6 +250,10 @@
     for ref in refs[1:-1]:
         total = total + ref[...].astype(F32)
     refs[-1][...] = total.astype(BF16)
+
+
+def turn_kernel(part, out):
+    out[...] = jnp.transpose(part[...].astype(F32)).astype(BF16)
 
 
 def relay_kernel(up, down, got_dk, got_dv, new_up, new_down):
@@ -271,8 +296,6 @@
     nz = lax.axis_size("z")
     scale = 1.0 / math.sqrt(width)
     factor = scale * LOG2E
-    x, y, z, c = (lax.axis_index(name) for name in ("x", "y", "z", "c"))
-    place = jnp.stack([x * NC + c, x, y, z, c]).astype(jnp.int32)
     share = tok // (NX * NC)
     shape = jax.ShapeDtypeStruct
     swap = ring(NC, 1)
@@ -284,11 +307,11 @@
     sent, pieces = call(
         prep_kernel,
         (shape((2 * (tok + EXTRA), width), BF16), shape((nz, 2 * share + EXTRA, width), BF16)),
-        [SMEM] + [VMEM] * 6,
+        [VMEM] * 6,
         [VMEM] * 2,
         moved=2 * 2**20,
         limit=60,
-    )(place, queries[0], dout[0], outputs[0], keys, values, docs.reshape(1, tok))
+    )(queries[0], dout[0], outputs[0], keys, values, docs.reshape(1, tok))
 
     skewed = lax.ppermute(sent, ("y", "x"), shift(0))
     along = lax.all_to_all(pieces, "z", 0, 0, tiled=True)
@@ -304,13 +327,13 @@
     )
     peer = lax.ppermute(own, "c", swap)
 
-    total = share * nz * NY
+    total = share * nz * NY + TILE // 2
     high, ends = call(
         functools.partial(high_kernel, share, nz),
         (shape((NY, 1, tok), F32), shape((NY, 2), jnp.int32)),
-        [SMEM],
+        [],
         [VMEM, SMEM],
-    )(place)
+    )()
     lse_part, key_all, low, bounds = call(
         functools.partial(stats_kernel, factor),
         (
@@ -319,22 +342,22 @@
             shape((NY, 1, tok), F32),
             shape((NY, 4), jnp.int32),
         ),
-        [SMEM] * 2 + [VMEM] * 7,
+        [SMEM] + [VMEM] * 7,
         [VMEM] * 3 + [SMEM],
         flops=2 * 10**9,
         moved=4 * 2**20,
-    )(place, ends, own, peer, high, along, before, far_keys, after)
+    )(ends, own, peer, high, along, before, far_keys, after)
 
     lse_chip = join(lse_part, lax.ppermute(lse_part, "c", swap))
     lse_all = [lse_chip] + [lax.ppermute(lse_chip, "x", ring(NX, k)) for k in (1, 3, 2)]
 
-    dq_shape = shape((NY, tok, width), F32)
+    dq_shape, peer_shape = (shape((NX, width, tok), kind) for kind in (F32, BF16))
     slab_shape = shape((nz, 2, share, width), BF16)
     far_shape = shape((nz, share, width), BF16)
     dq_own, dq_peer, here, up, down, far_dk, far_dv = call(
         functools.partial(grad_kernel, factor, scale),
-        (dq_shape, dq_shape, slab_shape, slab_shape, slab_shape, far_shape, far_shape),
-        [SMEM] * 2 + [VMEM] * 13,
+        (dq_shape, peer_shape, slab_shape, slab_shape, slab_shape, far_shape, far_shape),
+        [SMEM] + [VMEM] * 13,
         [VMEM] * 7,
         scratch=(
             pltpu.VMEM((total, width), BF16),
@@ -345,25 +368,27 @@
         ),
         flops=8 * 10**9,
         moved=8 * 2**20,
-    )(place, bounds, own, peer, high, along, before, far_values, after, key_all, low, *lse_all)
-
-    one = shape((tok, width), BF16)
+    )(bounds, own, peer, high, along, before, far_values, after, key_all, low, *lse_all)
+
+    one = shape((width, tok), BF16)
     kept, *away = call(query_kernel, (one,) * NX, [VMEM] * 2, [VMEM] * NX, moved=3 * 2**20)(
         dq_own, lax.ppermute(dq_peer, "c", swap)
     )
     got_dk = lax.ppermute(far_dk, "y", ring(NY, 1))
     got_dv = lax.ppermute(far_dv, "y", ring(NY, -1))
+    got_dk, got_dv, kept = lax.optimization_barrier((got_dk, got_dv, kept))
     up, down = call(relay_kernel, (slab_shape,) * 2, [VMEM] * 4, [VMEM] * 2, moved=5 * 2**18)(up, down, got_dk, got_dv)
     arrived = [here, lax.ppermute(up, "y", ring(NY, 1)), lax.ppermute(down, "y", ring(NY, -1))]
     away = [lax.ppermute(away[k - 1], "x", ring(NX, -k)) for k in (1, 2, 3)]
     arrived, away = lax.optimization_barrier((arrived, away))
     slab_sum = call(add_kernel, slab_shape, [VMEM] * 3, VMEM, moved=5 * 2**18)(*arrived)
     blocks = lax.all_to_all(slab_sum, "z", 0, 0, tiled=True)
+    dq = call(add_kernel, one, [VMEM] * 4, VMEM, moved=2**19)(kept, *away)
+    dq = lax.ppermute(dq, ("y", "x"), shift(0, True))
+    dq = call(turn_kernel, shape((tok, width), BF16), [VMEM], VMEM, moved=2**18)(dq)
+    blocks, dq = lax.optimization_barrier((blocks, dq))
     half = shape((share, width), BF16)
     dk, dv = call(last_kernel, (half, half), [VMEM], [VMEM] * 2, moved=2**18)(blocks)
-
-    dq = call(add_kernel, one, [VMEM] * 4, VMEM, moved=2**19)(kept, *away)
-    dq = lax.ppermute(dq, ("y", "x"), shift(0, True))
     return dq[None], dk, dv
 
 

time: 109 us -> 105 us (0.963)
  Pallas kernels: 23.1 us -> 15.9 us
  starting transfers between devices: 38.5 us -> 44.2 us
  local copies, waits for them, and re-layouts: 1.35 us -> 0.02 us
    all_to_all x1, starting transfers between devices: 4.69 us -> 9.14 us  [local(): blocks = lax.all_to_all(slab_sum, 'z', 0, 0, tiled=True)]
    pallas_call x1 -> x2, Pallas kernels: 11 us -> 7.03 us  [the longest x1 6.27 us: local(): call(functools.partial(grad_kernel, factor, scale), (dq_shape, peer_shape...]
    ppermute x1, waiting for transfers between devices: 3.62 us -> 0.01 us  [local(): lax.ppermute(up, 'y', ring(NY, 1))]
    ppermute x3, waiting for transfers between devices: 3.73 us -> 7.01 us  [local(): away = [lax.ppermute(away[k - 1], 'x', ring(NX, -k)) for k in (1, 2, 3)]]
    pallas_call x1, Pallas kernels: 7.15 us -> 4.4 us  [local(): call(functools.partial(stats_kernel, factor), (shape((NC * NY, 1, tok), F...]
  transfers between devices with their start and end apart: 24 -> 24, of which waited for: 16 -> 15; matrix products, arithmetic and copies ran while one was open for 0% -> 0% of each run, Pallas kernels for 1% -> 2%
where the time goes in v2:
time: 105 us
  starting transfers between devices  44.2 us (42%)
  waiting for transfers between devices  43.7 us (42%)
  Pallas kernels  15.9 us (15%)
    all_to_all x1, waiting for transfers between devices, local(): along = lax.all_to_all(pieces, 'z', 0, 0, tiled=True)  9.52 us
    all_to_all x1, starting transfers between devices, local(): blocks = lax.all_to_all(slab_sum, 'z', 0, 0, tiled=True)  9.14 us
    all_to_all x1, starting transfers between devices, local(): along = lax.all_to_all(pieces, 'z', 0, 0, tiled=True)  8.57 us
    all_to_all x1, waiting for transfers between devices, local(): blocks = lax.all_to_all(slab_sum, 'z', 0, 0, tiled=True)  8.07 us
    ppermute x3, waiting for transfers between devices, local(): lax.ppermute(skewed, 'x', ring(NX, k))  7.82 us
    ppermute x3, waiting for transfers between devices, local(): away = [lax.ppermute(away[k - 1], 'x', ring(NX, -k)) for k in (1, 2, 3)]  7.01 us
    pallas_call x1, Pallas kernels, local(): call(functools.partial(grad_kernel, factor, scale), (dq_shape, peer_shape...  6.27 us
    ppermute x3, starting transfers between devices, local(): lax.ppermute(skewed, 'x', ring(NX, k))  4.58 us
  transfers between devices with their start and end apart: 24, of which 15 were waited for; matrix products, arithmetic and copies ran while one was open for 0% of the time, Pallas kernels for 2%

profile of v2, /device:TPU:32, one launch (start us, length us, event | category | flops | bytes accessed | tf_op | source)
XLA Modules:
  0.0 104.6 jit_solution(4664322940654235930)
XLA Ops:
  0.6 2.1 %shard_map.86 = (bf16[1056,128]{1,0:T(8,128)(2,1)}, bf16[8,144,128]{2,1,0:T(8,128)(2,1)}) custom-call(bf16[512,128]{1,0:T(8,128)(2,1)} %bitcast.5, bf16[512,128]{1,0:T(8,128)(2,1)} %bitcast.6, bf16[512,128]{1,0:T(8,128)(2,1)} %bitcast.7, bf16[512,128]{1,0:T(8,128)(2,1)} %keys.1, bf16[512,128]{1,0:T(8,128)(2,1)} %values.1, s32[1,512]{1,0:T(1,128)} %bitcast.9), custom_call_target="tpu_custom_call" | custom-call | bytes 2097152 | tf_op jit(solution)/shard_map/pallas_call | solution.py:307
  2.7 8.6 %all-to-all-start = ((bf16[8,144,128]{2,1,0:T(8,128)(2,1)}), bf16[8,144,128]{2,1,0:T(8,128)(2,1)S(1)}, u32[]{:S(2)}, u32[]{:S(2)}) async-start(bf16[8,144,128]{2,1,0:T(8,128)(2,1)} %get-tuple-element.46), calls=%async_computation | async-start | bytes 589824 | tf_op jit(solution)/shard_map/all_to_all | solution.py:317
  11.3 1.6 %collective-permute-start = (bf16[1056,128]{1,0:T(8,128)(2,1)}, bf16[1056,128]{1,0:T(8,128)(2,1)S(1)}, u32[]{:S(2)}, u32[]{:S(2)}) collective-permute-start(bf16[1056,128]{1,0:T(8,128)(2,1)} %get-tuple-element.47), channel_id=1, source_target_pairs={{0,0},{2,194},{4,132},{6,70},{64,64},{66,2},{68,196},{70,134},{128... | collective-permute-start | bytes 811016 | tf_op jit(solution)/shard_map/ppermute | solution.py:316
  12.9 9.5 %all-to-all-done.p0 = bf16[8,144,128]{2,1,0:T(8,128)(2,1)S(1)} async-done(((bf16[8,144,128]{2,1,0:T(8,128)(2,1)}), bf16[8,144,128]{2,1,0:T(8,128)(2,1)S(1)}, u32[]{:S(2)}, u32[]{:S(2)}) %all-to-all-start) | async-done | bytes 294944 | tf_op jit(solution)/shard_map/all_to_all | solution.py:317
  22.4 1.6 %collective-permute-start.4 = (bf16[8,144,128]{2,1,0:T(8,128)(2,1)S(1)}, bf16[8,144,128]{2,1,0:T(8,128)(2,1)S(1)}, u32[]{:S(2)}, u32[]{:S(2)}) collective-permute-start(bf16[8,144,128]{2,1,0:T(8,128)(2,1)S(1)} %all-to-all-done.p0), channel_id=1, source_target_pairs={{0,64},{64,128},{128,192},{192,0},{1,65},{65,129},{129,193},{193,1... | collective-permute-start | bytes 884744 | tf_op jit(solution)/shard_map/ppermute | solution.py:320
  24.0 1.7 %collective-permute-start.6 = (bf16[8,144,128]{2,1,0:T(8,128)(2,1)S(1)}, bf16[8,144,128]{2,1,0:T(8,128)(2,1)S(1)}, u32[]{:S(2)}, u32[]{:S(2)}) collective-permute-start(bf16[8,144,128]{2,1,0:T(8,128)(2,1)S(1)} %all-to-all-done.p0), channel_id=1, source_target_pairs={{0,192},{64,0},{128,64},{192,128},{1,193},{65,1},{129,65},{193,129... | collective-permute-start | bytes 884744 | tf_op jit(solution)/shard_map/ppermute | solution.py:321
  25.6 2.8 %collective-permute-start.3 = (bf16[1056,128]{1,0:T(8,128)(2,1)S(1)}, bf16[1056,128]{1,0:T(8,128)(2,1)S(1)}, u32[]{:S(2)}, u32[]{:S(2)}) collective-permute-start(bf16[1056,128]{1,0:T(8,128)(2,1)S(1)} %collective-permute-done.refs_0_), channel_id=1, source_target_pairs={{0,6},{2,0},{4,2},{6,4},{1,7},{3,1},{5,3},{7,5},{8,14},{10,8},{12,... | collective-permute-start | bytes 811016 | tf_op jit(solution)/shard_map/ppermute | solution.py:319
  31.3 2.5 %collective-permute-start.7 = (bf16[8,64,128]{2,1,0:T(8,128)(2,1)S(1)}, bf16[8,64,128]{2,1,0:T(8,128)(2,1)S(1)}, u32[]{:S(2)}, u32[]{:S(2)}) collective-permute-start(bf16[8,64,128]{2,1,0:T(8,128)(2,1)S(1)} %slice.9), channel_id=1, source_target_pairs={{0,192},{64,0},{128,64},{192,128},{1,193},{65,1},{129,65},{193,129... | collective-permute-start | bytes 393224 | tf_op jit(solution)/shard_map/ppermute | solution.py:323
  33.7 4.1 %collective-permute-done.3.refs_3_ = bf16[1056,128]{1,0:T(8,128)(2,1)S(1)} collective-permute-done((bf16[1056,128]{1,0:T(8,128)(2,1)S(1)}, bf16[1056,128]{1,0:T(8,128)(2,1)S(1)}, u32[]{:S(2)}, u32[]{:S(2)}) %collective-permute-start.3) | collective-permute-done | bytes 270368 | tf_op jit(solution)/shard_map/ppermute | solution.py:319
  38.8 2.8 %collective-permute-done.1.refs_1_ = bf16[1056,128]{1,0:T(8,128)(2,1)S(1)} collective-permute-done((bf16[1056,128]{1,0:T(8,128)(2,1)S(1)}, bf16[1056,128]{1,0:T(8,128)(2,1)S(1)}, u32[]{:S(2)}, u32[]{:S(2)}) %collective-permute-start.1) | collective-permute-done | bytes 270368 | tf_op jit(solution)/shard_map/ppermute | solution.py:319
  42.4 2.0 %collective-permute-done.8.peer = bf16[4,1056,128]{2,1,0:T(8,128)(2,1)S(1)} collective-permute-done((bf16[4,1056,128]{2,1,0:T(8,128)(2,1)S(1)}, bf16[4,1056,128]{2,1,0:T(8,128)(2,1)S(1)}, u32[]{:S(2)}, u32[]{:S(2)}) %collective-permute-start.8) | collective-permute-done | bytes 1081376 | tf_op jit(solution)/shard_map/ppermute | solution.py:328
  44.4 4.4 %shard_map.88 = (f32[8,1,512]{2,1,0:T(1,128)S(1)}, bf16[2176,128]{1,0:T(8,128)(2,1)S(1)}, f32[4,1,512]{2,1,0:T(1,128)S(1)}, s32[4,4]{1,0:T(4,128)S(1)}) custom-call(s32[4,2]{1,0:T(4,128)S(1)} %get-tuple-element.45.ends, bf16[4,1056,128]{2,1,0:T(8,128)(2,1)S(1)} %shard_map.87.own, bf16[4,1056,128]{2,1,0:T(8,128)(2,1)S(1)} %collective-permute-done.8.peer, ...), custom_call_target="tpu_custom_call" | custom-call | flops 2000000000 | bytes 4194304 | tf_op jit(solution)/shard_map/pallas_call | solution.py:337
  51.5 1.4 %collective-permute-start.11 = (f32[8,1,512]{2,1,0:T(1,128)S(1)}, f32[8,1,512]{2,1,0:T(1,128)S(1)}, u32[]{:S(2)}, u32[]{:S(2)}) collective-permute-start(f32[8,1,512]{2,1,0:T(1,128)S(1)} %multiply_add_fusion.l0), channel_id=1, source_target_pairs={{0,6},{2,0},{4,2},{6,4},{1,7},{3,1},{5,3},{7,5},{8,14},{10,8},{12,... | collective-permute-start | bytes 49160 | tf_op jit(solution)/shard_map/ppermute | solution.py:352
  53.5 2.0 %collective-permute-done.12.l3 = f32[8,1,512]{2,1,0:T(1,128)S(1)} collective-permute-done((f32[8,1,512]{2,1,0:T(1,128)S(1)}, f32[8,1,512]{2,1,0:T(1,128)S(1)}, u32[]{:S(2)}, u32[]{:S(2)}) %collective-permute-start.12) | collective-permute-done | bytes 16416 | tf_op jit(solution)/shard_map/ppermute | solution.py:352
  55.5 2.3 %collective-permute-done.10.l1 = f32[8,1,512]{2,1,0:T(1,128)S(1)} collective-permute-done((f32[8,1,512]{2,1,0:T(1,128)S(1)}, f32[8,1,512]{2,1,0:T(1,128)S(1)}, u32[]{:S(2)}, u32[]{:S(2)}) %collective-permute-start.10) | collective-permute-done | bytes 16416 | tf_op jit(solution)/shard_map/ppermute | solution.py:352
  57.8 6.3 %shard_map.89 = (f32[4,128,512]{2,1,0:T(8,128)S(1)}, bf16[4,128,512]{2,1,0:T(8,128)(2,1)S(1)}, bf16[8,2,64,128]{3,2,1,0:T(8,128)(2,1)S(1)}, bf16[8,2,64,128]{3,2...) custom-call(s32[4,4]{1,0:T(4,128)S(1)} %get-tuple-element.56.bounds,, ...), custom_call_target="tpu_custom_call" | custom-call | flops 8000000000 | bytes 8388608 | tf_op jit(solution)/shard_map/pallas_call | solution.py:357
  64.6 2.9 %collective-permute-start.14 = (bf16[8,64,128]{2,1,0:T(8,128)(2,1)S(1)}, bf16[8,64,128]{2,1,0:T(8,128)(2,1)S(1)}, u32[]{:S(2)}, u32[]{:S(2)}) collective-permute-start(bf16[8,64,128]{2,1,0:T(8,128)(2,1)S(1)} %get-tuple-element.65), channel_id=1, source_target_pairs={{0,192},{64,0},{128,64},{192,128},{1,193},{65,1},{129,65},{193,129... | collective-permute-start | bytes 393224 | tf_op jit(solution)/shard_map/ppermute | solution.py:378
  67.7 3.7 %collective-permute-done.13.got_dk = bf16[8,64,128]{2,1,0:T(8,128)(2,1)S(1)} collective-permute-done((bf16[8,64,128]{2,1,0:T(8,128)(2,1)S(1)}, bf16[8,64,128]{2,1,0:T(8,128)(2,1)S(1)}, u32[]{:S(2)}, u32[]{:S(2)}) %collective-permute-start.13) | collective-permute-done | bytes 131104 | tf_op jit(solution)/shard_map/ppermute | solution.py:377
  71.9 2.8 %collective-permute-start.17 = (bf16[8,2,64,128]{3,2,1,0:T(8,128)(2,1)S(1)}, bf16[8,2,64,128]{3,2,1,0:T(8,128)(2,1)S(1)}, u32[]{:S(2)}, u32[]{:S(2)}) collective-permute-start(bf16[8,2,64,128]{3,2,1,0:T(8,128)(2,1)S(1)} %get-tuple-element.72), channel_id=1, source_target_pairs={{0,192},{64,0},{128,64},{192,128},{1,193},{65,1},{129,65},{193,129... | collective-permute-start | bytes 786440 | tf_op jit(solution)/shard_map/ppermute | solution.py:381
  75.9 1.5 %collective-permute-start.19 = (bf16[128,512]{1,0:T(8,128)(2,1)S(1)}, bf16[128,512]{1,0:T(8,128)(2,1)S(1)}, u32[]{:S(2)}, u32[]{:S(2)}) collective-permute-start(bf16[128,512]{1,0:T(8,128)(2,1)S(1)} %get-tuple-element.74), channel_id=1, source_target_pairs={{0,4},{2,6},{4,0},{6,2},{1,5},{3,7},{5,1},{7,3},{8,12},{10,14},{12... | collective-permute-start | bytes 393224 | tf_op jit(solution)/shard_map/ppermute | solution.py:382
  77.4 3.2 %collective-permute-done.18.refs_1_ = bf16[128,512]{1,0:T(8,128)(2,1)S(1)} collective-permute-done((bf16[128,512]{1,0:T(8,128)(2,1)S(1)}, bf16[128,512]{1,0:T(8,128)(2,1)S(1)}, u32[]{:S(2)}, u32[]{:S(2)}) %collective-permute-start.18) | collective-permute-done | bytes 131104 | tf_op jit(solution)/shard_map/ppermute | solution.py:382
  80.6 2.5 %collective-permute-done.19.refs_2_ = bf16[128,512]{1,0:T(8,128)(2,1)S(1)} collective-permute-done((bf16[128,512]{1,0:T(8,128)(2,1)S(1)}, bf16[128,512]{1,0:T(8,128)(2,1)S(1)}, u32[]{:S(2)}, u32[]{:S(2)}) %collective-permute-start.19) | collective-permute-done | bytes 131104 | tf_op jit(solution)/shard_map/ppermute | solution.py:382
  85.2 9.1 %all-to-all-start.1 = ((bf16[8,2,64,128]{3,2,1,0:T(8,128)(2,1)}), bf16[8,2,64,128]{3,2,1,0:T(8,128)(2,1)S(1)}, u32[]{:S(2)}, u32[]{:S(2)}) async-start(bf16[8,2,64,128]{3,2,1,0:T(8,128)(2,1)} %shard_map.92), calls=%async_computation.1 | async-start | bytes 524288 | tf_op jit(solution)/shard_map/all_to_all | solution.py:385
  95.9 8.1 %all-to-all-done.1.blocks = bf16[8,2,64,128]{3,2,1,0:T(8,128)(2,1)S(1)} async-done(((bf16[8,2,64,128]{3,2,1,0:T(8,128)(2,1)}), bf16[8,2,64,128]{3,2,1,0:T(8,128)(2,1)S(1)}, u32[]{:S(2)}, u32[]{:S(2)}) %all-to-all-start.1) | async-done | bytes 262176 | tf_op jit(solution)/shard_map/all_to_all | solution.py:385
  (38 shorter events, 14.6 us)
Async XLA Ops:
  2.7 19.7 %all-to-all-start = ((bf16[8,144,128]{2,1,0:T(8,128)(2,1)}), bf16[8,144,128]{2,1,0:T(8,128)(2,1)S(1)}, u32[]{:S(2)}, u32[]{:S(2)}) async-start(bf16[8,144,128]{2,1,0:T(8,128)(2,1)} %get-tuple-element.46), calls=%async_computation | async-start | bytes 589824 | tf_op jit(solution)/shard_map/all_to_all | solution.py:317
  11.3 1.6 %collective-permute-start = (bf16[1056,128]{1,0:T(8,128)(2,1)}, bf16[1056,128]{1,0:T(8,128)(2,1)S(1)}, u32[]{:S(2)}, u32[]{:S(2)}) collective-permute-start(bf16[1056,128]{1,0:T(8,128)(2,1)} %get-tuple-element.47), channel_id=1, source_target_pairs={{0,0},{2,194},{4,132},{6,70},{64,64},{66,2},{68,196},{70,134},{128... | collective-permute-start | bytes 811016 | tf_op jit(solution)/shard_map/ppermute | solution.py:316
  22.4 7.9 %collective-permute-start.4 = (bf16[8,144,128]{2,1,0:T(8,128)(2,1)S(1)}, bf16[8,144,128]{2,1,0:T(8,128)(2,1)S(1)}, u32[]{:S(2)}, u32[]{:S(2)}) collective-permute-start(bf16[8,144,128]{2,1,0:T(8,128)(2,1)S(1)} %all-to-all-done.p0), channel_id=1, source_target_pairs={{0,64},{64,128},{128,192},{192,0},{1,65},{65,129},{129,193},{193,1... | collective-permute-start | bytes 884744 | tf_op jit(solution)/shard_map/ppermute | solution.py:320
  24.0 7.3 %collective-permute-start.6 = (bf16[8,144,128]{2,1,0:T(8,128)(2,1)S(1)}, bf16[8,144,128]{2,1,0:T(8,128)(2,1)S(1)}, u32[]{:S(2)}, u32[]{:S(2)}) collective-permute-start(bf16[8,144,128]{2,1,0:T(8,128)(2,1)S(1)} %all-to-all-done.p0), channel_id=1, source_target_pairs={{0,192},{64,0},{128,64},{192,128},{1,193},{65,1},{129,65},{193,129... | collective-permute-start | bytes 884744 | tf_op jit(solution)/shard_map/ppermute | solution.py:321
  25.6 12.2 %collective-permute-start.3 = (bf16[1056,128]{1,0:T(8,128)(2,1)S(1)}, bf16[1056,128]{1,0:T(8,128)(2,1)S(1)}, u32[]{:S(2)}, u32[]{:S(2)}) collective-permute-start(bf16[1056,128]{1,0:T(8,128)(2,1)S(1)} %collective-permute-done.refs_0_), channel_id=1, source_target_pairs={{0,6},{2,0},{4,2},{6,4},{1,7},{3,1},{5,3},{7,5},{8,14},{10,8},{12,... | collective-permute-start | bytes 811016 | tf_op jit(solution)/shard_map/ppermute | solution.py:319
  28.4 10.4 %collective-permute-start.2 = (bf16[1056,128]{1,0:T(8,128)(2,1)S(1)}, bf16[1056,128]{1,0:T(8,128)(2,1)S(1)}, u32[]{:S(2)}, u32[]{:S(2)}) collective-permute-start(bf16[1056,128]{1,0:T(8,128)(2,1)S(1)} %collective-permute-done.refs_0_), channel_id=1, source_target_pairs={{0,4},{2,6},{4,0},{6,2},{1,5},{3,7},{5,1},{7,3},{8,12},{10,14},{12... | collective-permute-start | bytes 811016 | tf_op jit(solution)/shard_map/ppermute | solution.py:319
  29.2 12.4 %collective-permute-start.1 = (bf16[1056,128]{1,0:T(8,128)(2,1)S(1)}, bf16[1056,128]{1,0:T(8,128)(2,1)S(1)}, u32[]{:S(2)}, u32[]{:S(2)}) collective-permute-start(bf16[1056,128]{1,0:T(8,128)(2,1)S(1)} %collective-permute-done.refs_0_), channel_id=1, source_target_pairs={{0,2},{2,4},{4,6},{6,0},{1,3},{3,5},{5,7},{7,1},{8,10},{10,12},{12... | collective-permute-start | bytes 811016 | tf_op jit(solution)/shard_map/ppermute | solution.py:319
  30.3 11.2 %collective-permute-start.5 = (bf16[8,80,128]{2,1,0:T(8,128)(2,1)S(1)}, bf16[8,80,128]{2,1,0:T(8,128)(2,1)S(1)}, u32[]{:S(2)}, u32[]{:S(2)}) collective-permute-start(bf16[8,80,128]{2,1,0:T(8,128)(2,1)S(1)} %slice.8), channel_id=1, source_target_pairs={{0,64},{64,128},{128,192},{192,0},{1,65},{65,129},{129,193},{193,1... | collective-permute-start | bytes 491528 | tf_op jit(solution)/shard_map/ppermute | solution.py:322
  31.3 10.3 %collective-permute-start.7 = (bf16[8,64,128]{2,1,0:T(8,128)(2,1)S(1)}, bf16[8,64,128]{2,1,0:T(8,128)(2,1)S(1)}, u32[]{:S(2)}, u32[]{:S(2)}) collective-permute-start(bf16[8,64,128]{2,1,0:T(8,128)(2,1)S(1)} %slice.9), channel_id=1, source_target_pairs={{0,192},{64,0},{128,64},{192,128},{1,193},{65,1},{129,65},{193,129... | collective-permute-start | bytes 393224 | tf_op jit(solution)/shard_map/ppermute | solution.py:323
  41.6 2.8 %collective-permute-start.8 = (bf16[4,1056,128]{2,1,0:T(8,128)(2,1)S(1)}, bf16[4,1056,128]{2,1,0:T(8,128)(2,1)S(1)}, u32[]{:S(2)}, u32[]{:S(2)}) collective-permute-start(bf16[4,1056,128]{2,1,0:T(8,128)(2,1)S(1)} %shard_map.87.own), channel_id=1, source_target_pairs={{0,1},{1,0},{2,3},{3,2},{4,5},{5,4},{6,7},{7,6},{8,9},{9,8},{10,11... | collective-permute-start | bytes 3244040 | tf_op jit(solution)/shard_map/ppermute | solution.py:328
  48.9 1.3 %collective-permute-start.9 = (f32[8,1,512]{2,1,0:T(1,128)S(1)}, f32[8,1,512]{2,1,0:T(1,128)S(1)}, u32[]{:S(2)}, u32[]{:S(2)}) collective-permute-start(f32[8,1,512]{2,1,0:T(1,128)S(1)} %get-tuple-element.60), channel_id=1, source_target_pairs={{0,1},{1,0},{2,3},{3,2},{4,5},{5,4},{6,7},{7,6},{8,9},{9,8},{10,11... | collective-permute-start | bytes 49160 | tf_op jit(solution)/shard_map/ppermute | solution.py:351
  50.2 5.3 %collective-permute-start.12 = (f32[8,1,512]{2,1,0:T(1,128)S(1)}, f32[8,1,512]{2,1,0:T(1,128)S(1)}, u32[]{:S(2)}, u32[]{:S(2)}) collective-permute-start(f32[8,1,512]{2,1,0:T(1,128)S(1)} %multiply_add_fusion.l0), channel_id=1, source_target_pairs={{0,4},{2,6},{4,0},{6,2},{1,5},{3,7},{5,1},{7,3},{8,12},{10,14},{12... | collective-permute-start | bytes 49160 | tf_op jit(solution)/shard_map/ppermute | solution.py:352
  51.5 4.0 %collective-permute-start.11 = (f32[8,1,512]{2,1,0:T(1,128)S(1)}, f32[8,1,512]{2,1,0:T(1,128)S(1)}, u32[]{:S(2)}, u32[]{:S(2)}) collective-permute-start(f32[8,1,512]{2,1,0:T(1,128)S(1)} %multiply_add_fusion.l0), channel_id=1, source_target_pairs={{0,6},{2,0},{4,2},{6,4},{1,7},{3,1},{5,3},{7,5},{8,14},{10,8},{12,... | collective-permute-start | bytes 49160 | tf_op jit(solution)/shard_map/ppermute | solution.py:352
  52.9 5.0 %collective-permute-start.10 = (f32[8,1,512]{2,1,0:T(1,128)S(1)}, f32[8,1,512]{2,1,0:T(1,128)S(1)}, u32[]{:S(2)}, u32[]{:S(2)}) collective-permute-start(f32[8,1,512]{2,1,0:T(1,128)S(1)} %multiply_add_fusion.l0), channel_id=1, source_target_pairs={{0,2},{2,4},{4,6},{6,0},{1,3},{3,5},{5,7},{7,1},{8,10},{10,12},{12... | collective-permute-start | bytes 49160 | tf_op jit(solution)/shard_map/ppermute | solution.py:352
  64.1 3.4 %collective-permute-start.15 = (bf16[4,128,512]{2,1,0:T(8,128)(2,1)S(1)}, bf16[4,128,512]{2,1,0:T(8,128)(2,1)S(1)}, u32[]{:S(2)}, u32[]{:S(2)}) collective-permute-start(bf16[4,128,512]{2,1,0:T(8,128)(2,1)S(1)} %get-tuple-element.67), channel_id=1, source_target_pairs={{0,1},{1,0},{2,3},{3,2},{4,5},{5,4},{6,7},{7,6},{8,9},{9,8},{10,11... | collective-permute-start | bytes 1572872 | tf_op jit(solution)/shard_map/ppermute | solution.py:375
  64.2 7.1 %collective-permute-start.13 = (bf16[8,64,128]{2,1,0:T(8,128)(2,1)S(1)}, bf16[8,64,128]{2,1,0:T(8,128)(2,1)S(1)}, u32[]{:S(2)}, u32[]{:S(2)}) collective-permute-start(bf16[8,64,128]{2,1,0:T(8,128)(2,1)S(1)} %get-tuple-element.64), channel_id=1, source_target_pairs={{0,64},{64,128},{128,192},{192,0},{1,65},{65,129},{129,193},{193,1... | collective-permute-start | bytes 393224 | tf_op jit(solution)/shard_map/ppermute | solution.py:377
  64.6 6.7 %collective-permute-start.14 = (bf16[8,64,128]{2,1,0:T(8,128)(2,1)S(1)}, bf16[8,64,128]{2,1,0:T(8,128)(2,1)S(1)}, u32[]{:S(2)}, u32[]{:S(2)}) collective-permute-start(bf16[8,64,128]{2,1,0:T(8,128)(2,1)S(1)} %get-tuple-element.65), channel_id=1, source_target_pairs={{0,192},{64,0},{128,64},{192,128},{1,193},{65,1},{129,65},{193,129... | collective-permute-start | bytes 393224 | tf_op jit(solution)/shard_map/ppermute | solution.py:378
  71.4 13.0 %collective-permute-start.16 = (bf16[8,2,64,128]{3,2,1,0:T(8,128)(2,1)S(1)}, bf16[8,2,64,128]{3,2,1,0:T(8,128)(2,1)S(1)}, u32[]{:S(2)}, u32[]{:S(2)}) collective-permute-start(bf16[8,2,64,128]{3,2,1,0:T(8,128)(2,1)S(1)} %get-tuple-element.71), channel_id=1, source_target_pairs={{0,64},{64,128},{128,192},{192,0},{1,65},{65,129},{129,193},{193,1... | collective-permute-start | bytes 786440 | tf_op jit(solution)/shard_map/ppermute | solution.py:381
  71.9 12.5 %collective-permute-start.17 = (bf16[8,2,64,128]{3,2,1,0:T(8,128)(2,1)S(1)}, bf16[8,2,64,128]{3,2,1,0:T(8,128)(2,1)S(1)}, u32[]{:S(2)}, u32[]{:S(2)}) collective-permute-start(bf16[8,2,64,128]{3,2,1,0:T(8,128)(2,1)S(1)} %get-tuple-element.72), channel_id=1, source_target_pairs={{0,192},{64,0},{128,64},{192,128},{1,193},{65,1},{129,65},{193,129... | collective-permute-start | bytes 786440 | tf_op jit(solution)/shard_map/ppermute | solution.py:381
  74.7 5.9 %collective-permute-start.18 = (bf16[128,512]{1,0:T(8,128)(2,1)S(1)}, bf16[128,512]{1,0:T(8,128)(2,1)S(1)}, u32[]{:S(2)}, u32[]{:S(2)}) collective-permute-start(bf16[128,512]{1,0:T(8,128)(2,1)S(1)} %get-tuple-element.73), channel_id=1, source_target_pairs={{0,6},{2,0},{4,2},{6,4},{1,7},{3,1},{5,3},{7,5},{8,14},{10,8},{12,... | collective-permute-start | bytes 393224 | tf_op jit(solution)/shard_map/ppermute | solution.py:382
  75.9 7.2 %collective-permute-start.19 = (bf16[128,512]{1,0:T(8,128)(2,1)S(1)}, bf16[128,512]{1,0:T(8,128)(2,1)S(1)}, u32[]{:S(2)}, u32[]{:S(2)}) collective-permute-start(bf16[128,512]{1,0:T(8,128)(2,1)S(1)} %get-tuple-element.74), channel_id=1, source_target_pairs={{0,4},{2,6},{4,0},{6,2},{1,5},{3,7},{5,1},{7,3},{8,12},{10,14},{12... | collective-permute-start | bytes 393224 | tf_op jit(solution)/shard_map/ppermute | solution.py:382
  77.4 7.0 %collective-permute-start.20 = (bf16[128,512]{1,0:T(8,128)(2,1)S(1)}, bf16[128,512]{1,0:T(8,128)(2,1)S(1)}, u32[]{:S(2)}, u32[]{:S(2)}) collective-permute-start(bf16[128,512]{1,0:T(8,128)(2,1)S(1)} %get-tuple-element.75), channel_id=1, source_target_pairs={{0,2},{2,4},{4,6},{6,0},{1,3},{3,5},{5,7},{7,1},{8,10},{10,12},{12... | collective-permute-start | bytes 393224 | tf_op jit(solution)/shard_map/ppermute | solution.py:382
  85.2 18.7 %all-to-all-start.1 = ((bf16[8,2,64,128]{3,2,1,0:T(8,128)(2,1)}), bf16[8,2,64,128]{3,2,1,0:T(8,128)(2,1)S(1)}, u32[]{:S(2)}, u32[]{:S(2)}) async-start(bf16[8,2,64,128]{3,2,1,0:T(8,128)(2,1)} %shard_map.92), calls=%async_computation.1 | async-start | bytes 524288 | tf_op jit(solution)/shard_map/all_to_all | solution.py:385
  94.4 0.7 collective-permute-start.21

commit v3 on v2

--- a/solution.py
+++ b/solution.py
@@ -315,7 +315,6 @@
 
     skewed = lax.ppermute(sent, ("y", "x"), shift(0))
     along = lax.all_to_all(pieces, "z", 0, 0, tiled=True)
-    along, skewed = lax.optimization_barrier((along, skewed))
     moved = [skewed] + [lax.ppermute(skewed, "x", ring(NX, k)) for k in (1, 2, 3)]
     before = lax.ppermute(along, "y", ring(NY, 1))
     after = lax.ppermute(along, "y", ring(NY, -1))
@@ -376,10 +375,10 @@
     )
     got_dk = lax.ppermute(far_dk, "y", ring(NY, 1))
     got_dv = lax.ppermute(far_dv, "y", ring(NY, -1))
-    got_dk, got_dv, kept = lax.optimization_barrier((got_dk, got_dv, kept))
+    away = [lax.ppermute(away[k - 1], "x", ring(NX, -k)) for k in (1, 2, 3)]
+    got_dk, got_dv, away[0] = lax.optimization_barrier((got_dk, got_dv, away[0]))
     up, down = call(relay_kernel, (slab_shape,) * 2, [VMEM] * 4, [VMEM] * 2, moved=5 * 2**18)(up, down, got_dk, got_dv)
     arrived = [here, lax.ppermute(up, "y", ring(NY, 1)), lax.ppermute(down, "y", ring(NY, -1))]
-    away = [lax.ppermute(away[k - 1], "x", ring(NX, -k)) for k in (1, 2, 3)]
     arrived, away = lax.optimization_barrier((arrived, away))
     slab_sum = call(add_kernel, slab_shape, [VMEM] * 3, VMEM, moved=5 * 2**18)(*arrived)
     blocks = lax.all_to_all(slab_sum, "z", 0, 0, tiled=True)

time: 105 us -> 104 us (level)
  waiting for transfers between devices: 43.7 us -> 39.6 us
  starting transfers between devices: 44.2 us -> 46.3 us
  Pallas kernels: 15.9 us -> 17.3 us
    ppermute x3, starting transfers between devices: 2.68 us -> 5.07 us  [local(): away = [lax.ppermute(away[k - 1], 'x', ring(NX, -k)) for k in (1, 2, 3)]]
    ppermute x1, waiting for transfers between devices: 3.66 us -> 2.12 us  [local(): got_dk = lax.ppermute(far_dk, 'y', ring(NY, 1))]
    ppermute x3, waiting for transfers between devices: 7.82 us -> 6.32 us  [local(): lax.ppermute(skewed, 'x', ring(NX, k))]
  transfers between devices with their start and end apart: 24 -> 24, of which waited for: 15 -> 14; matrix products, arithmetic and copies ran while one was open for 0% -> 0% of each run, Pallas kernels for 2% -> 2%
where the time goes in v3:
time: 104 us
  starting transfers between devices  46.3 us (45%)
  waiting for transfers between devices  39.6 us (38%)
  Pallas kernels  17.3 us (17%)
    all_to_all x1, waiting for transfers between devices, local(): along = lax.all_to_all(pieces, 'z', 0, 0, tiled=True)  9.52 us
    all_to_all x1, starting transfers between devices, local(): blocks = lax.all_to_all(slab_sum, 'z', 0, 0, tiled=True)  8.75 us
    all_to_all x1, starting transfers between devices, local(): along = lax.all_to_all(pieces, 'z', 0, 0, tiled=True)  8.57 us
    all_to_all x1, waiting for transfers between devices, local(): blocks = lax.all_to_all(slab_sum, 'z', 0, 0, tiled=True)  7.9 us
    pallas_call x1, Pallas kernels, local(): call(functools.partial(grad_kernel, factor, scale), (dq_shape, peer_shape...  7.17 us
    ppermute x3, waiting for transfers between devices, local(): lax.ppermute(skewed, 'x', ring(NX, k))  6.32 us
    ppermute x3, waiting for transfers between devices, local(): away = [lax.ppermute(away[k - 1], 'x', ring(NX, -k)) for k in (1, 2, 3)]  6.32 us
    ppermute x3, starting transfers between devices, local(): away = [lax.ppermute(away[k - 1], 'x', ring(NX, -k)) for k in (1, 2, 3)]  5.07 us
  transfers between devices with their start and end apart: 24, of which 14 were waited for; matrix products, arithmetic and copies ran while one was open for 0% of the time, Pallas kernels for 2%

profile of v3, /device:TPU:32, one launch (start us, length us, event | category | flops | bytes accessed | tf_op | source)
XLA Modules:
  0.0 104.1 jit_solution(740581752933811444)
XLA Ops:
  0.6 2.1 %shard_map.86 = (bf16[1056,128]{1,0:T(8,128)(2,1)}, bf16[8,144,128]{2,1,0:T(8,128)(2,1)}) custom-call(bf16[512,128]{1,0:T(8,128)(2,1)} %bitcast.5, bf16[512,128]{1,0:T(8,128)(2,1)} %bitcast.6, bf16[512,128]{1,0:T(8,128)(2,1)} %bitcast.7, bf16[512,128]{1,0:T(8,128)(2,1)} %keys.1, bf16[512,128]{1,0:T(8,128)(2,1)} %values.1, s32[1,512]{1,0:T(1,128)} %bitcast.9), custom_call_target="tpu_custom_call" | custom-call | bytes 2097152 | tf_op jit(solution)/shard_map/pallas_call | solution.py:307
  2.7 8.6 %all-to-all-start = ((bf16[8,144,128]{2,1,0:T(8,128)(2,1)}), bf16[8,144,128]{2,1,0:T(8,128)(2,1)S(1)}, u32[]{:S(2)}, u32[]{:S(2)}) async-start(bf16[8,144,128]{2,1,0:T(8,128)(2,1)} %get-tuple-element.45), calls=%async_computation | async-start | bytes 589824 | tf_op jit(solution)/shard_map/all_to_all | solution.py:317
  11.3 1.6 %collective-permute-start = (bf16[1056,128]{1,0:T(8,128)(2,1)}, bf16[1056,128]{1,0:T(8,128)(2,1)S(1)}, u32[]{:S(2)}, u32[]{:S(2)}) collective-permute-start(bf16[1056,128]{1,0:T(8,128)(2,1)} %get-tuple-element.44), channel_id=1, source_target_pairs={{0,0},{2,194},{4,132},{6,70},{64,64},{66,2},{68,196},{70,134},{128... | collective-permute-start | bytes 811016 | tf_op jit(solution)/shard_map/ppermute | solution.py:316
  12.9 9.5 %all-to-all-done.p0 = bf16[8,144,128]{2,1,0:T(8,128)(2,1)S(1)} async-done(((bf16[8,144,128]{2,1,0:T(8,128)(2,1)}), bf16[8,144,128]{2,1,0:T(8,128)(2,1)S(1)}, u32[]{:S(2)}, u32[]{:S(2)}) %all-to-all-start) | async-done | bytes 294944 | tf_op jit(solution)/shard_map/all_to_all | solution.py:317
  22.4 1.6 %collective-permute-start.4 = (bf16[8,144,128]{2,1,0:T(8,128)(2,1)S(1)}, bf16[8,144,128]{2,1,0:T(8,128)(2,1)S(1)}, u32[]{:S(2)}, u32[]{:S(2)}) collective-permute-start(bf16[8,144,128]{2,1,0:T(8,128)(2,1)S(1)} %all-to-all-done.p0), channel_id=1, source_target_pairs={{0,64},{64,128},{128,192},{192,0},{1,65},{65,129},{129,193},{193,1... | collective-permute-start | bytes 884744 | tf_op jit(solution)/shard_map/ppermute | solution.py:319
  24.0 1.7 %collective-permute-start.6 = (bf16[8,144,128]{2,1,0:T(8,128)(2,1)S(1)}, bf16[8,144,128]{2,1,0:T(8,128)(2,1)S(1)}, u32[]{:S(2)}, u32[]{:S(2)}) collective-permute-start(bf16[8,144,128]{2,1,0:T(8,128)(2,1)S(1)} %all-to-all-done.p0), channel_id=1, source_target_pairs={{0,192},{64,0},{128,64},{192,128},{1,193},{65,1},{129,65},{193,129... | collective-permute-start | bytes 884744 | tf_op jit(solution)/shard_map/ppermute | solution.py:320
  25.6 2.8 %collective-permute-start.3 = (bf16[1056,128]{1,0:T(8,128)(2,1)S(1)}, bf16[1056,128]{1,0:T(8,128)(2,1)S(1)}, u32[]{:S(2)}, u32[]{:S(2)}) collective-permute-start(bf16[1056,128]{1,0:T(8,128)(2,1)S(1)} %collective-permute-done.refs_0_), channel_id=1, source_target_pairs={{0,6},{2,0},{4,2},{6,4},{1,7},{3,1},{5,3},{7,5},{8,14},{10,8},{12,... | collective-permute-start | bytes 811016 | tf_op jit(solution)/shard_map/ppermute | solution.py:318
  30.5 1.7 %collective-permute-start.5 = (bf16[8,80,128]{2,1,0:T(8,128)(2,1)S(1)}, bf16[8,80,128]{2,1,0:T(8,128)(2,1)S(1)}, u32[]{:S(2)}, u32[]{:S(2)}) collective-permute-start(bf16[8,80,128]{2,1,0:T(8,128)(2,1)S(1)} %slice.8), channel_id=1, source_target_pairs={{0,64},{64,128},{128,192},{192,0},{1,65},{65,129},{129,193},{193,1... | collective-permute-start | bytes 491528 | tf_op jit(solution)/shard_map/ppermute | solution.py:321
  32.2 1.8 %collective-permute-start.7 = (bf16[8,64,128]{2,1,0:T(8,128)(2,1)S(1)}, bf16[8,64,128]{2,1,0:T(8,128)(2,1)S(1)}, u32[]{:S(2)}, u32[]{:S(2)}) collective-permute-start(bf16[8,64,128]{2,1,0:T(8,128)(2,1)S(1)} %slice.9), channel_id=1, source_target_pairs={{0,192},{64,0},{128,64},{192,128},{1,193},{65,1},{129,65},{193,129... | collective-permute-start | bytes 393224 | tf_op jit(solution)/shard_map/ppermute | solution.py:322
  34.0 2.7 %collective-permute-done.3.refs_3_ = bf16[1056,128]{1,0:T(8,128)(2,1)S(1)} collective-permute-done((bf16[1056,128]{1,0:T(8,128)(2,1)S(1)}, bf16[1056,128]{1,0:T(8,128)(2,1)S(1)}, u32[]{:S(2)}, u32[]{:S(2)}) %collective-permute-start.3) | collective-permute-done | bytes 270368 | tf_op jit(solution)/shard_map/ppermute | solution.py:318
  37.5 2.7 %collective-permute-done.1.refs_1_ = bf16[1056,128]{1,0:T(8,128)(2,1)S(1)} collective-permute-done((bf16[1056,128]{1,0:T(8,128)(2,1)S(1)}, bf16[1056,128]{1,0:T(8,128)(2,1)S(1)}, u32[]{:S(2)}, u32[]{:S(2)}) %collective-permute-start.1) | collective-permute-done | bytes 270368 | tf_op jit(solution)/shard_map/ppermute | solution.py:318
  41.1 2.0 %collective-permute-done.8.peer = bf16[4,1056,128]{2,1,0:T(8,128)(2,1)S(1)} collective-permute-done((bf16[4,1056,128]{2,1,0:T(8,128)(2,1)S(1)}, bf16[4,1056,128]{2,1,0:T(8,128)(2,1)S(1)}, u32[]{:S(2)}, u32[]{:S(2)}) %collective-permute-start.8) | collective-permute-done | bytes 1081376 | tf_op jit(solution)/shard_map/ppermute | solution.py:327
  43.2 4.9 %shard_map.88 = (f32[8,1,512]{2,1,0:T(1,128)S(1)}, bf16[2176,128]{1,0:T(8,128)(2,1)S(1)}, f32[4,1,512]{2,1,0:T(1,128)S(1)}, s32[4,4]{1,0:T(4,128)S(1)}) custom-call(s32[4,2]{1,0:T(4,128)S(1)} %get-tuple-element.43.ends, bf16[4,1056,128]{2,1,0:T(8,128)(2,1)S(1)} %shard_map.87.own, bf16[4,1056,128]{2,1,0:T(8,128)(2,1)S(1)} %collective-permute-done.8.peer, ...), custom_call_target="tpu_custom_call" | custom-call | flops 2000000000 | bytes 4194304 | tf_op jit(solution)/shard_map/pallas_call | solution.py:336
  52.7 2.4 %collective-permute-done.12.l3 = f32[8,1,512]{2,1,0:T(1,128)S(1)} collective-permute-done((f32[8,1,512]{2,1,0:T(1,128)S(1)}, f32[8,1,512]{2,1,0:T(1,128)S(1)}, u32[]{:S(2)}, u32[]{:S(2)}) %collective-permute-start.12) | collective-permute-done | bytes 16416 | tf_op jit(solution)/shard_map/ppermute | solution.py:351
  55.0 1.8 %collective-permute-done.10.l1 = f32[8,1,512]{2,1,0:T(1,128)S(1)} collective-permute-done((f32[8,1,512]{2,1,0:T(1,128)S(1)}, f32[8,1,512]{2,1,0:T(1,128)S(1)}, u32[]{:S(2)}, u32[]{:S(2)}) %collective-permute-start.10) | collective-permute-done | bytes 16416 | tf_op jit(solution)/shard_map/ppermute | solution.py:351
  56.8 7.2 %shard_map.89 = (f32[4,128,512]{2,1,0:T(8,128)S(1)}, bf16[4,128,512]{2,1,0:T(8,128)(2,1)S(1)}, bf16[8,2,64,128]{3,2,1,0:T(8,128)(2,1)S(1)}, bf16[8,2,64,128]{3,2...) custom-call(s32[4,4]{1,0:T(4,128)S(1)} %get-tuple-element.52.bounds,, ...), custom_call_target="tpu_custom_call" | custom-call | flops 8000000000 | bytes 8388608 | tf_op jit(solution)/shard_map/pallas_call | solution.py:356
  64.8 2.6 %collective-permute-start.14 = (bf16[8,64,128]{2,1,0:T(8,128)(2,1)S(1)}, bf16[8,64,128]{2,1,0:T(8,128)(2,1)S(1)}, u32[]{:S(2)}, u32[]{:S(2)}) collective-permute-start(bf16[8,64,128]{2,1,0:T(8,128)(2,1)S(1)} %get-tuple-element.61), channel_id=1, source_target_pairs={{0,192},{64,0},{128,64},{192,128},{1,193},{65,1},{129,65},{193,129... | collective-permute-start | bytes 393224 | tf_op jit(solution)/shard_map/ppermute | solution.py:377
  69.1 2.1 %collective-permute-done.13.got_dk = bf16[8,64,128]{2,1,0:T(8,128)(2,1)S(1)} collective-permute-done((bf16[8,64,128]{2,1,0:T(8,128)(2,1)S(1)}, bf16[8,64,128]{2,1,0:T(8,128)(2,1)S(1)}, u32[]{:S(2)}, u32[]{:S(2)}) %collective-permute-start.13) | collective-permute-done | bytes 131104 | tf_op jit(solution)/shard_map/ppermute | solution.py:376
  71.2 1.7 %collective-permute-done.16.refs_1_ = bf16[128,512]{1,0:T(8,128)(2,1)S(1)} collective-permute-done((bf16[128,512]{1,0:T(8,128)(2,1)S(1)}, bf16[128,512]{1,0:T(8,128)(2,1)S(1)}, u32[]{:S(2)}, u32[]{:S(2)}) %collective-permute-start.16) | collective-permute-done | bytes 131104 | tf_op jit(solution)/shard_map/ppermute | solution.py:378
  73.1 3.2 %collective-permute-start.18 = (bf16[8,2,64,128]{3,2,1,0:T(8,128)(2,1)S(1)}, bf16[8,2,64,128]{3,2,1,0:T(8,128)(2,1)S(1)}, u32[]{:S(2)}, u32[]{:S(2)}) collective-permute-start(bf16[8,2,64,128]{3,2,1,0:T(8,128)(2,1)S(1)} %get-tuple-element.68), channel_id=1, source_target_pairs={{0,192},{64,0},{128,64},{192,128},{1,193},{65,1},{129,65},{193,129... | collective-permute-start | bytes 786440 | tf_op jit(solution)/shard_map/ppermute | solution.py:381
  77.5 2.3 %collective-permute-start.20 = (bf16[128,512]{1,0:T(8,128)(2,1)S(1)}, bf16[128,512]{1,0:T(8,128)(2,1)S(1)}, u32[]{:S(2)}, u32[]{:S(2)}) collective-permute-start(bf16[128,512]{1,0:T(8,128)(2,1)S(1)} %get-tuple-element.71), channel_id=1, source_target_pairs={{0,2},{2,4},{4,6},{6,0},{1,3},{3,5},{5,7},{7,1},{8,10},{10,12},{12... | collective-permute-start | bytes 393224 | tf_op jit(solution)/shard_map/ppermute | solution.py:378
  79.9 3.3 %collective-permute-done.19.refs_2_ = bf16[128,512]{1,0:T(8,128)(2,1)S(1)} collective-permute-done((bf16[128,512]{1,0:T(8,128)(2,1)S(1)}, bf16[128,512]{1,0:T(8,128)(2,1)S(1)}, u32[]{:S(2)}, u32[]{:S(2)}) %collective-permute-start.19) | collective-permute-done | bytes 131104 | tf_op jit(solution)/shard_map/ppermute | solution.py:378
  85.3 8.7 %all-to-all-start.1 = ((bf16[8,2,64,128]{3,2,1,0:T(8,128)(2,1)}), bf16[8,2,64,128]{3,2,1,0:T(8,128)(2,1)S(1)}, u32[]{:S(2)}, u32[]{:S(2)}) async-start(bf16[8,2,64,128]{3,2,1,0:T(8,128)(2,1)} %shard_map.92), calls=%async_computation.1 | async-start | bytes 524288 | tf_op jit(solution)/shard_map/all_to_all | solution.py:384
  95.6 7.9 %all-to-all-done.1.blocks = bf16[8,2,64,128]{3,2,1,0:T(8,128)(2,1)S(1)} async-done(((bf16[8,2,64,128]{3,2,1,0:T(8,128)(2,1)}), bf16[8,2,64,128]{3,2,1,0:T(8,128)(2,1)S(1)}, u32[]{:S(2)}, u32[]{:S(2)}) %all-to-all-start.1) | async-done | bytes 262176 | tf_op jit(solution)/shard_map/all_to_all | solution.py:384
  (38 shorter events, 16.5 us)
Async XLA Ops:
  2.7 19.7 %all-to-all-start = ((bf16[8,144,128]{2,1,0:T(8,128)(2,1)}), bf16[8,144,128]{2,1,0:T(8,128)(2,1)S(1)}, u32[]{:S(2)}, u32[]{:S(2)}) async-start(bf16[8,144,128]{2,1,0:T(8,128)(2,1)} %get-tuple-element.45), calls=%async_computation | async-start | bytes 589824 | tf_op jit(solution)/shard_map/all_to_all | solution.py:317
  11.3 14.4 %collective-permute-start = (bf16[1056,128]{1,0:T(8,128)(2,1)}, bf16[1056,128]{1,0:T(8,128)(2,1)S(1)}, u32[]{:S(2)}, u32[]{:S(2)}) collective-permute-start(bf16[1056,128]{1,0:T(8,128)(2,1)} %get-tuple-element.44), channel_id=1, source_target_pairs={{0,0},{2,194},{4,132},{6,70},{64,64},{66,2},{68,196},{70,134},{128... | collective-permute-start | bytes 811016 | tf_op jit(solution)/shard_map/ppermute | solution.py:316
  22.4 8.1 %collective-permute-start.4 = (bf16[8,144,128]{2,1,0:T(8,128)(2,1)S(1)}, bf16[8,144,128]{2,1,0:T(8,128)(2,1)S(1)}, u32[]{:S(2)}, u32[]{:S(2)}) collective-permute-start(bf16[8,144,128]{2,1,0:T(8,128)(2,1)S(1)} %all-to-all-done.p0), channel_id=1, source_target_pairs={{0,64},{64,128},{128,192},{192,0},{1,65},{65,129},{129,193},{193,1... | collective-permute-start | bytes 884744 | tf_op jit(solution)/shard_map/ppermute | solution.py:319
  24.0 8.2 %collective-permute-start.6 = (bf16[8,144,128]{2,1,0:T(8,128)(2,1)S(1)}, bf16[8,144,128]{2,1,0:T(8,128)(2,1)S(1)}, u32[]{:S(2)}, u32[]{:S(2)}) collective-permute-start(bf16[8,144,128]{2,1,0:T(8,128)(2,1)S(1)} %all-to-all-done.p0), channel_id=1, source_target_pairs={{0,192},{64,0},{128,64},{192,128},{1,193},{65,1},{129,65},{193,129... | collective-permute-start | bytes 884744 | tf_op jit(solution)/shard_map/ppermute | solution.py:320
  25.6 11.0 %collective-permute-start.3 = (bf16[1056,128]{1,0:T(8,128)(2,1)S(1)}, bf16[1056,128]{1,0:T(8,128)(2,1)S(1)}, u32[]{:S(2)}, u32[]{:S(2)}) collective-permute-start(bf16[1056,128]{1,0:T(8,128)(2,1)S(1)} %collective-permute-done.refs_0_), channel_id=1, source_target_pairs={{0,6},{2,0},{4,2},{6,4},{1,7},{3,1},{5,3},{7,5},{8,14},{10,8},{12,... | collective-permute-start | bytes 811016 | tf_op jit(solution)/shard_map/ppermute | solution.py:318
  28.4 9.2 %collective-permute-start.2 = (bf16[1056,128]{1,0:T(8,128)(2,1)S(1)}, bf16[1056,128]{1,0:T(8,128)(2,1)S(1)}, u32[]{:S(2)}, u32[]{:S(2)}) collective-permute-start(bf16[1056,128]{1,0:T(8,128)(2,1)S(1)} %collective-permute-done.refs_0_), channel_id=1, source_target_pairs={{0,4},{2,6},{4,0},{6,2},{1,5},{3,7},{5,1},{7,3},{8,12},{10,14},{12... | collective-permute-start | bytes 811016 | tf_op jit(solution)/shard_map/ppermute | solution.py:318
  29.2 11.1 %collective-permute-start.1 = (bf16[1056,128]{1,0:T(8,128)(2,1)S(1)}, bf16[1056,128]{1,0:T(8,128)(2,1)S(1)}, u32[]{:S(2)}, u32[]{:S(2)}) collective-permute-start(bf16[1056,128]{1,0:T(8,128)(2,1)S(1)} %collective-permute-done.refs_0_), channel_id=1, source_target_pairs={{0,2},{2,4},{4,6},{6,0},{1,3},{3,5},{5,7},{7,1},{8,10},{10,12},{12... | collective-permute-start | bytes 811016 | tf_op jit(solution)/shard_map/ppermute | solution.py:318
  30.5 9.8 %collective-permute-start.5 = (bf16[8,80,128]{2,1,0:T(8,128)(2,1)S(1)}, bf16[8,80,128]{2,1,0:T(8,128)(2,1)S(1)}, u32[]{:S(2)}, u32[]{:S(2)}) collective-permute-start(bf16[8,80,128]{2,1,0:T(8,128)(2,1)S(1)} %slice.8), channel_id=1, source_target_pairs={{0,64},{64,128},{128,192},{192,0},{1,65},{65,129},{129,193},{193,1... | collective-permute-start | bytes 491528 | tf_op jit(solution)/shard_map/ppermute | solution.py:321
  32.2 8.1 %collective-permute-start.7 = (bf16[8,64,128]{2,1,0:T(8,128)(2,1)S(1)}, bf16[8,64,128]{2,1,0:T(8,128)(2,1)S(1)}, u32[]{:S(2)}, u32[]{:S(2)}) collective-permute-start(bf16[8,64,128]{2,1,0:T(8,128)(2,1)S(1)} %slice.9), channel_id=1, source_target_pairs={{0,192},{64,0},{128,64},{192,128},{1,193},{65,1},{129,65},{193,129... | collective-permute-start | bytes 393224 | tf_op jit(solution)/shard_map/ppermute | solution.py:322
  40.4 2.8 %collective-permute-start.8 = (bf16[4,1056,128]{2,1,0:T(8,128)(2,1)S(1)}, bf16[4,1056,128]{2,1,0:T(8,128)(2,1)S(1)}, u32[]{:S(2)}, u32[]{:S(2)}) collective-permute-start(bf16[4,1056,128]{2,1,0:T(8,128)(2,1)S(1)} %shard_map.87.own), channel_id=1, source_target_pairs={{0,1},{1,0},{2,3},{3,2},{4,5},{5,4},{6,7},{7,6},{8,9},{9,8},{10,11... | collective-permute-start | bytes 3244040 | tf_op jit(solution)/shard_map/ppermute | solution.py:327
  48.1 1.6 %collective-permute-start.9 = (f32[8,1,512]{2,1,0:T(1,128)S(1)}, f32[8,1,512]{2,1,0:T(1,128)S(1)}, u32[]{:S(2)}, u32[]{:S(2)}) collective-permute-start(f32[8,1,512]{2,1,0:T(1,128)S(1)} %get-tuple-element.56), channel_id=1, source_target_pairs={{0,1},{1,0},{2,3},{3,2},{4,5},{5,4},{6,7},{7,6},{8,9},{9,8},{10,11... | collective-permute-start | bytes 49160 | tf_op jit(solution)/shard_map/ppermute | solution.py:350
  49.7 5.3 %collective-permute-start.12 = (f32[8,1,512]{2,1,0:T(1,128)S(1)}, f32[8,1,512]{2,1,0:T(1,128)S(1)}, u32[]{:S(2)}, u32[]{:S(2)}) collective-permute-start(f32[8,1,512]{2,1,0:T(1,128)S(1)} %multiply_add_fusion.l0), channel_id=1, source_target_pairs={{0,4},{2,6},{4,0},{6,2},{1,5},{3,7},{5,1},{7,3},{8,12},{10,14},{12... | collective-permute-start | bytes 49160 | tf_op jit(solution)/shard_map/ppermute | solution.py:351
  50.6 4.4 %collective-permute-start.11 = (f32[8,1,512]{2,1,0:T(1,128)S(1)}, f32[8,1,512]{2,1,0:T(1,128)S(1)}, u32[]{:S(2)}, u32[]{:S(2)}) collective-permute-start(f32[8,1,512]{2,1,0:T(1,128)S(1)} %multiply_add_fusion.l0), channel_id=1, source_target_pairs={{0,6},{2,0},{4,2},{6,4},{1,7},{3,1},{5,3},{7,5},{8,14},{10,8},{12,... | collective-permute-start | bytes 49160 | tf_op jit(solution)/shard_map/ppermute | solution.py:351
  51.9 5.0 %collective-permute-start.10 = (f32[8,1,512]{2,1,0:T(1,128)S(1)}, f32[8,1,512]{2,1,0:T(1,128)S(1)}, u32[]{:S(2)}, u32[]{:S(2)}) collective-permute-start(f32[8,1,512]{2,1,0:T(1,128)S(1)} %multiply_add_fusion.l0), channel_id=1, source_target_pairs={{0,2},{2,4},{4,6},{6,0},{1,3},{3,5},{5,7},{7,1},{8,10},{10,12},{12... | collective-permute-start | bytes 49160 | tf_op jit(solution)/shard_map/ppermute | solution.py:351
  64.0 3.4 %collective-permute-start.15 = (bf16[4,128,512]{2,1,0:T(8,128)(2,1)S(1)}, bf16[4,128,512]{2,1,0:T(8,128)(2,1)S(1)}, u32[]{:S(2)}, u32[]{:S(2)}) collective-permute-start(bf16[4,128,512]{2,1,0:T(8,128)(2,1)S(1)} %get-tuple-element.63), channel_id=1, source_target_pairs={{0,1},{1,0},{2,3},{3,2},{4,5},{5,4},{6,7},{7,6},{8,9},{9,8},{10,11... | collective-permute-start | bytes 1572872 | tf_op jit(solution)/shard_map/ppermute | solution.py:374
  64.1 7.1 %collective-permute-start.13 = (bf16[8,64,128]{2,1,0:T(8,128)(2,1)S(1)}, bf16[8,64,128]{2,1,0:T(8,128)(2,1)S(1)}, u32[]{:S(2)}, u32[]{:S(2)}) collective-permute-start(bf16[8,64,128]{2,1,0:T(8,128)(2,1)S(1)} %get-tuple-element.60), channel_id=1, source_target_pairs={{0,64},{64,128},{128,192},{192,0},{1,65},{65,129},{129,193},{193,1... | collective-permute-start | bytes 393224 | tf_op jit(solution)/shard_map/ppermute | solution.py:376
  64.8 6.4 %collective-permute-start.14 = (bf16[8,64,128]{2,1,0:T(8,128)(2,1)S(1)}, bf16[8,64,128]{2,1,0:T(8,128)(2,1)S(1)}, u32[]{:S(2)}, u32[]{:S(2)}) collective-permute-start(bf16[8,64,128]{2,1,0:T(8,128)(2,1)S(1)} %get-tuple-element.61), channel_id=1, source_target_pairs={{0,192},{64,0},{128,64},{192,128},{1,193},{65,1},{129,65},{193,129... | collective-permute-start | bytes 393224 | tf_op jit(solution)/shard_map/ppermute | solution.py:377
  67.6 5.4 %collective-permute-start.16 = (bf16[128,512]{1,0:T(8,128)(2,1)S(1)}, bf16[128,512]{1,0:T(8,128)(2,1)S(1)}, u32[]{:S(2)}, u32[]{:S(2)}) collective-permute-start(bf16[128,512]{1,0:T(8,128)(2,1)S(1)} %get-tuple-element.64), channel_id=1, source_target_pairs={{0,6},{2,0},{4,2},{6,4},{1,7},{3,1},{5,3},{7,5},{8,14},{10,8},{12,... | collective-permute-start | bytes 393224 | tf_op jit(solution)/shard_map/ppermute | solution.py:378
  73.0 11.5 %collective-permute-start.17 = (bf16[8,2,64,128]{3,2,1,0:T(8,128)(2,1)S(1)}, bf16[8,2,64,128]{3,2,1,0:T(8,128)(2,1)S(1)}, u32[]{:S(2)}, u32[]{:S(2)}) collective-permute-start(bf16[8,2,64,128]{3,2,1,0:T(8,128)(2,1)S(1)} %get-tuple-element.67), channel_id=1, source_target_pairs={{0,64},{64,128},{128,192},{192,0},{1,65},{65,129},{129,193},{193,1... | collective-permute-start | bytes 786440 | tf_op jit(solution)/shard_map/ppermute | solution.py:381
  73.1 11.4 %collective-permute-start.18 = (bf16[8,2,64,128]{3,2,1,0:T(8,128)(2,1)S(1)}, bf16[8,2,64,128]{3,2,1,0:T(8,128)(2,1)S(1)}, u32[]{:S(2)}, u32[]{:S(2)}) collective-permute-start(bf16[8,2,64,128]{3,2,1,0:T(8,128)(2,1)S(1)} %get-tuple-element.68), channel_id=1, source_target_pairs={{0,192},{64,0},{128,64},{192,128},{1,193},{65,1},{129,65},{193,129... | collective-permute-start | bytes 786440 | tf_op jit(solution)/shard_map/ppermute | solution.py:381
  76.3 6.8 %collective-permute-start.19 = (bf16[128,512]{1,0:T(8,128)(2,1)S(1)}, bf16[128,512]{1,0:T(8,128)(2,1)S(1)}, u32[]{:S(2)}, u32[]{:S(2)}) collective-permute-start(bf16[128,512]{1,0:T(8,128)(2,1)S(1)} %get-tuple-element.70), channel_id=1, source_target_pairs={{0,4},{2,6},{4,0},{6,2},{1,5},{3,7},{5,1},{7,3},{8,12},{10,14},{12... | collective-permute-start | bytes 393224 | tf_op jit(solution)/shard_map/ppermute | solution.py:378
  77.5 7.0 %collective-permute-start.20 = (bf16[128,512]{1,0:T(8,128)(2,1)S(1)}, bf16[128,512]{1,0:T(8,128)(2,1)S(1)}, u32[]{:S(2)}, u32[]{:S(2)}) collective-permute-start(bf16[128,512]{1,0:T(8,128)(2,1)S(1)} %get-tuple-element.71), channel_id=1, source_target_pairs={{0,2},{2,4},{4,6},{6,0},{1,3},{3,5},{5,7},{7,1},{8,10},{10,12},{12... | collective-permute-start | bytes 393224 | tf_op jit(solution)/shard_map/ppermute | solution.py:378
  85.3 18.2 %all-to-all-start.1 = ((bf16[8,2,64,128]{3,2,1,0:T(8,128)(2,1)}), bf16[8,2,64,128]{3,2,1,0:T(8,128)(2,1)S(1)}, u32[]{:S(2)}, u32[]{:S(2)}) async-start(bf16[8,2,64,128]{3,2,1,0:T(8,128)(2,1)} %shard_map.92), calls=%async_computation.1 | async-start | bytes 524288 | tf_op jit(solution)/shard_map/all_to_all | solution.py:384
  94.1 0.7 collective-permute-start.21

commit v4 on v3

--- a/solution.py
+++ b/solution.py
@@ -105,7 +105,7 @@
     x, y, c = (lax.axis_index(name) for name in ("x", "y", "c"))
     nz, rows, width = p2.shape
     share = rows - EXTRA
-    tok = own.shape[1] // 2 - EXTRA
+    tok = own.shape[1] - EXTRA
     number = lax.broadcasted_iota(jnp.int32, (DOCS, width), 0).astype(F32)
     below = jnp.zeros((DOCS, width), F32)
     for k, piece in enumerate((p0, p1, p2, p3)):
@@ -166,13 +166,13 @@
 
 
 def grad_kernel(
-    factor, scale, bounds, own, peer, high_in, p0, p1, p2, p3, key_all, low_in, l0, l1, l2, l3,
-    dq_own, dq_peer, here, up, down, far_dk, far_dv, value_all, dk, dv, lse, dq_turned,
+    factor, scale, bounds, own, peer, grad_own, grad_peer, high_in, p0, p1, p2, p3, key_all, low_in, l0, l1, l2, l3,
+    dq_own, dq_peer, here, up_dk, up_dv, down_dk, down_dv, far_dk, far_dv, value_all, dk, dv, lse, dq_turned,
 ):
     x, y, c = (lax.axis_index(name) for name in ("x", "y", "c"))
     nz, share, width = p2.shape
     slab = nz * share
-    tok = own.shape[1] // 2 - EXTRA
+    tok = own.shape[1] - EXTRA
     for k, piece in enumerate((p0, p1, p2, p3)):
         for i in range(nz):
             where = block_row(y, k, i, nz, share)
@@ -187,11 +187,11 @@
         low = low_in[m]
         high = high_in[m]
         heads = []
-        for sets, head in ((own, c), (peer, NC - 1 - c)):
-            at = tok + EXTRA
-            extra = sets[m, at + tok : 2 * at, :].astype(F32)
+        for queries, grads, head in ((own, grad_own, c), (peer, grad_peer, NC - 1 - c)):
+            extra = grads[m, tok : tok + EXTRA, :].astype(F32)
             delta = rows_to_line(extra[0:n] + extra[n : 2 * n] + extra[2 * n : 3 * n])
-            heads.append((sets[m, 0:tok, :], sets[m, at : at + tok, :], delta, lse[NC * lax.rem(x - m + NX, NX) + head]))
+            norm = lse[NC * lax.rem(x - m + NX, NX) + head]
+            heads.append((queries[m, 0:tok, :], grads[m, 0:tok, :], delta, norm))
         dq_turned[...] = jnp.zeros_like(dq_turned)
 
         def step(masked, size, first, carry):
@@ -224,11 +224,11 @@
         at = pl.ds(pl.multiple_of(lax.rem(y + by, NY) * slab, slab), slab)
         return (ref[at, :] * (scale if ref is dk else 1.0)).astype(BF16).reshape(nz, share, width)
 
-    for out, by in ((here, 0), (up, 1), (down, NY - 1)):
-        out[:, 0] = slab_of(dk, by)
-        out[:, 1] = slab_of(dv, by)
-    far_dk[...] = slab_of(dk, 2)
-    far_dv[...] = slab_of(dv, 2)
+    here[:, 0] = slab_of(dk, 0)
+    here[:, 1] = slab_of(dv, 0)
+    for out_dk, out_dv, by in ((up_dk, up_dv, 1), (down_dk, down_dv, NY - 1), (far_dk, far_dv, 2)):
+        out_dk[...] = slab_of(dk, by)
+        out_dv[...] = slab_of(dv, by)
 
 
 def block_row(y, k, i, nz, share):
@@ -241,8 +241,11 @@
 
 
 def stack_kernel(*refs):
-    for i, piece in enumerate(refs[:-1]):
-        refs[-1][i] = piece[...]
+    *pieces, queries, grads = refs
+    half = queries.shape[1]
+    for i, piece in enumerate(pieces):
+        queries[i] = piece[0:half, :]
+        grads[i] = piece[half : 2 * half, :]
 
 
 def add_kernel(*refs):
@@ -256,11 +259,9 @@
     out[...] = jnp.transpose(part[...].astype(F32)).astype(BF16)
 
 
-def relay_kernel(up, down, got_dk, got_dv, new_up, new_down):
-    new_up[:, 0] = (up[:, 0].astype(F32) + got_dk[...].astype(F32)).astype(BF16)
-    new_up[:, 1] = up[:, 1]
-    new_down[:, 0] = down[:, 0]
-    new_down[:, 1] = (down[:, 1].astype(F32) + got_dv[...].astype(F32)).astype(BF16)
+def slab_kernel(here, below_dk, below_dv, above_dk, above_dv, out):
+    for i, parts in enumerate(((below_dk, above_dk), (below_dv, above_dv))):
+        out[:, i] = (here[:, i].astype(F32) + parts[0][...].astype(F32) + parts[1][...].astype(F32)).astype(BF16)
 
 
 def last_kernel(blocks, dk, dv):
@@ -321,10 +322,10 @@
     far_keys = lax.ppermute(before[:, : share + EXTRA], "y", ring(NY, 1))
     far_values = lax.ppermute(after[:, share + EXTRA :], "y", ring(NY, -1))
     moved, far_keys, far_values = lax.optimization_barrier((moved, far_keys, far_values))
-    own = call(stack_kernel, shape((NX,) + sent.shape, BF16), [VMEM] * NX, VMEM, moved=2**21)(
-        *moved
-    )
+    half_shape = shape((NX, tok + EXTRA, width), BF16)
+    own, grad_own = call(stack_kernel, (half_shape, half_shape), [VMEM] * NX, [VMEM] * 2, moved=2**21)(*moved)
     peer = lax.ppermute(own, "c", swap)
+    grad_peer = lax.ppermute(grad_own, "c", swap)
 
     total = share * nz * NY + TILE // 2
     high, ends = call(
@@ -353,11 +354,11 @@
     dq_shape, peer_shape = (shape((NX, width, tok), kind) for kind in (F32, BF16))
     slab_shape = shape((nz, 2, share, width), BF16)
     far_shape = shape((nz, share, width), BF16)
-    dq_own, dq_peer, here, up, down, far_dk, far_dv = call(
+    dq_own, dq_peer, here, up_dk, up_dv, down_dk, down_dv, far_dk, far_dv = call(
         functools.partial(grad_kernel, factor, scale),
-        (dq_shape, peer_shape, slab_shape, slab_shape, slab_shape, far_shape, far_shape),
-        [SMEM] + [VMEM] * 13,
-        [VMEM] * 7,
+        (dq_shape, peer_shape, slab_shape) + (far_shape,) * 6,
+        [SMEM] + [VMEM] * 15,
+        [VMEM] * 9,
         scratch=(
             pltpu.VMEM((total, width), BF16),
             pltpu.VMEM((total, width), F32),
@@ -367,7 +368,7 @@
         ),
         flops=8 * 10**9,
         moved=8 * 2**20,
-    )(bounds, own, peer, high, along, before, far_values, after, key_all, low, *lse_all)
+    )(bounds, own, peer, grad_own, grad_peer, high, along, before, far_values, after, key_all, low, *lse_all)
 
     one = shape((width, tok), BF16)
     kept, *away = call(query_kernel, (one,) * NX, [VMEM] * 2, [VMEM] * NX, moved=3 * 2**20)(
@@ -376,11 +377,12 @@
     got_dk = lax.ppermute(far_dk, "y", ring(NY, 1))
     got_dv = lax.ppermute(far_dv, "y", ring(NY, -1))
     away = [lax.ppermute(away[k - 1], "x", ring(NX, -k)) for k in (1, 2, 3)]
-    got_dk, got_dv, away[0] = lax.optimization_barrier((got_dk, got_dv, away[0]))
-    up, down = call(relay_kernel, (slab_shape,) * 2, [VMEM] * 4, [VMEM] * 2, moved=5 * 2**18)(up, down, got_dk, got_dv)
-    arrived = [here, lax.ppermute(up, "y", ring(NY, 1)), lax.ppermute(down, "y", ring(NY, -1))]
+    got_dk, got_dv, kept = lax.optimization_barrier((got_dk, got_dv, kept))
+    up_dk = call(add_kernel, far_shape, [VMEM] * 2, VMEM, moved=2**19)(up_dk, got_dk)
+    down_dv = call(add_kernel, far_shape, [VMEM] * 2, VMEM, moved=2**19)(down_dv, got_dv)
+    arrived = [here] + [lax.ppermute(part, "y", ring(NY, by)) for part, by in ((up_dk, 1), (up_dv, 1), (down_dk, -1), (down_dv, -1))]
     arrived, away = lax.optimization_barrier((arrived, away))
-    slab_sum = call(add_kernel, slab_shape, [VMEM] * 3, VMEM, moved=5 * 2**18)(*arrived)
+    slab_sum = call(slab_kernel, slab_shape, [VMEM] * 5, VMEM, moved=5 * 2**18)(*arrived)
     blocks = lax.all_to_all(slab_sum, "z", 0, 0, tiled=True)
     dq = call(add_kernel, one, [VMEM] * 4, VMEM, moved=2**19)(kept, *away)
     dq = lax.ppermute(dq, ("y", "x"), shift(0, True))

time: 104 us -> 104 us (level); the launches traced: 104 us -> 102 us
    ppermute x2 -> x5, waiting for transfers between devices: 0.01 us -> 3.66 us  [the longest x4 3.66 us: local(): lax.ppermute(part, 'y', ring(NY, by))]
    ppermute x2 -> x5, starting transfers between devices: 3.31 us -> 6.85 us  [the longest x4 6.35 us: local(): lax.ppermute(part, 'y', ring(NY, by))]
    ppermute x3, waiting for transfers between devices: 6.32 us -> 3.36 us  [local(): away = [lax.ppermute(away[k - 1], 'x', ring(NX, -k)) for k in (1, 2, 3)]]
    ppermute x3, starting transfers between devices: 5.07 us -> 2.5 us  [local(): away = [lax.ppermute(away[k - 1], 'x', ring(NX, -k)) for k in (1, 2, 3)]]
    ppermute x1, waiting for transfers between devices: 2.12 us -> 0.48 us  [local(): got_dk = lax.ppermute(far_dk, 'y', ring(NY, 1))]
    ppermute x1, waiting for transfers between devices: 2.03 us -> 0.78 us  [local(): peer = lax.ppermute(own, 'c', swap)]
  transfers between devices with their start and end apart: 24 -> 27, of which waited for: 14 -> 14; matrix products, arithmetic and copies ran while one was open for 0% -> 0% of each run, Pallas kernels for 2% -> 6%
where the time goes in v4:
time: 104 us; the launch traced here: 102 us
  starting transfers between devices  45.7 us (44%)
  waiting for transfers between devices  38.6 us (37%)
  Pallas kernels  17.3 us (17%)
    all_to_all x1, waiting for transfers between devices, local(): along = lax.all_to_all(pieces, 'z', 0, 0, tiled=True)  10.4 us
    all_to_all x1, starting transfers between devices, local(): along = lax.all_to_all(pieces, 'z', 0, 0, tiled=True)  8.7 us
    all_to_all x1, starting transfers between devices, local(): blocks = lax.all_to_all(slab_sum, 'z', 0, 0, tiled=True)  8.17 us
    all_to_all x1, waiting for transfers between devices, local(): blocks = lax.all_to_all(slab_sum, 'z', 0, 0, tiled=True)  7.76 us
    pallas_call x1, Pallas kernels, local(): call(functools.partial(grad_kernel, factor, scale), (dq_shape, peer_shape...  7.2 us
    ppermute x4, starting transfers between devices, local(): lax.ppermute(part, 'y', ring(NY, by))  6.35 us
    ppermute x3, waiting for transfers between devices, local(): lax.ppermute(skewed, 'x', ring(NX, k))  6.32 us
    pallas_call x1, Pallas kernels, local(): call(functools.partial(stats_kernel, factor), (shape((NC * NY, 1, tok), F...  4.88 us
  transfers between devices with their start and end apart: 27, of which 14 were waited for; matrix products, arithmetic and copies ran while one was open for 0% of the time, Pallas kernels for 6%

profile of v4, /device:TPU:32, one launch (start us, length us, event | category | flops | bytes accessed | tf_op | source)
XLA Modules:
  0.0 102.5 jit_solution(6091239417576864051)
XLA Ops:
  0.6 2.1 %shard_map.86 = (bf16[1056,128]{1,0:T(8,128)(2,1)}, bf16[8,144,128]{2,1,0:T(8,128)(2,1)}) custom-call(bf16[512,128]{1,0:T(8,128)(2,1)} %bitcast.5, bf16[512,128]{1,0:T(8,128)(2,1)} %bitcast.6, bf16[512,128]{1,0:T(8,128)(2,1)} %bitcast.7, bf16[512,128]{1,0:T(8,128)(2,1)} %keys.1, bf16[512,128]{1,0:T(8,128)(2,1)} %values.1, s32[1,512]{1,0:T(1,128)} %bitcast.9), custom_call_target="tpu_custom_call" | custom-call | bytes 2097152 | tf_op jit(solution)/shard_map/pallas_call | solution.py:308
  2.7 8.7 %all-to-all-start = ((bf16[8,144,128]{2,1,0:T(8,128)(2,1)}), bf16[8,144,128]{2,1,0:T(8,128)(2,1)S(1)}, u32[]{:S(2)}, u32[]{:S(2)}) async-start(bf16[8,144,128]{2,1,0:T(8,128)(2,1)} %get-tuple-element.49), calls=%async_computation | async-start | bytes 589824 | tf_op jit(solution)/shard_map/all_to_all | solution.py:318
  12.1 10.4 %all-to-all-done.p0 = bf16[8,144,128]{2,1,0:T(8,128)(2,1)S(1)} async-done(((bf16[8,144,128]{2,1,0:T(8,128)(2,1)}), bf16[8,144,128]{2,1,0:T(8,128)(2,1)S(1)}, u32[]{:S(2)}, u32[]{:S(2)}) %all-to-all-start) | async-done | bytes 294944 | tf_op jit(solution)/shard_map/all_to_all | solution.py:318
  22.5 1.6 %collective-permute-start.4 = (bf16[8,144,128]{2,1,0:T(8,128)(2,1)S(1)}, bf16[8,144,128]{2,1,0:T(8,128)(2,1)S(1)}, u32[]{:S(2)}, u32[]{:S(2)}) collective-permute-start(bf16[8,144,128]{2,1,0:T(8,128)(2,1)S(1)} %all-to-all-done.p0), channel_id=1, source_target_pairs={{0,64},{64,128},{128,192},{192,0},{1,65},{65,129},{129,193},{193,1... | collective-permute-start | bytes 884744 | tf_op jit(solution)/shard_map/ppermute | solution.py:320
  24.1 1.7 %collective-permute-start.6 = (bf16[8,144,128]{2,1,0:T(8,128)(2,1)S(1)}, bf16[8,144,128]{2,1,0:T(8,128)(2,1)S(1)}, u32[]{:S(2)}, u32[]{:S(2)}) collective-permute-start(bf16[8,144,128]{2,1,0:T(8,128)(2,1)S(1)} %all-to-all-done.p0), channel_id=1, source_target_pairs={{0,192},{64,0},{128,64},{192,128},{1,193},{65,1},{129,65},{193,129... | collective-permute-start | bytes 884744 | tf_op jit(solution)/shard_map/ppermute | solution.py:321
  25.8 2.8 %collective-permute-start.3 = (bf16[1056,128]{1,0:T(8,128)(2,1)S(1)}, bf16[1056,128]{1,0:T(8,128)(2,1)S(1)}, u32[]{:S(2)}, u32[]{:S(2)}) collective-permute-start(bf16[1056,128]{1,0:T(8,128)(2,1)S(1)} %collective-permute-done.refs_0_), channel_id=1, source_target_pairs={{0,6},{2,0},{4,2},{6,4},{1,7},{3,1},{5,3},{7,5},{8,14},{10,8},{12,... | collective-permute-start | bytes 811016 | tf_op jit(solution)/shard_map/ppermute | solution.py:319
  30.6 1.7 %collective-permute-start.5 = (bf16[8,80,128]{2,1,0:T(8,128)(2,1)S(1)}, bf16[8,80,128]{2,1,0:T(8,128)(2,1)S(1)}, u32[]{:S(2)}, u32[]{:S(2)}) collective-permute-start(bf16[8,80,128]{2,1,0:T(8,128)(2,1)S(1)} %slice.8), channel_id=1, source_target_pairs={{0,64},{64,128},{128,192},{192,0},{1,65},{65,129},{129,193},{193,1... | collective-permute-start | bytes 491528 | tf_op jit(solution)/shard_map/ppermute | solution.py:322
  32.3 1.8 %collective-permute-start.7 = (bf16[8,64,128]{2,1,0:T(8,128)(2,1)S(1)}, bf16[8,64,128]{2,1,0:T(8,128)(2,1)S(1)}, u32[]{:S(2)}, u32[]{:S(2)}) collective-permute-start(bf16[8,64,128]{2,1,0:T(8,128)(2,1)S(1)} %slice.9), channel_id=1, source_target_pairs={{0,192},{64,0},{128,64},{192,128},{1,193},{65,1},{129,65},{193,129... | collective-permute-start | bytes 393224 | tf_op jit(solution)/shard_map/ppermute | solution.py:323
  34.1 2.7 %collective-permute-done.3.refs_3_ = bf16[1056,128]{1,0:T(8,128)(2,1)S(1)} collective-permute-done((bf16[1056,128]{1,0:T(8,128)(2,1)S(1)}, bf16[1056,128]{1,0:T(8,128)(2,1)S(1)}, u32[]{:S(2)}, u32[]{:S(2)}) %collective-permute-start.3) | collective-permute-done | bytes 270368 | tf_op jit(solution)/shard_map/ppermute | solution.py:319
  37.7 2.7 %collective-permute-done.1.refs_1_ = bf16[1056,128]{1,0:T(8,128)(2,1)S(1)} collective-permute-done((bf16[1056,128]{1,0:T(8,128)(2,1)S(1)}, bf16[1056,128]{1,0:T(8,128)(2,1)S(1)}, u32[]{:S(2)}, u32[]{:S(2)}) %collective-permute-start.1) | collective-permute-done | bytes 270368 | tf_op jit(solution)/shard_map/ppermute | solution.py:319
  42.5 4.9 %shard_map.88 = (f32[8,1,512]{2,1,0:T(1,128)S(1)}, bf16[2176,128]{1,0:T(8,128)(2,1)S(1)}, f32[4,1,512]{2,1,0:T(1,128)S(1)}, s32[4,4]{1,0:T(4,128)S(1)}) custom-call(s32[4,2]{1,0:T(4,128)S(1)} %get-tuple-element.47.ends, bf16[4,528,128]{2,1,0:T(8,128)(2,1)S(1)} %get-tuple-element.54.own, bf16[4,528,128]{2,1,0:T(8,128)(2,1)S(1)} %collective-permute-done.8.peer, ...), custom_call_target="tpu_custom_call" | custom-call | flops 2000000000 | bytes 4194304 | tf_op jit(solution)/shard_map/pallas_call | solution.py:337
  50.0 1.4 %collective-permute-start.12 = (f32[8,1,512]{2,1,0:T(1,128)S(1)}, f32[8,1,512]{2,1,0:T(1,128)S(1)}, u32[]{:S(2)}, u32[]{:S(2)}) collective-permute-start(f32[8,1,512]{2,1,0:T(1,128)S(1)} %multiply_add_fusion.l0), channel_id=1, source_target_pairs={{0,6},{2,0},{4,2},{6,4},{1,7},{3,1},{5,3},{7,5},{8,14},{10,8},{12,... | collective-permute-start | bytes 49160 | tf_op jit(solution)/shard_map/ppermute | solution.py:352
  52.0 2.1 %collective-permute-done.13.l3 = f32[8,1,512]{2,1,0:T(1,128)S(1)} collective-permute-done((f32[8,1,512]{2,1,0:T(1,128)S(1)}, f32[8,1,512]{2,1,0:T(1,128)S(1)}, u32[]{:S(2)}, u32[]{:S(2)}) %collective-permute-start.13) | collective-permute-done | bytes 16416 | tf_op jit(solution)/shard_map/ppermute | solution.py:352
  54.1 2.3 %collective-permute-done.11.l1 = f32[8,1,512]{2,1,0:T(1,128)S(1)} collective-permute-done((f32[8,1,512]{2,1,0:T(1,128)S(1)}, f32[8,1,512]{2,1,0:T(1,128)S(1)}, u32[]{:S(2)}, u32[]{:S(2)}) %collective-permute-start.11) | collective-permute-done | bytes 16416 | tf_op jit(solution)/shard_map/ppermute | solution.py:352
  56.3 7.2 %shard_map.89 = (f32[4,128,512]{2,1,0:T(8,128)S(1)}, bf16[4,128,512]{2,1,0:T(8,128)(2,1)S(1)}, bf16[8,2,64,128]{3,2,1,0:T(8,128)(2,1)S(1)}, bf16[8,64,128]{2,1,0...) custom-call(s32[4,4]{1,0:T(4,128)S(1)} %get-tuple-element.57.bounds,, ...), custom_call_target="tpu_custom_call" | custom-call | flops 8000000000 | bytes 8388608 | tf_op jit(solution)/shard_map/pallas_call | solution.py:357
  64.4 2.6 %collective-permute-start.15 = (bf16[8,64,128]{2,1,0:T(8,128)(2,1)S(1)}, bf16[8,64,128]{2,1,0:T(8,128)(2,1)S(1)}, u32[]{:S(2)}, u32[]{:S(2)}) collective-permute-start(bf16[8,64,128]{2,1,0:T(8,128)(2,1)S(1)} %get-tuple-element.66), channel_id=1, source_target_pairs={{0,192},{64,0},{128,64},{192,128},{1,193},{65,1},{129,65},{193,129... | collective-permute-start | bytes 393224 | tf_op jit(solution)/shard_map/ppermute | solution.py:378
  67.0 3.2 %collective-permute-start.19 = (bf16[8,64,128]{2,1,0:T(8,128)(2,1)S(1)}, bf16[8,64,128]{2,1,0:T(8,128)(2,1)S(1)}, u32[]{:S(2)}, u32[]{:S(2)}) collective-permute-start(bf16[8,64,128]{2,1,0:T(8,128)(2,1)S(1)} %get-tuple-element.72), channel_id=1, source_target_pairs={{0,192},{64,0},{128,64},{192,128},{1,193},{65,1},{129,65},{193,129... | collective-permute-start | bytes 393224 | tf_op jit(solution)/shard_map/ppermute | solution.py:383
  70.9 3.0 %collective-permute-start.20 = (bf16[8,64,128]{2,1,0:T(8,128)(2,1)S(1)}, bf16[8,64,128]{2,1,0:T(8,128)(2,1)S(1)}, u32[]{:S(2)}, u32[]{:S(2)}) collective-permute-start(bf16[8,64,128]{2,1,0:T(8,128)(2,1)S(1)} %shard_map.92), channel_id=1, source_target_pairs={{0,192},{64,0},{128,64},{192,128},{1,193},{65,1},{129,65},{193,129... | collective-permute-start | bytes 393224 | tf_op jit(solution)/shard_map/ppermute | solution.py:383
  75.1 1.4 %collective-permute-start.22 = (bf16[128,512]{1,0:T(8,128)(2,1)S(1)}, bf16[128,512]{1,0:T(8,128)(2,1)S(1)}, u32[]{:S(2)}, u32[]{:S(2)}) collective-permute-start(bf16[128,512]{1,0:T(8,128)(2,1)S(1)} %get-tuple-element.76), channel_id=1, source_target_pairs={{0,4},{2,6},{4,0},{6,2},{1,5},{3,7},{5,1},{7,3},{8,12},{10,14},{12... | collective-permute-start | bytes 393224 | tf_op jit(solution)/shard_map/ppermute | solution.py:379
  76.6 3.6 %collective-permute-done.17.below_dk = bf16[8,64,128]{2,1,0:T(8,128)(2,1)S(1)} collective-permute-done((bf16[8,64,128]{2,1,0:T(8,128)(2,1)S(1)}, bf16[8,64,128]{2,1,0:T(8,128)(2,1)S(1)}, u32[]{:S(2)}, u32[]{:S(2)}) %collective-permute-start.17) | collective-permute-done | bytes 131104 | tf_op jit(solution)/shard_map/ppermute | solution.py:383
  80.2 2.0 %collective-permute-done.22.refs_2_ = bf16[128,512]{1,0:T(8,128)(2,1)S(1)} collective-permute-done((bf16[128,512]{1,0:T(8,128)(2,1)S(1)}, bf16[128,512]{1,0:T(8,128)(2,1)S(1)}, u32[]{:S(2)}, u32[]{:S(2)}) %collective-permute-start.22) | collective-permute-done | bytes 131104 | tf_op jit(solution)/shard_map/ppermute | solution.py:379
  82.2 1.3 %collective-permute-done.23.refs_3_ = bf16[128,512]{1,0:T(8,128)(2,1)S(1)} collective-permute-done((bf16[128,512]{1,0:T(8,128)(2,1)S(1)}, bf16[128,512]{1,0:T(8,128)(2,1)S(1)}, u32[]{:S(2)}, u32[]{:S(2)}) %collective-permute-start.23) | collective-permute-done | bytes 131104 | tf_op jit(solution)/shard_map/ppermute | solution.py:379
  84.4 8.2 %all-to-all-start.1 = ((bf16[8,2,64,128]{3,2,1,0:T(8,128)(2,1)}), bf16[8,2,64,128]{3,2,1,0:T(8,128)(2,1)S(1)}, u32[]{:S(2)}, u32[]{:S(2)}) async-start(bf16[8,2,64,128]{3,2,1,0:T(8,128)(2,1)} %shard_map.93), calls=%async_computation.1 | async-start | bytes 524288 | tf_op jit(solution)/shard_map/all_to_all | solution.py:386
  94.0 7.8 %all-to-all-done.1.blocks = bf16[8,2,64,128]{3,2,1,0:T(8,128)(2,1)S(1)} async-done(((bf16[8,2,64,128]{3,2,1,0:T(8,128)(2,1)}), bf16[8,2,64,128]{3,2,1,0:T(8,128)(2,1)S(1)}, u32[]{:S(2)}, u32[]{:S(2)}) %all-to-all-start.1) | async-done | bytes 262176 | tf_op jit(solution)/shard_map/all_to_all | solution.py:386
  (47 shorter events, 14.6 us)
Async XLA Ops:
  2.7 19.8 %all-to-all-start = ((bf16[8,144,128]{2,1,0:T(8,128)(2,1)}), bf16[8,144,128]{2,1,0:T(8,128)(2,1)S(1)}, u32[]{:S(2)}, u32[]{:S(2)}) async-start(bf16[8,144,128]{2,1,0:T(8,128)(2,1)} %get-tuple-element.49), calls=%async_computation | async-start | bytes 589824 | tf_op jit(solution)/shard_map/all_to_all | solution.py:318
  11.4 14.4 %collective-permute-start = (bf16[1056,128]{1,0:T(8,128)(2,1)S(1)}, bf16[1056,128]{1,0:T(8,128)(2,1)S(1)}, u32[]{:S(2)}, u32[]{:S(2)}) collective-permute-start(bf16[1056,128]{1,0:T(8,128)(2,1)S(1)} %copy-done), channel_id=1, source_target_pairs={{0,0},{2,194},{4,132},{6,70},{64,64},{66,2},{68,196},{70,134},{128... | collective-permute-start | bytes 811016 | tf_op jit(solution)/shard_map/ppermute | solution.py:317
  22.5 8.1 %collective-permute-start.4 = (bf16[8,144,128]{2,1,0:T(8,128)(2,1)S(1)}, bf16[8,144,128]{2,1,0:T(8,128)(2,1)S(1)}, u32[]{:S(2)}, u32[]{:S(2)}) collective-permute-start(bf16[8,144,128]{2,1,0:T(8,128)(2,1)S(1)} %all-to-all-done.p0), channel_id=1, source_target_pairs={{0,64},{64,128},{128,192},{192,0},{1,65},{65,129},{129,193},{193,1... | collective-permute-start | bytes 884744 | tf_op jit(solution)/shard_map/ppermute | solution.py:320
  24.1 8.2 %collective-permute-start.6 = (bf16[8,144,128]{2,1,0:T(8,128)(2,1)S(1)}, bf16[8,144,128]{2,1,0:T(8,128)(2,1)S(1)}, u32[]{:S(2)}, u32[]{:S(2)}) collective-permute-start(bf16[8,144,128]{2,1,0:T(8,128)(2,1)S(1)} %all-to-all-done.p0), channel_id=1, source_target_pairs={{0,192},{64,0},{128,64},{192,128},{1,193},{65,1},{129,65},{193,129... | collective-permute-start | bytes 884744 | tf_op jit(solution)/shard_map/ppermute | solution.py:321
  25.8 11.0 %collective-permute-start.3 = (bf16[1056,128]{1,0:T(8,128)(2,1)S(1)}, bf16[1056,128]{1,0:T(8,128)(2,1)S(1)}, u32[]{:S(2)}, u32[]{:S(2)}) collective-permute-start(bf16[1056,128]{1,0:T(8,128)(2,1)S(1)} %collective-permute-done.refs_0_), channel_id=1, source_target_pairs={{0,6},{2,0},{4,2},{6,4},{1,7},{3,1},{5,3},{7,5},{8,14},{10,8},{12,... | collective-permute-start | bytes 811016 | tf_op jit(solution)/shard_map/ppermute | solution.py:319
  28.5 9.2 %collective-permute-start.2 = (bf16[1056,128]{1,0:T(8,128)(2,1)S(1)}, bf16[1056,128]{1,0:T(8,128)(2,1)S(1)}, u32[]{:S(2)}, u32[]{:S(2)}) collective-permute-start(bf16[1056,128]{1,0:T(8,128)(2,1)S(1)} %collective-permute-done.refs_0_), channel_id=1, source_target_pairs={{0,4},{2,6},{4,0},{6,2},{1,5},{3,7},{5,1},{7,3},{8,12},{10,14},{12... | collective-permute-start | bytes 811016 | tf_op jit(solution)/shard_map/ppermute | solution.py:319
  29.3 11.1 %collective-permute-start.1 = (bf16[1056,128]{1,0:T(8,128)(2,1)S(1)}, bf16[1056,128]{1,0:T(8,128)(2,1)S(1)}, u32[]{:S(2)}, u32[]{:S(2)}) collective-permute-start(bf16[1056,128]{1,0:T(8,128)(2,1)S(1)} %collective-permute-done.refs_0_), channel_id=1, source_target_pairs={{0,2},{2,4},{4,6},{6,0},{1,3},{3,5},{5,7},{7,1},{8,10},{10,12},{12... | collective-permute-start | bytes 811016 | tf_op jit(solution)/shard_map/ppermute | solution.py:319
  30.6 9.8 %collective-permute-start.5 = (bf16[8,80,128]{2,1,0:T(8,128)(2,1)S(1)}, bf16[8,80,128]{2,1,0:T(8,128)(2,1)S(1)}, u32[]{:S(2)}, u32[]{:S(2)}) collective-permute-start(bf16[8,80,128]{2,1,0:T(8,128)(2,1)S(1)} %slice.8), channel_id=1, source_target_pairs={{0,64},{64,128},{128,192},{192,0},{1,65},{65,129},{129,193},{193,1... | collective-permute-start | bytes 491528 | tf_op jit(solution)/shard_map/ppermute | solution.py:322
  32.3 8.1 %collective-permute-start.7 = (bf16[8,64,128]{2,1,0:T(8,128)(2,1)S(1)}, bf16[8,64,128]{2,1,0:T(8,128)(2,1)S(1)}, u32[]{:S(2)}, u32[]{:S(2)}) collective-permute-start(bf16[8,64,128]{2,1,0:T(8,128)(2,1)S(1)} %slice.9), channel_id=1, source_target_pairs={{0,192},{64,0},{128,64},{192,128},{1,193},{65,1},{129,65},{193,129... | collective-permute-start | bytes 393224 | tf_op jit(solution)/shard_map/ppermute | solution.py:323
  40.6 11.4 %collective-permute-start.9 = (bf16[4,528,128]{2,1,0:T(8,128)(2,1)S(1)}, bf16[4,528,128]{2,1,0:T(8,128)(2,1)S(1)}, u32[]{:S(2)}, u32[]{:S(2)}) collective-permute-start(bf16[4,528,128]{2,1,0:T(8,128)(2,1)S(1)} %get-tuple-element.58.grad_own), channel_id=1, source_target_pairs={{0,1},{1,0},{2,3},{3,2},{4,5},{5,4},{6,7},{7,6},{8,9},{9,8},{10,11... | collective-permute-start | bytes 1622024 | tf_op jit(solution)/shard_map/ppermute | solution.py:328
  48.8 5.3 %collective-permute-start.13 = (f32[8,1,512]{2,1,0:T(1,128)S(1)}, f32[8,1,512]{2,1,0:T(1,128)S(1)}, u32[]{:S(2)}, u32[]{:S(2)}) collective-permute-start(f32[8,1,512]{2,1,0:T(1,128)S(1)} %multiply_add_fusion.l0), channel_id=1, source_target_pairs={{0,4},{2,6},{4,0},{6,2},{1,5},{3,7},{5,1},{7,3},{8,12},{10,14},{12... | collective-permute-start | bytes 49160 | tf_op jit(solution)/shard_map/ppermute | solution.py:352
  50.0 4.1 %collective-permute-start.12 = (f32[8,1,512]{2,1,0:T(1,128)S(1)}, f32[8,1,512]{2,1,0:T(1,128)S(1)}, u32[]{:S(2)}, u32[]{:S(2)}) collective-permute-start(f32[8,1,512]{2,1,0:T(1,128)S(1)} %multiply_add_fusion.l0), channel_id=1, source_target_pairs={{0,6},{2,0},{4,2},{6,4},{1,7},{3,1},{5,3},{7,5},{8,14},{10,8},{12,... | collective-permute-start | bytes 49160 | tf_op jit(solution)/shard_map/ppermute | solution.py:352
  51.4 5.0 %collective-permute-start.11 = (f32[8,1,512]{2,1,0:T(1,128)S(1)}, f32[8,1,512]{2,1,0:T(1,128)S(1)}, u32[]{:S(2)}, u32[]{:S(2)}) collective-permute-start(f32[8,1,512]{2,1,0:T(1,128)S(1)} %multiply_add_fusion.l0), channel_id=1, source_target_pairs={{0,2},{2,4},{4,6},{6,0},{1,3},{3,5},{5,7},{7,1},{8,10},{10,12},{12... | collective-permute-start | bytes 49160 | tf_op jit(solution)/shard_map/ppermute | solution.py:352
  63.6 6.7 %collective-permute-start.16 = (bf16[4,128,512]{2,1,0:T(8,128)(2,1)S(1)}, bf16[4,128,512]{2,1,0:T(8,128)(2,1)S(1)}, u32[]{:S(2)}, u32[]{:S(2)}) collective-permute-start(bf16[4,128,512]{2,1,0:T(8,128)(2,1)S(1)} %get-tuple-element.68), channel_id=1, source_target_pairs={{0,1},{1,0},{2,3},{3,2},{4,5},{5,4},{6,7},{7,6},{8,9},{9,8},{10,11... | collective-permute-start | bytes 1572872 | tf_op jit(solution)/shard_map/ppermute | solution.py:375
  63.7 7.2 %collective-permute-start.14 = (bf16[8,64,128]{2,1,0:T(8,128)(2,1)S(1)}, bf16[8,64,128]{2,1,0:T(8,128)(2,1)S(1)}, u32[]{:S(2)}, u32[]{:S(2)}) collective-permute-start(bf16[8,64,128]{2,1,0:T(8,128)(2,1)S(1)} %get-tuple-element.65), channel_id=1, source_target_pairs={{0,64},{64,128},{128,192},{192,0},{1,65},{65,129},{129,193},{193,1... | collective-permute-start | bytes 393224 | tf_op jit(solution)/shard_map/ppermute | solution.py:377
  64.4 6.5 %collective-permute-start.15 = (bf16[8,64,128]{2,1,0:T(8,128)(2,1)S(1)}, bf16[8,64,128]{2,1,0:T(8,128)(2,1)S(1)}, u32[]{:S(2)}, u32[]{:S(2)}) collective-permute-start(bf16[8,64,128]{2,1,0:T(8,128)(2,1)S(1)} %get-tuple-element.66), channel_id=1, source_target_pairs={{0,192},{64,0},{128,64},{192,128},{1,193},{65,1},{129,65},{193,129... | collective-permute-start | bytes 393224 | tf_op jit(solution)/shard_map/ppermute | solution.py:378
  67.0 8.2 %collective-permute-start.18 = (bf16[8,64,128]{2,1,0:T(8,128)(2,1)S(1)}, bf16[8,64,128]{2,1,0:T(8,128)(2,1)S(1)}, u32[]{:S(2)}, u32[]{:S(2)}) collective-permute-start(bf16[8,64,128]{2,1,0:T(8,128)(2,1)S(1)} %get-tuple-element.71), channel_id=1, source_target_pairs={{0,64},{64,128},{128,192},{192,0},{1,65},{65,129},{129,193},{193,1... | collective-permute-start | bytes 393224 | tf_op jit(solution)/shard_map/ppermute | solution.py:383
  67.0 9.6 %collective-permute-start.19 = (bf16[8,64,128]{2,1,0:T(8,128)(2,1)S(1)}, bf16[8,64,128]{2,1,0:T(8,128)(2,1)S(1)}, u32[]{:S(2)}, u32[]{:S(2)}) collective-permute-start(bf16[8,64,128]{2,1,0:T(8,128)(2,1)S(1)} %get-tuple-element.72), channel_id=1, source_target_pairs={{0,192},{64,0},{128,64},{192,128},{1,193},{65,1},{129,65},{193,129... | collective-permute-start | bytes 393224 | tf_op jit(solution)/shard_map/ppermute | solution.py:383
  70.9 5.7 %collective-permute-start.20 = (bf16[8,64,128]{2,1,0:T(8,128)(2,1)S(1)}, bf16[8,64,128]{2,1,0:T(8,128)(2,1)S(1)}, u32[]{:S(2)}, u32[]{:S(2)}) collective-permute-start(bf16[8,64,128]{2,1,0:T(8,128)(2,1)S(1)} %shard_map.92), channel_id=1, source_target_pairs={{0,192},{64,0},{128,64},{192,128},{1,193},{65,1},{129,65},{193,129... | collective-permute-start | bytes 393224 | tf_op jit(solution)/shard_map/ppermute | solution.py:383
  73.9 6.3 %collective-permute-start.17 = (bf16[8,64,128]{2,1,0:T(8,128)(2,1)S(1)}, bf16[8,64,128]{2,1,0:T(8,128)(2,1)S(1)}, u32[]{:S(2)}, u32[]{:S(2)}) collective-permute-start(bf16[8,64,128]{2,1,0:T(8,128)(2,1)S(1)} %shard_map.91), channel_id=1, source_target_pairs={{0,64},{64,128},{128,192},{192,0},{1,65},{65,129},{129,193},{193,1... | collective-permute-start | bytes 393224 | tf_op jit(solution)/shard_map/ppermute | solution.py:383
  74.0 6.2 %collective-permute-start.21 = (bf16[128,512]{1,0:T(8,128)(2,1)S(1)}, bf16[128,512]{1,0:T(8,128)(2,1)S(1)}, u32[]{:S(2)}, u32[]{:S(2)}) collective-permute-start(bf16[128,512]{1,0:T(8,128)(2,1)S(1)} %get-tuple-element.75), channel_id=1, source_target_pairs={{0,6},{2,0},{4,2},{6,4},{1,7},{3,1},{5,3},{7,5},{8,14},{10,8},{12,... | collective-permute-start | bytes 393224 | tf_op jit(solution)/shard_map/ppermute | solution.py:379
  75.1 7.1 %collective-permute-start.22 = (bf16[128,512]{1,0:T(8,128)(2,1)S(1)}, bf16[128,512]{1,0:T(8,128)(2,1)S(1)}, u32[]{:S(2)}, u32[]{:S(2)}) collective-permute-start(bf16[128,512]{1,0:T(8,128)(2,1)S(1)} %get-tuple-element.76), channel_id=1, source_target_pairs={{0,4},{2,6},{4,0},{6,2},{1,5},{3,7},{5,1},{7,3},{8,12},{10,14},{12... | collective-permute-start | bytes 393224 | tf_op jit(solution)/shard_map/ppermute | solution.py:379
  76.5 7.0 %collective-permute-start.23 = (bf16[128,512]{1,0:T(8,128)(2,1)S(1)}, bf16[128,512]{1,0:T(8,128)(2,1)S(1)}, u32[]{:S(2)}, u32[]{:S(2)}) collective-permute-start(bf16[128,512]{1,0:T(8,128)(2,1)S(1)} %get-tuple-element.77), channel_id=1, source_target_pairs={{0,2},{2,4},{4,6},{6,0},{1,3},{3,5},{5,7},{7,1},{8,10},{10,12},{12... | collective-permute-start | bytes 393224 | tf_op jit(solution)/shard_map/ppermute | solution.py:379
  84.4 17.5 %all-to-all-start.1 = ((bf16[8,2,64,128]{3,2,1,0:T(8,128)(2,1)}), bf16[8,2,64,128]{3,2,1,0:T(8,128)(2,1)S(1)}, u32[]{:S(2)}, u32[]{:S(2)}) async-start(bf16[8,2,64,128]{3,2,1,0:T(8,128)(2,1)} %shard_map.93), calls=%async_computation.1 | async-start | bytes 524288 | tf_op jit(solution)/shard_map/all_to_all | solution.py:386
  (4 other events, 12.7 us)
